TPU v7x, 32 devices: a whole 2x2x4 slice. The times are simulated.
32 devices in a mesh: rep: 4 (over x, core), seq: 8 (over z, y).
Axes of the slice: x: 2, y: 2, z: 4, core: 2. Of those that a mesh axis runs over, the one named last changes fastest.
Arguments:
- tokens: bfloat16 [8192, 1024], P(('rep', 'seq')), may hold values from -6 to 6
- norm_first: bfloat16 [1024], P('seq'), may hold values from 0.25 to 1.75
- joint_weight: bfloat16 [1024, 3072], P('seq'), may hold values from -0.1875 to 0.1875
- output_weight: bfloat16 [1024, 1024], P('seq'), may hold values from -2.5 to 2.5
- norm_second: bfloat16 [1024], P('seq'), may hold values from 0.25 to 1.75
- expand_weight: bfloat16 [1024, 5248], P('seq'), may hold values from -0.1875 to 0.1875
- shrink_weight: bfloat16 [2624, 1024], P('seq'), may hold values from -0.125 to 0.125
- document_start: int32 [8192], P(('rep', 'seq')), may hold values from 0 to 7692, as said below
- cotangent: bfloat16 [8192, 1024], P(('rep', 'seq')), may hold values from -6 to 6
Outputs:
- block_output: bfloat16 [8192, 1024], P(('rep', 'seq'))
- tokens_gradient: bfloat16 [8192, 1024], P(('rep', 'seq'))
- first_gradient: float32 [1024], P('seq')
- joint_gradient: float32 [1024, 3072], P('seq')
- output_gradient: float32 [1024, 1024], P('seq')
- second_gradient: float32 [1024], P('seq')
- expand_gradient: float32 [1024, 5248], P('seq')
- shrink_gradient: float32 [2624, 1024], P('seq')
Inputs may be any that keep to these rules, and one draw needn't show every extreme that they name: `document_start`: tokens of one document are contiguous and share the value, the index of the document's first token; a document has 100 to 500 tokens (the one just before a stream's last may be cut shorter) and lies inside one aligned stream of 2048 tokens; the last document of every stream has exactly 500 tokens.
All inputs are finite; a program needn't handle non-finite values.
Results may differ from a plain program's by a relative error of at most 0.017.
Values may be sent and summed in bfloat16 or wider, within the bound.
No kernel may reach another device: no remote copies, remote signals or barrier semaphores. Data moves between devices by JAX's collectives and lax.ppermute only.
A program may use at most 192 MiB of HBM per device.

v0:
```python
import jax
import jax.numpy as jnp
from jax import lax
from jax.sharding import PartitionSpec as P

HEADS = 16
HEAD_DIM = 64
FF = 2624
HALO = 512


EPSILON = 1e-05
THETA = 160000.0
SCALE = 0.125


def from_behind(block, axis, distance):
    devices = range(lax.axis_size(axis))
    route = [(i - distance, i) for i in devices if i - distance in devices]
    return lax.ppermute(block, axis, route)


def as_sent(x):
    return jax.tree.map(lambda a: a.astype(jnp.bfloat16) if a.dtype == jnp.float32 else a, x)


def normalize(rows, gain):
    middle = jnp.mean(rows, axis=-1, keepdims=True)
    centered = rows - middle
    spread = jnp.mean(centered * centered, axis=-1, keepdims=True)
    return centered * lax.rsqrt(spread + EPSILON) * gain


def activate(inner_part, gate_part):
    return jax.nn.gelu(inner_part, approximate=False) * gate_part


def rotate(values, cosine, sine):
    halves = values.shape[-1] // 2
    first = values[..., :halves]
    second = values[..., halves:]
    return jnp.concatenate(
        [first * cosine - second * sine, second * cosine + first * sine], axis=-1
    )


def rotate_back(grads, cosine, sine):
    halves = grads.shape[-1] // 2
    first = grads[..., :halves]
    second = grads[..., halves:]
    return jnp.concatenate(
        [first * cosine + second * sine, second * cosine - first * sine], axis=-1
    )


def inner_rows(left, right):
    return lax.dot_general(
        left, right, (((0,), (0,)), ((), ())), preferred_element_type=jnp.float32
    )


def outer_rows(left, right):
    return lax.dot_general(
        left, right, (((1,), (1,)), ((), ())), preferred_element_type=jnp.float32
    )


def scores(queries, block_keys, query_doc, block_doc):
    raw = (
        jnp.einsum("qhd,khd->hqk", queries, block_keys, preferred_element_type=jnp.float32) * SCALE
    )
    allowed = query_doc[:, None] == block_doc[None, :]
    return jnp.where(allowed[None], raw, -jnp.inf)


def on_device(
    tokens,
    norm_first,
    joint_weight,
    output_weight,
    norm_second,
    expand_weight,
    shrink_weight,
    document_start,
    cotangent,
):
    rows = tokens.shape[0]
    width = tokens.shape[1]
    reach = min(HALO // rows, lax.axis_size("seq") - 1)
    whole = (
        lax.all_gather(norm_first, "seq", axis=0, tiled=True),
        lax.all_gather(joint_weight, "seq", axis=0, tiled=True),
        lax.all_gather(output_weight, "seq", axis=0, tiled=True),
        lax.all_gather(norm_second, "seq", axis=0, tiled=True),
        lax.all_gather(expand_weight, "seq", axis=0, tiled=True),
        lax.all_gather(shrink_weight, "seq", axis=0, tiled=True),
    )
    gain_one = whole[0].astype(jnp.float32)
    gain_two = whole[3].astype(jnp.float32)
    anchor = (lax.axis_index("rep") * lax.axis_size("seq") + lax.axis_index("seq")) * rows
    position = (anchor + jnp.arange(rows, dtype=jnp.int32) - document_start).astype(jnp.float32)
    halves = HEAD_DIM // 2
    frequency = THETA ** (-(jnp.arange(halves, dtype=jnp.float32) * 2.0) / HEAD_DIM)
    angle = position[:, None] * frequency[None, :]
    cosine = jnp.cos(angle)[:, None, :]
    sine = jnp.sin(angle)[:, None, :]
    stream = tokens.astype(jnp.float32)
    first_low = normalize(stream, gain_one).astype(jnp.bfloat16)
    mixed = jnp.dot(first_low, whole[1], preferred_element_type=jnp.float32)
    queries = mixed[:, :width].reshape(rows, HEADS, HEAD_DIM)
    keys = mixed[:, width : 2 * width].reshape(rows, HEADS, HEAD_DIM)
    queries_low = rotate(queries, cosine, sine).astype(jnp.bfloat16)
    keys_low = rotate(keys, cosine, sine).astype(jnp.bfloat16)
    values_low = mixed[:, 2 * width :].reshape(rows, HEADS, HEAD_DIM).astype(jnp.bfloat16)
    own_doc = document_start + 1
    own_block = (keys_low, values_low, own_doc)
    blocks = {0: own_block}
    for distance in range(1, reach + 1):
        for direction in (1, -1):
            blocks[direction * distance] = from_behind(
                (own_block[0], own_block[1], own_block[2]), "seq", direction * distance
            )
    order = [0] + [offset for offset in sorted(blocks.keys()) if offset != 0]
    running_top = None
    running_total = None
    for offset in order:
        block_keys, block_values, block_doc = blocks[offset]
        logits = scores(queries_low, block_keys, own_doc, block_doc)
        block_top = jnp.max(logits, axis=-1)
        if running_top is None:
            running_top = block_top
            running_total = jnp.sum(jnp.exp(logits - running_top[..., None]), axis=-1)
        else:
            new_top = jnp.maximum(running_top, block_top)
            running_total = running_total * jnp.exp(running_top - new_top) + jnp.sum(
                jnp.exp(logits - new_top[..., None]), axis=-1
            )
            running_top = new_top
    log_total = running_top + jnp.log(running_total)
    attended = jnp.zeros((rows, HEADS, HEAD_DIM), jnp.float32)
    for offset in order:
        block_keys, block_values, block_doc = blocks[offset]
        logits = scores(queries_low, block_keys, own_doc, block_doc)
        weights_low = jnp.exp(logits - log_total[..., None]).astype(jnp.bfloat16)
        attended = attended + jnp.einsum(
            "hqk,khd->qhd", weights_low, block_values, preferred_element_type=jnp.float32
        )
    attended_low = attended.reshape(rows, width).astype(jnp.bfloat16)
    middle = stream + jnp.dot(attended_low, whole[2], preferred_element_type=jnp.float32)
    second_low = normalize(middle, gain_two).astype(jnp.bfloat16)
    lifted = jnp.dot(second_low, whole[4], preferred_element_type=jnp.float32)
    inner_part = lifted[:, :FF]
    gate_part = lifted[:, FF:]
    active_low = activate(inner_part, gate_part).astype(jnp.bfloat16)
    result = middle + jnp.dot(active_low, whole[5], preferred_element_type=jnp.float32)
    again = (
        lax.all_gather(norm_first, "seq", axis=0, tiled=True),
        lax.all_gather(joint_weight, "seq", axis=0, tiled=True),
        lax.all_gather(output_weight, "seq", axis=0, tiled=True),
        lax.all_gather(norm_second, "seq", axis=0, tiled=True),
        lax.all_gather(expand_weight, "seq", axis=0, tiled=True),
        lax.all_gather(shrink_weight, "seq", axis=0, tiled=True),
    )
    gain_one = again[0].astype(jnp.float32)
    gain_two = again[3].astype(jnp.float32)
    shrink_grad = inner_rows(active_low, cotangent)
    active_grad = outer_rows(cotangent, again[5])
    unused, active_pull = jax.vjp(activate, inner_part, gate_part)
    inner_grad, gate_grad = active_pull(active_grad)
    lifted_grad_low = jnp.concatenate([inner_grad, gate_grad], axis=1).astype(jnp.bfloat16)
    expand_grad = inner_rows(second_low, lifted_grad_low)
    second_rows_grad = outer_rows(lifted_grad_low, again[4])
    unused, second_pull = jax.vjp(normalize, middle, gain_two)
    middle_part, gain_two_grad = second_pull(second_rows_grad)
    middle_grad = cotangent.astype(jnp.float32) + middle_part
    branch_low = middle_grad.astype(jnp.bfloat16)
    output_grad = inner_rows(attended_low, branch_low)
    attended_grad_low = (
        outer_rows(branch_low, again[2]).astype(jnp.bfloat16).reshape(rows, HEADS, HEAD_DIM)
    )
    delta = jnp.transpose(jnp.sum(attended_grad_low.astype(jnp.float32) * attended, axis=-1))
    query_grad = jnp.zeros((rows, HEADS, HEAD_DIM), jnp.float32)
    key_grads = {}
    for offset in order:
        block_keys, block_values, block_doc = blocks[offset]
        logits = scores(queries_low, block_keys, own_doc, block_doc)
        weights = jnp.exp(logits - log_total[..., None])
        weights_low = weights.astype(jnp.bfloat16)
        weights_grad = jnp.einsum(
            "qhd,khd->hqk", attended_grad_low, block_values, preferred_element_type=jnp.float32
        )
        logits_grad = (weights * (weights_grad - delta[..., None])).astype(jnp.bfloat16)
        query_grad = (
            query_grad
            + jnp.einsum(
                "hqk,khd->qhd", logits_grad, block_keys, preferred_element_type=jnp.float32
            )
            * SCALE
        )
        block_key_grad = (
            jnp.einsum("hqk,qhd->khd", logits_grad, queries_low, preferred_element_type=jnp.float32)
            * SCALE
        )
        block_value_grad = jnp.einsum(
            "hqk,qhd->khd", weights_low, attended_grad_low, preferred_element_type=jnp.float32
        )
        key_grads[offset] = (block_key_grad, block_value_grad)
    key_total, value_total = key_grads[0]
    for offset in order[1:]:
        moved = from_behind(as_sent(key_grads[offset]), "seq", -offset)
        key_total = key_total + moved[0]
        value_total = value_total + moved[1]
    query_pre = rotate_back(query_grad, cosine, sine).reshape(rows, width)
    key_pre = rotate_back(key_total, cosine, sine).reshape(rows, width)
    joint_grad_low = jnp.concatenate(
        [query_pre, key_pre, value_total.reshape(rows, width)], axis=1
    ).astype(jnp.bfloat16)
    joint_grad = inner_rows(first_low, joint_grad_low)
    first_rows_grad = outer_rows(joint_grad_low, again[1])
    unused, first_pull = jax.vjp(normalize, stream, gain_one)
    stream_part, gain_one_grad = first_pull(first_rows_grad)
    tokens_grad = (middle_grad + stream_part).astype(jnp.bfloat16)
    shards = (
        lax.psum_scatter(gain_one_grad, "seq", scatter_dimension=0, tiled=True),
        lax.psum_scatter(joint_grad, "seq", scatter_dimension=0, tiled=True),
        lax.psum_scatter(output_grad, "seq", scatter_dimension=0, tiled=True),
        lax.psum_scatter(gain_two_grad, "seq", scatter_dimension=0, tiled=True),
        lax.psum_scatter(expand_grad, "seq", scatter_dimension=0, tiled=True),
        lax.psum_scatter(shrink_grad, "seq", scatter_dimension=0, tiled=True),
    )
    summed = (
        lax.psum(shards[0].astype(jnp.bfloat16), "rep").astype(jnp.float32),
        lax.psum(shards[1].astype(jnp.bfloat16), "rep").astype(jnp.float32),
        lax.psum(shards[2].astype(jnp.bfloat16), "rep").astype(jnp.float32),
        lax.psum(shards[3].astype(jnp.bfloat16), "rep").astype(jnp.float32),
        lax.psum(shards[4].astype(jnp.bfloat16), "rep").astype(jnp.float32),
        lax.psum(shards[5].astype(jnp.bfloat16), "rep").astype(jnp.float32),
    )
    return (
        result.astype(jnp.bfloat16),
        tokens_grad,
        summed[0],
        summed[1],
        summed[2],
        summed[3],
        summed[4],
        summed[5],
    )


def solution(mesh):
    placed = (
        P(("rep", "seq"), None),
        P("seq"),
        P("seq", None),
        P("seq", None),
        P("seq"),
        P("seq", None),
        P("seq", None),
        P(("rep", "seq")),
        P(("rep", "seq"), None),
    )
    return jax.shard_map(
        on_device,
        mesh=mesh,
        in_specs=placed,
        out_specs=(
            P(("rep", "seq"), None),
            P(("rep", "seq"), None),
            P("seq"),
            P("seq", None),
            P("seq", None),
            P("seq"),
            P("seq", None),
            P("seq", None),
        ),
        check_vma=False,
    )
```

profile of v0, /device:TPU:0, one launch (start us, length us, event | category | flops | bytes accessed | tf_op | source)
XLA Modules:
  0.0 1421.5 jit_solution(17414841466716876406)
XLA Ops:
  12.7 5.5 collective-permute-start.4
  18.2 4.6 collective-permute-start.6
  22.9 19.5 %all-gather = bf16[8,1,128]{2,1,0:T(2,128)(2,1)S(1)} all-gather(bf16[1,1,128]{2,1,0:T(2,128)(2,1)} %bitcast.135), channel_id=1, replica_groups=mesh['rep'=4,'seq'=8] {'seq'}, dimensions={0}, use_global_device_ids=true | all-gather | bytes 2304 | tf_op jit(solution)/shard_map/all_gather | solution.py:91
  45.8 16.3 %all-gather.1 = bf16[8,1,128]{2,1,0:T(2,128)(2,1)S(1)} all-gather(bf16[1,1,128]{2,1,0:T(2,128)(2,1)S(1)} %bitcast.136), channel_id=1, replica_groups=mesh['rep'=4,'seq'=8] {'seq'}, dimensions={0}, use_global_device_ids=true | all-gather | bytes 2304 | tf_op jit(solution)/shard_map/all_gather | solution.py:94
  63.1 48.9 %all-gather.7.cloned.1.call-done = bf16[1024,3072]{1,0:T(8,128)(2,1)} async-done(((bf16[128,3072]{1,0:T(8,128)(2,1)}), bf16[1024,3072]{1,0:T(8,128)(2,1)}) %all-gather.7.cloned.1.call-update) | async-done | bytes 6291472 | tf_op jit(solution)/shard_map/all_gather | solution.py:92
  112.0 4.7 fusion.93
  132.4 7.7 collective-permute-start.11
  146.2 12.3 collective-permute-done.5
  163.1 7.7 collective-permute-done.1
  178.9 7.4 collective-permute-done.8
  192.8 144.6 %all-gather.11.cloned.1.call-done = bf16[1024,5248]{1,0:T(8,128)(2,1)} async-done(((bf16[128,5248]{1,0:T(8,128)(2,1)}), bf16[1024,5248]{1,0:T(8,128)(2,1)}) %all-gather.11.cloned.1.call-update) | async-done | bytes 10747920 | tf_op jit(solution)/shard_map/all_gather | solution.py:95
  337.4 9.4 fusion.98
  346.8 78.7 %all-gather.13.cloned.1.call-done = bf16[2624,1024]{1,0:T(8,128)(2,1)} async-done(((bf16[328,1024]{1,0:T(8,128)(2,1)}), bf16[2624,1024]{1,0:T(8,128)(2,1)}) %all-gather.13.cloned.1.call-update) | async-done | bytes 5373968 | tf_op jit(solution)/shard_map/all_gather | solution.py:96
  425.5 12.0 add_convert_fusion
  442.6 6.0 multiply_reduce_fusion
  455.8 7.0 fusion.112
  468.2 3.5 fusion.43
  483.1 4.8 collective-permute-start.13
  490.1 5.5 collective-permute-start.12
  504.0 15.6 %collective-permute-done.15 = bf16[256,16,64]{0,2,1:T(8,128)(2,1)S(1)} collective-permute-done((bf16[256,16,64]{0,2,1:T(8,128)(2,1)S(1)}, bf16[256,16,64]{0,2,1:T(8,128)(2,1)S(1)}, u32[]{:S(2)}, u32[]{:S(2)}) %collective-permute-start.15) | collective-permute-done | bytes 524320 | tf_op jit(solution)/shard_map/ppermute | solution.py:20
  520.9 13.4 collective-permute-start.17
  539.0 18.6 %collective-permute-done.17 = bf16[256,16,64]{0,2,1:T(8,128)(2,1)S(1)} collective-permute-done((bf16[256,16,64]{0,2,1:T(8,128)(2,1)S(1)}, bf16[256,16,64]{0,2,1:T(8,128)(2,1)S(1)}, u32[]{:S(2)}, u32[]{:S(2)}) %collective-permute-start.17) | collective-permute-done | bytes 524320 | tf_op jit(solution)/shard_map/ppermute | solution.py:20
  558.0 6.6 fusion.51
  565.0 11.3 fusion.17
  578.2 5.5 fusion.31
  588.0 183.6 %reduce-scatter.11.cloned.1.call-done = f32[328,1024]{1,0:T(8,128)} async-done(((f32[2624,1024]{1,0:T(8,128)}), f32[328,1024]{1,0:T(8,128)}) %reduce-scatter.11.cloned.1.call-update) | async-done | bytes 1343504 | tf_op jit(solution)/shard_map/reduce_scatter | solution.py:229
  773.9 207.7 %reduce-scatter.5.cloned.1.call-done = f32[128,3072]{1,0:T(8,128)} async-done(((f32[1024,3072]{1,0:T(8,128)}), f32[128,3072]{1,0:T(8,128)}) %reduce-scatter.5.cloned.1.call-update) | async-done | bytes 1572880 | tf_op jit(solution)/shard_map/reduce_scatter | solution.py:225
  983.9 351.6 %reduce-scatter.9.cloned.1.call-done = f32[128,5248]{1,0:T(8,128)} async-done(((f32[1024,5248]{1,0:T(8,128)}), f32[128,5248]{1,0:T(8,128)}) %reduce-scatter.9.cloned.1.call-update) | async-done | bytes 2686992 | tf_op jit(solution)/shard_map/reduce_scatter | solution.py:228
  1338.6 5.3 fusion.49
  1344.4 19.7 %all-reduce.2 = (bf16[1024]{0:T(1024)(128)(2,1)S(1)}, bf16[1024]{0:T(1024)(128)(2,1)S(1)}) all-reduce(f32[1024]{0:T(1024)S(1)} %get-tuple-element.10, f32[1024]{0:T(1024)S(1)} %copy-done.61), channel_id=2, replica_groups=mesh['rep'=4,'seq'=8] {'seq'}, use_global_device_ids=true, to_apply=%region_20.21.clone | all-reduce | flops 2048 | bytes 12288
  1364.3 6.3 all-reduce.3
  1372.9 33.1 %all-reduce.7.cloned.1.call-done = (bf16[128,3072]{1,0:T(8,128)(2,1)}, bf16[128,1024]{1,0:T(8,128)(2,1)}, bf16[128,5248]{1,0:T(8,128)(2,1)}, bf16[328,1024]{1,0:T(8,128)(2,1)}) async-done(((bf16[128,3072]{1,0:T(8,128)(2,1)}, bf16[128,1024]{1,0:T(8,128)(2,1)}, bf16[128,5248]{1,0:T(8,128)(2,1)}, bf16[328,1024]{1,0:T(8,128)(2,1)}), (bf16[128,3072]{1,0:T(8,128)(2,1)}, bf16[128,1024]{1,0:T(8,128)(2,1)}, ...) | async-done | bytes 3063824 | tf_op jit(solution)/shard_map/psum | solution.py:233
  (270 shorter events, 120.7 us)
Async XLA Ops:
  7.2 104.9 %copy-start.5 = (bf16[256,1024]{1,0:T(8,128)(2,1)S(1)}, bf16[256,1024]{1,0:T(8,128)(2,1)}, u32[]{:S(2)}) copy-start(bf16[256,1024]{1,0:T(8,128)(2,1)} %param.9) | copy-start | bytes 1572868
  7.2 104.8 %all-gather.7.cloned.1.call-start = ((), (), s32[]{:S(2)}) async-start(), calls=%async_computation.4 | async-start | bytes 7077888 | tf_op jit(solution)/shard_map/all_gather | solution.py:92
  7.9 181.7 %all-gather.9.cloned.1.call-start = ((), (), s32[]{:S(2)}) async-start(), calls=%async_computation.5 | async-start | bytes 2359296 | tf_op jit(solution)/shard_map/all_gather | solution.py:93
  8.7 328.7 %all-gather.11.cloned.1.call-start = ((), (), s32[]{:S(2)}) async-start(), calls=%async_computation.6 | async-start | bytes 12091392 | tf_op jit(solution)/shard_map/all_gather | solution.py:95
  9.4 416.1 %all-gather.13.cloned.1.call-start = ((), (), s32[]{:S(2)}) async-start(), calls=%async_computation.7 | async-start | bytes 6045696 | tf_op jit(solution)/shard_map/all_gather | solution.py:96
  10.1 52.0 %collective-permute-start = (s32[256]{0:T(256)S(1)}, s32[256]{0:T(256)S(1)}, u32[]{:S(2)}, u32[]{:S(2)}) collective-permute-start(s32[256]{0:T(256)S(1)} %get-tuple-element.51), channel_id=1, source_target_pairs={{2,0},{3,1},{4,2},{5,3},{6,4},{7,5},{10,8},{11,9},{12,10},{13,11},... | collective-permute-start | bytes 3080 | tf_op jit(solution)/shard_map/ppermute | solution.py:20
  11.4 50.7 %collective-permute-start.2 = (s32[256]{0:T(256)S(1)}, s32[256]{0:T(256)S(1)}, u32[]{:S(2)}, u32[]{:S(2)}) collective-permute-start(s32[256]{0:T(256)S(1)} %get-tuple-element.51), channel_id=1, source_target_pairs={{1,0},{2,1},{3,2},{4,3},{5,4},{6,5},{7,6},{9,8},{10,9},{11,10},{12... | collective-permute-start | bytes 3080 | tf_op jit(solution)/shard_map/ppermute | solution.py:20
  12.7 49.4 %collective-permute-start.4 = (s32[256]{0:T(256)S(1)}, s32[256]{0:T(256)S(1)}, u32[]{:S(2)}, u32[]{:S(2)}) collective-permute-start(s32[256]{0:T(256)S(1)} %get-tuple-element.51), channel_id=1, source_target_pairs={{0,1},{1,2},{2,3},{3,4},{4,5},{5,6},{6,7},{8,9},{9,10},{10,11},{11... | collective-permute-start | bytes 3080 | tf_op jit(solution)/shard_map/ppermute | solution.py:20
  18.2 43.9 %collective-permute-start.6 = (s32[256]{0:T(256)S(1)}, s32[256]{0:T(256)S(1)}, u32[]{:S(2)}, u32[]{:S(2)}) collective-permute-start(s32[256]{0:T(256)S(1)} %get-tuple-element.51), channel_id=1, source_target_pairs={{0,2},{1,3},{2,4},{3,5},{4,6},{5,7},{8,10},{9,11},{10,12},{11,13},... | collective-permute-start | bytes 3080 | tf_op jit(solution)/shard_map/ppermute | solution.py:20
  22.9 563.3 %reduce-scatter.7.cloned.1.call-start = ((), (), s32[]{:S(2)}) async-start(), calls=%async_computation.9 | async-start | bytes 4718592 | tf_op jit(solution)/shard_map/reduce_scatter | solution.py:226
  123.3 19.5 %collective-permute-start.7 = (bf16[256,16,64]{0,2,1:T(8,128)(2,1)}, bf16[256,16,64]{0,2,1:T(8,128)(2,1)S(1)}, u32[]{:S(2)}, u32[]{:S(2)}) collective-permute-start(bf16[256,16,64]{0,2,1:T(8,128)(2,1)} %pad_maximum_fusion.7), channel_id=1, source_target_pairs={{0,2},{1,3},{2,4},{3,5},{4,6},{5,7},{8,10},{9,11},{10,12},{11,13},... | collective-permute-start | bytes 1572872 | tf_op jit(solution)/shard_map/ppermute | solution.py:20
  125.2 33.3 %collective-permute-start.5 = (bf16[256,16,64]{0,2,1:T(8,128)(2,1)}, bf16[256,16,64]{0,2,1:T(8,128)(2,1)S(1)}, u32[]{:S(2)}, u32[]{:S(2)}) collective-permute-start(bf16[256,16,64]{0,2,1:T(8,128)(2,1)} %pad_maximum_fusion.7), channel_id=1, source_target_pairs={{0,1},{1,2},{2,3},{3,4},{4,5},{5,6},{6,7},{8,9},{9,10},{10,11},{11... | collective-permute-start | bytes 1572872 | tf_op jit(solution)/shard_map/ppermute | solution.py:20
  127.7 33.0 %collective-permute-start.3 = (bf16[256,16,64]{0,2,1:T(8,128)(2,1)}, bf16[256,16,64]{0,2,1:T(8,128)(2,1)S(1)}, u32[]{:S(2)}, u32[]{:S(2)}) collective-permute-start(bf16[256,16,64]{0,2,1:T(8,128)(2,1)} %pad_maximum_fusion.7), channel_id=1, source_target_pairs={{1,0},{2,1},{3,2},{4,3},{5,4},{6,5},{7,6},{9,8},{10,9},{11,10},{12... | collective-permute-start | bytes 1572872 | tf_op jit(solution)/shard_map/ppermute | solution.py:20
  129.0 41.7 %collective-permute-start.1 = (bf16[256,16,64]{0,2,1:T(8,128)(2,1)}, bf16[256,16,64]{0,2,1:T(8,128)(2,1)S(1)}, u32[]{:S(2)}, u32[]{:S(2)}) collective-permute-start(bf16[256,16,64]{0,2,1:T(8,128)(2,1)} %pad_maximum_fusion.7), channel_id=1, source_target_pairs={{2,0},{3,1},{4,2},{5,3},{6,4},{7,5},{10,8},{11,9},{12,10},{13,11},... | collective-permute-start | bytes 1572872 | tf_op jit(solution)/shard_map/ppermute | solution.py:20
  132.4 44.3 %collective-permute-start.11 = (bf16[256,16,64]{0,2,1:T(8,128)(2,1)}, bf16[256,16,64]{0,2,1:T(8,128)(2,1)S(1)}, u32[]{:S(2)}, u32[]{:S(2)}) collective-permute-start(bf16[256,16,64]{0,2,1:T(8,128)(2,1)} %bitcast.119), channel_id=1, source_target_pairs={{0,2},{1,3},{2,4},{3,5},{4,6},{5,7},{8,10},{9,11},{10,12},{11,13},... | collective-permute-start | bytes 1572872 | tf_op jit(solution)/shard_map/ppermute | solution.py:20
  142.8 34.9 %collective-permute-start.10 = (bf16[256,16,64]{0,2,1:T(8,128)(2,1)S(1)}, bf16[256,16,64]{0,2,1:T(8,128)(2,1)S(1)}, u32[]{:S(2)}, u32[]{:S(2)}) collective-permute-start(bf16[256,16,64]{0,2,1:T(8,128)(2,1)S(1)} %bitcast.120), channel_id=1, source_target_pairs={{0,1},{1,2},{2,3},{3,4},{4,5},{5,6},{6,7},{8,9},{9,10},{10,11},{11... | collective-permute-start | bytes 1572872 | tf_op jit(solution)/shard_map/ppermute | solution.py:20
  158.5 27.8 %collective-permute-start.8 = (bf16[256,16,64]{0,2,1:T(8,128)(2,1)S(1)}, bf16[256,16,64]{0,2,1:T(8,128)(2,1)S(1)}, u32[]{:S(2)}, u32[]{:S(2)}) collective-permute-start(bf16[256,16,64]{0,2,1:T(8,128)(2,1)S(1)} %bitcast.121), channel_id=1, source_target_pairs={{2,0},{3,1},{4,2},{5,3},{6,4},{7,5},{10,8},{11,9},{12,10},{13,11},... | collective-permute-start | bytes 1572872 | tf_op jit(solution)/shard_map/ppermute | solution.py:20
  160.7 26.7 %collective-permute-start.9 = (bf16[256,16,64]{0,2,1:T(8,128)(2,1)S(1)}, bf16[256,16,64]{0,2,1:T(8,128)(2,1)S(1)}, u32[]{:S(2)}, u32[]{:S(2)}) collective-permute-start(bf16[256,16,64]{0,2,1:T(8,128)(2,1)S(1)} %bitcast.122), channel_id=1, source_target_pairs={{1,0},{2,1},{3,2},{4,3},{5,4},{6,5},{7,6},{9,8},{10,9},{11,10},{12... | collective-permute-start | bytes 1572872 | tf_op jit(solution)/shard_map/ppermute | solution.py:20
  189.6 157.1 %copy-start.11 = (bf16[256,16,64]{0,2,1:T(8,128)(2,1)}, bf16[256,16,64]{0,2,1:T(8,128)(2,1)S(1)}, u32[]{:S(2)}) copy-start(bf16[256,16,64]{0,2,1:T(8,128)(2,1)S(1)} %get-tuple-element.63) | copy-start | bytes 1572868
  192.8 144.6 %copy-start.57 = (f32[256]{0:T(256)}, f32[256]{0:T(256)S(1)}, u32[]{:S(2)}) copy-start(f32[256]{0:T(256)S(1)} %multiply_reduce_fusion.3) | copy-start | bytes 3076
  455.5 316.1 %reduce-scatter.11.cloned.1.call-start = ((), (), s32[]{:S(2)}) async-start(), calls=%async_computation.11 | async-start | bytes 12091392 | tf_op jit(solution)/shard_map/reduce_scatter | solution.py:229
  462.8 518.8 %reduce-scatter.5.cloned.1.call-start = ((), (), s32[]{:S(2)}) async-start(), calls=%async_computation.8 | async-start | bytes 14155776 | tf_op jit(solution)/shard_map/reduce_scatter | solution.py:225
  471.7 67.2 %collective-permute-start.19 = (bf16[256,16,64]{0,2,1:T(8,128)(2,1)S(1)}, bf16[256,16,64]{0,2,1:T(8,128)(2,1)S(1)}, u32[]{:S(2)}, u32[]{:S(2)}) collective-permute-start(bf16[256,16,64]{0,2,1:T(8,128)(2,1)S(1)} %fusion.43), channel_id=1, source_target_pairs={{2,0},{3,1},{4,2},{5,3},{6,4},{7,5},{10,8},{11,9},{12,10},{13,11},... | collective-permute-start | bytes 1572872 | tf_op jit(solution)/shard_map/ppermute | solution.py:20
  475.5 44.1 %collective-permute-start.15 = (bf16[256,16,64]{0,2,1:T(8,128)(2,1)S(1)}, bf16[256,16,64]{0,2,1:T(8,128)(2,1)S(1)}, u32[]{:S(2)}, u32[]{:S(2)}) collective-permute-start(bf16[256,16,64]{0,2,1:T(8,128)(2,1)S(1)} %fusion.36), channel_id=1, source_target_pairs={{2,0},{3,1},{4,2},{5,3},{6,4},{7,5},{10,8},{11,9},{12,10},{13,11},... | collective-permute-start | bytes 1572872 | tf_op jit(solution)/shard_map/ppermute | solution.py:20
  479.3 41.6 %collective-permute-start.14 = (bf16[256,16,64]{0,2,1:T(8,128)(2,1)S(1)}, bf16[256,16,64]{0,2,1:T(8,128)(2,1)S(1)}, u32[]{:S(2)}, u32[]{:S(2)}) collective-permute-start(bf16[256,16,64]{0,2,1:T(8,128)(2,1)S(1)} %fusion.37), channel_id=1, source_target_pairs={{1,0},{2,1},{3,2},{4,3},{5,4},{6,5},{7,6},{9,8},{10,9},{11,10},{12... | collective-permute-start | bytes 1572872 | tf_op jit(solution)/shard_map/ppermute | solution.py:20
  483.1 51.2 %collective-permute-start.13 = (bf16[256,16,64]{0,2,1:T(8,128)(2,1)S(1)}, bf16[256,16,64]{0,2,1:T(8,128)(2,1)S(1)}, u32[]{:S(2)}, u32[]{:S(2)}) collective-permute-start(bf16[256,16,64]{0,2,1:T(8,128)(2,1)S(1)} %fusion.38), channel_id=1, source_target_pairs={{0,1},{1,2},{2,3},{3,4},{4,5},{5,6},{6,7},{8,9},{9,10},{10,11},{11... | collective-permute-start | bytes 1572872 | tf_op jit(solution)/shard_map/ppermute | solution.py:20
  490.1 47.5 %collective-permute-start.12 = (bf16[256,16,64]{0,2,1:T(8,128)(2,1)S(1)}, bf16[256,16,64]{0,2,1:T(8,128)(2,1)S(1)}, u32[]{:S(2)}, u32[]{:S(2)}) collective-permute-start(bf16[256,16,64]{0,2,1:T(8,128)(2,1)S(1)} %fusion.39), channel_id=1, source_target_pairs={{0,2},{1,3},{2,4},{3,5},{4,6},{5,7},{8,10},{9,11},{10,12},{11,13},... | collective-permute-start | bytes 1572872 | tf_op jit(solution)/shard_map/ppermute | solution.py:20
  519.6 19.4 %collective-permute-start.18 = (bf16[256,16,64]{0,2,1:T(8,128)(2,1)S(1)}, bf16[256,16,64]{0,2,1:T(8,128)(2,1)S(1)}, u32[]{:S(2)}, u32[]{:S(2)}) collective-permute-start(bf16[256,16,64]{0,2,1:T(8,128)(2,1)S(1)} %fusion.42), channel_id=1, source_target_pairs={{1,0},{2,1},{3,2},{4,3},{5,4},{6,5},{7,6},{9,8},{10,9},{11,10},{12... | collective-permute-start | bytes 1572872 | tf_op jit(solution)/shard_map/ppermute | solution.py:20
  520.9 36.7 %collective-permute-start.17 = (bf16[256,16,64]{0,2,1:T(8,128)(2,1)S(1)}, bf16[256,16,64]{0,2,1:T(8,128)(2,1)S(1)}, u32[]{:S(2)}, u32[]{:S(2)}) collective-permute-start(bf16[256,16,64]{0,2,1:T(8,128)(2,1)S(1)} %fusion.41), channel_id=1, source_target_pairs={{0,1},{1,2},{2,3},{3,4},{4,5},{5,6},{6,7},{8,9},{9,10},{10,11},{11... | collective-permute-start | bytes 1572872 | tf_op jit(solution)/shard_map/ppermute | solution.py:20
  534.3 23.2 %collective-permute-start.16 = (bf16[256,16,64]{0,2,1:T(8,128)(2,1)S(1)}, bf16[256,16,64]{0,2,1:T(8,128)(2,1)S(1)}, u32[]{:S(2)}, u32[]{:S(2)}) collective-permute-start(bf16[256,16,64]{0,2,1:T(8,128)(2,1)S(1)} %fusion.40), channel_id=1, source_target_pairs={{0,2},{1,3},{2,4},{3,5},{4,6},{5,7},{8,10},{9,11},{10,12},{11,13},... | collective-permute-start | bytes 1572872 | tf_op jit(solution)/shard_map/ppermute | solution.py:20
  564.7 770.9 %reduce-scatter.9.cloned.1.call-start = ((), (), s32[]{:S(2)}) async-start(), calls=%async_computation.10 | async-start | bytes 24182784 | tf_op jit(solution)/shard_map/reduce_scatter | solution.py:228
  576.3 829.7 %all-reduce.7.cloned.1.call-start = ((), (), s32[]{:S(2)}) async-start(), calls=%async_computation.12 | async-start | bytes 6127616 | tf_op jit(solution)/shard_map/psum | solution.py:233
  (65 other events, 892.7 us)
Sparse Core Ops, SparseCore 0:
  10.2 101.7 all-gather.6
  114.1 63.4 all-gather.8
  179.9 157.4 all-gather.10
  339.4 86.0 all-gather.12
  455.7 130.4 reduce-scatter.6
  590.1 181.4 reduce-scatter.10
  775.2 206.3 reduce-scatter.4
  985.4 350.0 reduce-scatter.8
  1338.9 67.0 all-reduce.6
where the time goes:
time: 1430 us; the launch traced here: 1420 us
  waiting for transfers between devices  1110 us (78%)
  matrix products  109 us (8%)
  starting transfers between devices  66.2 us (5%)
  blocking collectives  61.8 us (4%)
  other arithmetic  38.6 us (3%)
  between operations  16.2 us (1%)
  local copies, waits for them, and re-layouts  14.7 us (1%)
    reduce_scatter x1, waiting for transfers between devices, on_device(): lax.psum_scatter(expand_grad, 'seq', scatter_dimension=0, tiled=True)  352 us
    reduce_scatter x1, waiting for transfers between devices, on_device(): lax.psum_scatter(joint_grad, 'seq', scatter_dimension=0, tiled=True)  208 us
    reduce_scatter x1, waiting for transfers between devices, on_device(): lax.psum_scatter(shrink_grad, 'seq', scatter_dimension=0, tiled=True)  184 us
    all_gather x1, waiting for transfers between devices, on_device(): lax.all_gather(expand_weight, 'seq', axis=0, tiled=True)  145 us
    all_gather x1, waiting for transfers between devices, on_device(): lax.all_gather(shrink_weight, 'seq', axis=0, tiled=True)  78.7 us
    ppermute x20, starting transfers between devices, from_behind(): return lax.ppermute(block, axis, route)  65.4 us
    ppermute x20, waiting for transfers between devices, from_behind(): return lax.ppermute(block, axis, route)  61.6 us
    all_gather x1, waiting for transfers between devices, on_device(): lax.all_gather(joint_weight, 'seq', axis=0, tiled=True)  48.9 us
  transfers between devices with their start and end apart: 29, of which 13 were waited for; matrix products, arithmetic and copies ran while one was open for 8% of the time, Pallas kernels for 0%

commit v1 on v0

v1 whole, which is shorter than its diff:
```python
import functools

import jax
import jax.numpy as jnp
from jax import lax
from jax.experimental import pallas as pl
from jax.experimental.pallas import tpu as pltpu
from jax.sharding import PartitionSpec as P

HEADS = 16
HEAD_DIM = 64
FF = 2624
HALO = 512
EPSILON = 1e-05
THETA = 160000.0
SCALE = 0.125
LANES = 128
GROUP = 256
FAR = -1e6
BF = jnp.bfloat16
F32 = jnp.float32


def dot(left, right):
    return jnp.dot(left, right, preferred_element_type=F32)


def inner_rows(left, right):
    return lax.dot_general(left, right, (((0,), (0,)), ((), ())), preferred_element_type=F32)


def outer_rows(left, right):
    return lax.dot_general(left, right, (((1,), (1,)), ((), ())), preferred_element_type=F32)


def pick(flag, one, two):
    return [jnp.where(flag, a, b) for a, b in zip(one, two)]


def centre(rows):
    middle = jnp.mean(rows, axis=-1, keepdims=True)
    centered = rows - middle
    spread = jnp.mean(centered * centered, axis=-1, keepdims=True)
    scale = lax.rsqrt(spread + EPSILON)
    return centered * scale, scale


def centre_back(normal, scale, grads):
    return scale * (
        grads
        - jnp.mean(grads, axis=-1, keepdims=True)
        - normal * jnp.mean(grads * normal, axis=-1, keepdims=True)
    )


def two_parts(values):
    high = lax.reduce_precision(values, 8, 7)
    return high.astype(BF), (values - high).astype(BF)


def swap_core(array):
    return lax.ppermute(array, "rep", [(i, i ^ 1) for i in range(lax.axis_size("rep"))])


def swap_far(array):
    return lax.ppermute(array, "rep", [(i, i ^ 2) for i in range(lax.axis_size("rep"))])


class Direct:
    depth = 4

    def __init__(self):
        self.place = lax.axis_index("seq")
        self.z = self.place // 2
        self.y = self.place % 2
        self.x = lax.axis_index("rep") // 2
        self.core = lax.axis_index("rep") % 2
        self.front = self.core == 0

    def halves(self, four):
        rows, once, other, last = four
        return (
            (rows, jnp.where(self.front, other, once)),
            (jnp.where(self.front, once, other), last),
        )

    def along(self, array, steps):
        n = self.depth
        route = [(s, 2 * ((s // 2 + steps) % n) + s % 2) for s in range(2 * n)]
        return lax.ppermute(array, "seq", route)

    def cross(self, array, turn):
        n = 2 * self.depth
        route = []
        for r in range(4):
            for s in range(n):
                to = (r ^ 2, s) if r % 2 == turn else (r, s ^ 1)
                route.append((r * n + s, to[0] * n + to[1]))
        return lax.ppermute(array, ("rep", "seq"), route)

    def collect(self, piece):
        return jnp.concatenate([piece] + [self.along(piece, k) for k in (1, 2, 3)], axis=0)

    def share(self, rows):
        once = self.cross(rows, 0)
        other = self.cross(rows, 1)
        last = self.cross(once, 1)
        return rows, once, other, last

    def to_near(self, grid):
        n = self.depth
        turned = [pick(self.y == 0, grid[z], grid[z][::-1]) for z in range(n)]
        near = []
        for y in (0, 1):
            line = [turned[-k % n][y] for k in range(n)]
            line = pick(self.z % 2 == 1, line[-1:] + line[:-1], line)
            near.append(pick(self.z // 2 == 1, line[-2:] + line[:-2], line))
        return near

    def to_mesh(self, near):
        n = self.depth
        lines = []
        for line in near:
            line = pick(self.z // 2 == 1, line[2:] + line[:2], line)
            line = pick(self.z % 2 == 1, line[1:] + line[:1], line)
            lines.append([line[-z % n] for z in range(n)])
        return [pick(self.y == 0, [lines[0][z], lines[1][z]], [lines[1][z], lines[0][z]]) for z in range(n)]

    def rows_of(self, size):
        n = self.depth
        return [
            (2 * ((self.z - k) % n) + (self.y + y) % 2) * size for y in (0, 1) for k in range(n)
        ]

    def order(self, array, size):
        n = self.depth
        cut = lambda s: array[..., s * size : (s + 1) * size]
        near = self.to_near([[cut(2 * z), cut(2 * z + 1)] for z in range(n)])
        return jnp.concatenate(near[0] + near[1], axis=-1)

    def restore(self, array, size):
        n = self.depth
        cut = lambda j: array[..., j * size : (j + 1) * size]
        grid = self.to_mesh([[cut(n * y + k) for k in range(n)] for y in (0, 1)])
        return jnp.concatenate([part for pair in grid for part in pair], axis=-1)

    def down(self, blocks):
        total = blocks[0].astype(F32)
        for k in (1, 2, 3):
            total = total + self.along(blocks[k], -k).astype(F32)
        return total.astype(BF)

    def reduce(self, left, near, far):
        half = left.shape[1] // 2
        rows = half // self.depth
        top, bottom = left[:, :half], left[:, half:]
        last = inner_rows(bottom, far).astype(BF)
        other = inner_rows(
            jnp.where(self.front, bottom, top), jnp.where(self.front, near, far)
        ).astype(BF)
        last_in = self.cross(last, 1)
        other_in = self.cross(other, 1)
        once = inner_rows(jnp.where(self.front, top, bottom), jnp.where(self.front, far, near))
        once_in = self.cross((once + last_in).astype(BF), 0)
        mine = (inner_rows(top, near) + other_in + once_in).astype(BF)
        return self.down([mine[k * rows : (k + 1) * rows] for k in range(self.depth)])

    def reduce_rows(self, left, near, far):
        rows = left.shape[1] // (2 * self.depth)
        blocks = []
        for part in (near, far):
            whole = inner_rows(left, part).astype(BF)
            cut = lambda s: whole[s * rows : (s + 1) * rows]
            lines = self.to_near([[cut(2 * z), cut(2 * z + 1)] for z in range(self.depth)])
            blocks.append([jnp.concatenate(line, axis=0) for line in lines])
        last_in = self.cross(blocks[1][1], 1)
        other_in = self.cross(jnp.where(self.front, blocks[0][1], blocks[1][0]), 1)
        once = jnp.where(self.front, blocks[1][0], blocks[0][1])
        once_in = self.cross((once.astype(F32) + last_in).astype(BF), 0)
        mine = (blocks[0][0].astype(F32) + other_in + once_in).astype(BF)
        return self.down([mine[k * rows : (k + 1) * rows] for k in range(self.depth)])


class Plain:
    def __init__(self):
        self.x = lax.axis_index("rep") // 2
        self.core = lax.axis_index("rep") % 2
        self.front = jnp.bool_(True)

    def collect(self, piece):
        return lax.all_gather(piece, "seq", axis=0, tiled=True)

    def share(self, near):
        far = swap_far(near)
        half = near.shape[0] // 2
        return near[:half], far[:half], near[half:], far[half:]

    def halves(self, four):
        return (four[0], four[2]), (four[1], four[3])

    def rows_of(self, size):
        return [jnp.int32(0), jnp.int32(lax.axis_size("seq") // 2 * size)]

    def order(self, array, size):
        return array

    def restore(self, array, size):
        return array

    def reduce(self, left, near, far):
        mine = inner_rows(left, near) + swap_far(inner_rows(left, far).astype(BF))
        return lax.psum_scatter(mine, "seq", scatter_dimension=0, tiled=True).astype(BF)

    reduce_rows = reduce


def times_back(near_grads, far_grads, near, far):
    return jnp.concatenate(
        [
            outer_rows(near_grads, near[0]) + outer_rows(far_grads, far[0]),
            outer_rows(near_grads, near[1]) + outer_rows(far_grads, far[1]),
        ],
        axis=-1,
    )


def lane_masks():
    lane = lax.broadcasted_iota(jnp.int32, (1, GROUP), 1)
    turned = [(lane % LANES) // (HEAD_DIM // 2) == i for i in range(4)]
    plain = [lane // HEAD_DIM == i for i in range(4)]
    return turned, plain


def only(mask, array):
    return jnp.where(mask, array, jnp.zeros_like(array))


def mix_kernel(rows, near_top, near_bottom, far_top, far_bottom, cosine, sine, near, far):
    half = near_top.shape[0]
    c, s = cosine[...], sine[...]
    for top, bottom, out in ((near_top, near_bottom, near), (far_top, far_bottom, far)):
        raw = dot(rows[:, :half], top[...]) + dot(rows[:, half:], bottom[...])
        for kind, scale in ((0, SCALE), (1, 1.0)):
            at = kind * GROUP
            a, b = raw[:, at : at + LANES], raw[:, at + LANES : at + GROUP]
            out[:, at : at + LANES] = ((a * c - b * s) * scale).astype(BF)
            out[:, at + LANES : at + GROUP] = ((b * c + a * s) * scale).astype(BF)
        out[:, 2 * GROUP :] = raw[:, 2 * GROUP :].astype(BF)


def attend_kernel(q0, k0, v0, q1, k1, v1, doc_row, doc_column, attended, logs):
    turned, plain = lane_masks()
    allowed = doc_column[...] == doc_row[...]
    lane = lax.broadcasted_iota(jnp.int32, (1, LANES), 1)
    totals = jnp.zeros((q0.shape[0], LANES), F32)
    for group, (q, k, v) in enumerate(((q0, k0, v0), (q1, k1, v1))):
        queries, keys, values = q[...], k[...], v[...]
        kept = jnp.zeros(queries.shape, F32)
        for i in range(4):
            raw = outer_rows(only(turned[i], queries), keys)
            raw = jnp.where(allowed, raw, -jnp.inf)
            top = jnp.max(raw, axis=-1, keepdims=True)
            weights = jnp.exp(raw - top)
            total = jnp.sum(weights, axis=-1, keepdims=True)
            found = dot(weights.astype(BF), values) / total
            kept = jnp.where(plain[i], found, kept)
            totals = jnp.where(lane == 4 * group + i, top + jnp.log(total), totals)
        attended[:, group * GROUP : (group + 1) * GROUP] = kept
    logs[...] = totals


def query_kernel(q0, k0, v0, q1, k1, v1, d_out, doc_row, doc_column, logs, delta, d_q):
    turned, plain = lane_masks()
    allowed = doc_column[...] == doc_row[...]
    for group, (q, k, v) in enumerate(((q0, k0, v0), (q1, k1, v1))):
        queries, keys, values = q[...], k[...], v[...]
        grads = d_out[:, group * GROUP : (group + 1) * GROUP]
        kept = jnp.zeros(queries.shape, F32)
        for i in range(4):
            at = 4 * group + i
            raw = outer_rows(only(turned[i], queries), keys)
            weights = jnp.where(allowed, jnp.exp(raw - logs[:, at : at + 1]), 0.0)
            d_weights = outer_rows(only(plain[i], grads), values)
            d_raw = (weights * (d_weights - delta[:, at : at + 1])).astype(BF)
            kept = jnp.where(turned[i], dot(d_raw, keys), kept)
        d_q[:, group * GROUP : (group + 1) * GROUP] = kept * SCALE


def key_kernel(q0, k0, v0, q1, k1, v1, d_out, doc_row, doc_column, logs, delta, d_k, d_v):
    turned, plain = lane_masks()
    allowed = doc_column[...] == doc_row[...]
    for group, (q, k, v) in enumerate(((q0, k0, v0), (q1, k1, v1))):
        queries, keys, values = q[...], k[...], v[...]
        grads = d_out[:, group * GROUP : (group + 1) * GROUP]
        kept_k = jnp.zeros(keys.shape, F32)
        kept_v = jnp.zeros(keys.shape, F32)
        for i in range(4):
            at = 4 * group + i
            raw = outer_rows(only(turned[i], keys), queries)
            weights = jnp.where(allowed, jnp.exp(raw - logs[at : at + 1, :]), 0.0)
            kept_v = jnp.where(plain[i], dot(weights.astype(BF), grads), kept_v)
            d_weights = outer_rows(only(plain[i], values), grads)
            d_raw = (weights * (d_weights - delta[at : at + 1, :])).astype(BF)
            kept_k = jnp.where(turned[i], dot(d_raw, queries), kept_k)
        d_k[:, group * GROUP : (group + 1) * GROUP] = kept_k
        d_v[:, group * GROUP : (group + 1) * GROUP] = kept_v


def call_kernel(kernel, ins, outs, flops, grid=(1,)):
    moving = lambda i: (i, 0)
    specs = [
        pl.BlockSpec(block, moving if at is None else functools.partial(lambda at, i: at, at))
        for _, block, at in ins
    ]
    return pl.pallas_call(
        kernel,
        grid=grid,
        in_specs=specs,
        out_specs=tuple(pl.BlockSpec((s[0] // grid[0], s[1]), moving) for s, _ in outs),
        out_shape=tuple(jax.ShapeDtypeStruct(s, t) for s, t in outs),
        compiler_params=pltpu.CompilerParams(vmem_limit_bytes=40 * 2**20),
        cost_estimate=pl.CostEstimate(
            flops=flops, bytes_accessed=8 * 2**20, transcendentals=3 * 2**20
        ),
    )(*[a for a, _, _ in ins])


def gelu_parts(inner):
    share = 0.5 * (1.0 + lax.erf(inner * 0.7071067811865476))
    return inner * share, share + inner * (0.3989422804014327 * jnp.exp(-0.5 * inner * inner))


def hidden_kernel(marks, rows, grads, *refs):
    expand, shrink = refs[0:4], refs[4:8]
    active, near_grads, far_grads, out, d_rows = refs[8:13]
    near_w, far_w, shrink_w, semaphore = refs[13:]
    units = near_w.shape[1]
    half = near_w.shape[0] // 2
    wide = shrink[0].shape[1]
    places = marks.shape[0] - 2
    block = units // places
    front = marks[0] == 1
    near_x = marks[1] == 0

    def settled():
        found = [(expand[0], near_w.at[:half]), (expand[3], far_w.at[half:])]
        for j in range(places // 2):
            part = pl.ds(j * block, block)
            low = pl.multiple_of(marks[2 + places // 2 + j], 16)
            high = pl.multiple_of(marks[2 + j], 16)
            found.append((shrink[0].at[part], shrink_w.at[pl.ds(high, block), pl.ds(0, wide)]))
            found.append((shrink[3].at[part], shrink_w.at[pl.ds(low, block), pl.ds(wide, wide)]))
        return found

    def crossed(one, two):
        found = [(expand[two], near_w.at[half:]), (expand[one], far_w.at[:half])]
        for j in range(places // 2):
            part = pl.ds(j * block, block)
            low = pl.multiple_of(marks[2 + places // 2 + j], 16)
            high = pl.multiple_of(marks[2 + j], 16)
            found.append((shrink[two].at[part], shrink_w.at[pl.ds(low, block), pl.ds(0, wide)]))
            found.append(
                (shrink[one].at[part], shrink_w.at[pl.ds(high, block), pl.ds(wide, wide)])
            )
        return found

    @pl.when(pl.program_id(0) == 0)
    def _():
        always = [
            pltpu.make_async_copy(s, t, semaphore.at[k]) for k, (s, t) in enumerate(settled())
        ]
        for copy in always:
            copy.start()
        shift = len(always)
        for flag, one, two in ((front, 1, 2), (jnp.logical_not(front), 2, 1)):

            @pl.when(flag)
            def _():
                moved = [
                    pltpu.make_async_copy(s, t, semaphore.at[shift + k])
                    for k, (s, t) in enumerate(crossed(one, two))
                ]
                for copy in moved:
                    copy.start()
                for copy in moved:
                    copy.wait()

        for copy in always:
            copy.wait()

    x, dy = rows[...], grads[...]
    tile = 256
    for at in range(0, units, tile):
        cut = slice(at, min(at + tile, units))
        first = dot(x, near_w[:, cut])
        second = dot(x, far_w[:, cut])
        d_active = outer_rows(dy, shrink_w[cut, :])
        inner = jnp.where(near_x, first, second)
        gate = jnp.where(near_x, second, first)
        value, slope = gelu_parts(inner)
        active[:, cut] = (value * gate).astype(BF)
        d_inner = d_active * gate * slope
        d_gate = d_active * value
        near_grads[:, cut] = jnp.where(near_x, d_inner, d_gate).astype(BF)
        far_grads[:, cut] = jnp.where(near_x, d_gate, d_inner).astype(BF)
    out[...] = dot(active[...], shrink_w[...])
    d_rows[...] = outer_rows(near_grads[...], near_w[...]) + outer_rows(far_grads[...], far_w[...])


def hidden(marks, rows, grads, expand, shrink):
    count, width = rows.shape
    units = expand[0].shape[1]
    size = count // 2
    moving = lambda i: (i, 0)
    held = pl.BlockSpec(memory_space=pl.ANY)
    outs = [(units, BF), (units, BF), (units, BF), (width, F32), (width, F32)]
    return pl.pallas_call(
        hidden_kernel,
        grid=(2,),
        in_specs=[pl.BlockSpec(memory_space=pltpu.SMEM)]
        + [pl.BlockSpec((size, width), moving)] * 2
        + [held] * 8,
        out_specs=tuple(pl.BlockSpec((size, w), moving) for w, _ in outs),
        out_shape=tuple(jax.ShapeDtypeStruct((count, w), t) for w, t in outs),
        scratch_shapes=[
            pltpu.VMEM((width, units), BF),
            pltpu.VMEM((width, units), BF),
            pltpu.VMEM((units, width), BF),
            pltpu.SemaphoreType.DMA((2 * marks.shape[0],)),
        ],
        compiler_params=pltpu.CompilerParams(vmem_limit_bytes=48 * 2**20),
        cost_estimate=pl.CostEstimate(
            flops=12 * count * width * units,
            bytes_accessed=20 * 2**20,
            transcendentals=2 * count * units,
        ),
    )(marks, rows, grads, *expand, *shrink)


def after(array, *earlier):
    return lax.optimization_barrier((array,) + earlier)[0]


def on_device(
    direct,
    tokens,
    norm_first,
    joint_weight,
    output_weight,
    norm_second,
    expand_weight,
    shrink_weight,
    document_start,
    cotangent,
):
    plan = Direct() if direct else Plain()
    rows, width = tokens.shape
    length = lax.axis_size("seq")
    reach = min(HALO // rows, length - 1)
    block_count = 2 * reach + 1
    span = block_count * rows
    here = lax.axis_index("seq")
    x, core = plan.x, plan.core
    near_x = x == 0
    heads_wide = width // 2
    depth = joint_weight.shape[0]
    unit_rows = shrink_weight.shape[0]
    unit_half = (unit_rows + 1) // 2
    units = -(-unit_half * length // LANES) * LANES
    while units % length:
        units += LANES
    unit_pad = units // length
    half_width = width // 2

    def mine(array, start):
        parts = [array[:, start + i * GROUP : start + (i + 1) * GROUP] for i in range(4)]
        low, high = pick(near_x, parts[0::2], parts[1::2])
        return jnp.where(core == 0, low, high)

    source = jnp.arange(GROUP)
    turn = (
        source[:, None]
        == ((source % LANES) // 32 * HEAD_DIM + source // LANES * 32 + source % 32)[None, :]
    ).astype(BF)
    gain_one = norm_first.astype(F32)[:, None]
    gain_two = norm_second.astype(F32)[:, None]
    joint_piece = jnp.concatenate(
        [
            (dot(mine(joint_weight, 0), turn) * gain_one).astype(BF),
            (dot(mine(joint_weight, width), turn) * gain_one).astype(BF),
            (mine(joint_weight, 2 * width).astype(F32) * gain_one).astype(BF),
            mine(output_weight, 0),
        ],
        axis=1,
    )
    slot = jnp.arange(units)
    inner = core * unit_half + slot % unit_pad
    fits = (slot % unit_pad < unit_half) & (inner < unit_rows)
    unit_of = jnp.where(fits, slot // unit_pad * unit_rows + inner, -2 * FF)
    spread_units = (jnp.arange(2 * FF)[:, None] == (unit_of + x * FF)[None, :]).astype(BF)
    expand_piece = (dot(expand_weight, spread_units) * gain_two).astype(BF)
    slot_row = jnp.arange(unit_pad)

    def picked(c):
        row = c * unit_half + slot_row
        row = jnp.where((slot_row < unit_half) & (row < unit_rows), row, -1)
        return (row[:, None] == jnp.arange(unit_rows)[None, :]).astype(BF)

    shrink_piece = dot(
        picked(core),
        jnp.where(near_x, shrink_weight[:, :half_width], shrink_weight[:, half_width:]),
    ).astype(BF)

    joint_rows = plan.collect(joint_piece)
    anchor = (lax.axis_index("rep") * length + here) * rows
    position = anchor + jnp.arange(rows, dtype=jnp.int32) - document_start
    marks = jnp.pad(
        jnp.stack([(position + 1) // 16, (position + 1) % 16], axis=1), ((0, 0), (0, LANES - 2))
    ).astype(BF)
    packed = jnp.concatenate([tokens, marks], axis=1)
    offsets = [0]
    blocks = [packed]
    for offset in list(range(-reach, 0)) + list(range(1, reach + 1)):
        route = [(i + offset, i) for i in range(length) if 0 <= i + offset < length]
        offsets.append(offset)
        blocks.append(lax.ppermute(packed, "seq", route))
    sent = []
    for block in blocks:
        normal = centre(block[:, :width].astype(F32))[0].astype(BF)
        sent.append(jnp.concatenate([plan.order(normal, depth), block[:, width:]], axis=1))
    sent = jnp.concatenate(sent, axis=0)
    first = (sent, swap_core(sent))
    offset_rows = jnp.repeat(jnp.array(offsets, jnp.int32), rows) * rows
    index = (here * rows + offset_rows + jnp.tile(jnp.arange(rows), block_count)).astype(F32)
    halves = HEAD_DIM // 2
    frequency = THETA ** (-(jnp.arange(halves, dtype=F32) * 2.0) / HEAD_DIM)
    frequency = jnp.tile(frequency, LANES // halves)
    document_rows, document_columns, cosines, sines = [], [], [], []
    for rows_in in first:
        code = rows_in[:, width : width + 2].astype(F32)
        code = code[:, :1] * 16.0 + code[:, 1:]
        document = jnp.where(code > 0, index[:, None] - (code - 1.0), FAR)
        document_rows.append(document.reshape(1, span))
        document_columns.append(document[:rows])
        angle = (code - 1.0) * frequency[None, :]
        cosines.append(jnp.cos(angle))
        sines.append(jnp.sin(angle))
    cotangents = jnp.concatenate([cotangent, swap_core(cotangent)], axis=0)

    expand_rows = plan.collect(after(expand_piece, joint_rows))
    shrink_rows = plan.collect(after(shrink_piece, expand_rows))
    joint_near, joint_far = plan.halves(plan.share(joint_rows))
    expand_four = plan.share(expand_rows)
    shrink_four = plan.share(shrink_rows)
    output_mine = jnp.concatenate(
        [
            jnp.concatenate([part[:, 3 * GROUP :] for part in pair], axis=0)
            for pair in (joint_near, joint_far)
        ],
        axis=1,
    )
    output_all = jnp.concatenate([output_mine, swap_core(output_mine)], axis=1)

    def turn_columns(array):
        parts = [array[:, i * GROUP : (i + 1) * GROUP] for i in range(4)]
        parts = pick(core == 0, parts, parts[2:] + parts[:2])
        left, right = pick(near_x, parts[:2], parts[1::-1]), pick(near_x, parts[2:], parts[:1:-1])
        return jnp.concatenate(left + right, axis=-1)

    def turn_halves(array):
        left, right = array[:, :half_width], array[:, half_width:]
        return jnp.concatenate(
            [jnp.where(near_x, left, right), jnp.where(near_x, right, left)], axis=-1
        )

    mixed = []
    wide = 3 * GROUP
    half_depth = joint_near[0].shape[0]
    for t in (0, 1):
        mixed.append(
            call_kernel(
                mix_kernel,
                [(first[t], (rows, width), None)]
                + [(part, (half_depth, wide), (0, 0)) for part in joint_near + joint_far]
                + [(cosines[t], (rows, LANES), None), (sines[t], (rows, LANES), None)],
                [((span, wide), BF), ((span, wide), BF)],
                2 * span * width * 2 * wide,
                (block_count,),
            )
        )
    score_flops = 2 * rows * span * GROUP * 8
    own, every = (rows, GROUP), (span, GROUP)

    def operands(t, sizes):
        found = [
            (array, size, (0, column))
            for array in mixed[t]
            for column, size in enumerate(sizes)
        ]
        return found, [
            (document_rows[t], (1, span), (0, 0)),
            (document_columns[t], (rows, 1), (0, 0)),
        ]

    attended, logs = [], []
    for t in (0, 1):
        wide_keys, documents = operands(t, (own, every, every))
        found, found_logs = call_kernel(
            attend_kernel,
            wide_keys + documents,
            [((rows, 2 * GROUP), F32), ((rows, LANES), F32)],
            2 * score_flops,
        )
        attended.append(found)
        logs.append(found_logs)
    attended_low = jnp.concatenate(attended, axis=0).astype(BF)
    attended_there = swap_core(jnp.concatenate(attended[::-1], axis=0).astype(BF))
    attended_rows = plan.order(
        turn_columns(jnp.concatenate([attended_low, attended_there], axis=1)), depth
    )
    middle = tokens.astype(F32) + turn_columns(dot(attended_rows[:rows], output_all))
    second, second_scale = centre(middle)
    second_low = plan.order(second.astype(BF), depth)
    second_both = jnp.concatenate([second_low, swap_core(second_low)], axis=0)

    cotangents_turned = turn_halves(cotangents)
    where = jnp.stack(
        [plan.front.astype(jnp.int32), x.astype(jnp.int32)]
        + [row.astype(jnp.int32) for row in plan.rows_of(unit_pad)]
    )
    active_low, lifted_near_grad, lifted_far_grad, part, second_part = hidden(
        where, second_both, cotangents_turned, expand_four, shrink_four
    )
    part = turn_halves(part)
    result = middle + part[:rows] + swap_core(part[rows:].astype(BF)).astype(F32)
    second_grad = second_part[:rows] + swap_core(second_part[rows:].astype(BF)).astype(F32)
    middle_grad = cotangent.astype(F32) + centre_back(
        second, second_scale, plan.restore(second_grad, depth)
    )
    branch = middle_grad.astype(BF)
    branch_both = turn_columns(jnp.concatenate([branch, swap_core(branch)], axis=0))
    attended_grad = turn_columns(plan.restore(outer_rows(branch_both, output_all), depth))
    attended_grad = attended_grad[:, : 2 * GROUP].astype(BF)
    arounds, deltas = [], []
    for t in (0, 1):
        grads = attended_grad[t * rows : (t + 1) * rows]
        delta = jnp.sum(
            (grads.astype(F32) * attended[t]).reshape(rows, HEADS // 2, HEAD_DIM), axis=-1
        )
        deltas.append(delta)
        log_high, log_low = two_parts(logs[t][:, : HEADS // 2])
        delta_high, delta_low = two_parts(delta)
        around = jnp.concatenate([grads, log_high, log_low, delta_high, delta_low], axis=1)
        arounds.append(jnp.pad(around, ((0, 0), (0, -around.shape[1] % LANES))))
    around = jnp.stack(arounds)
    blocks = [around]
    for offset in offsets[1:]:
        route = [(i + offset, i) for i in range(length) if 0 <= i + offset < length]
        blocks.append(lax.ppermute(around, "seq", route))

    mixed_grads = [[], []]
    for t in (0, 1):
        wide_keys, documents = operands(t, (own, every, every))
        (query_grad,) = call_kernel(
            query_kernel,
            wide_keys
            + [(arounds[t], (rows, 2 * GROUP), (0, 0))]
            + documents
            + [(logs[t], (rows, LANES), (0, 0)), (deltas[t], (rows, HEADS // 2), (0, 0))],
            [((rows, 2 * GROUP), F32)],
            3 * score_flops,
        )
        there = jnp.concatenate([block[t] for block in blocks], axis=0)
        numbers = there[:, 2 * GROUP : 2 * GROUP + 32].astype(F32).T
        wide_keys, documents = operands(t, (every, own, own))
        key_grad, value_grad = call_kernel(
            key_kernel,
            wide_keys
            + [(there, (span, 2 * GROUP), (0, 0))]
            + documents
            + [
                (numbers[:8] + numbers[8:16], (HEADS // 2, span), (0, 0)),
                (numbers[16:24] + numbers[24:], (HEADS // 2, span), (0, 0)),
            ],
            [((rows, 2 * GROUP), F32), ((rows, 2 * GROUP), F32)],
            4 * score_flops,
        )
        c, s = cosines[t][:rows], sines[t][:rows]
        for i in (0, 1):
            parts = []
            for grads in (query_grad, key_grad):
                a = grads[:, i * GROUP : i * GROUP + LANES]
                b = grads[:, i * GROUP + LANES : (i + 1) * GROUP]
                parts += [a * c + b * s, b * c - a * s]
            parts.append(value_grad[:, i * GROUP : (i + 1) * GROUP])
            mixed_grads[i].append(jnp.concatenate(parts, axis=1).astype(BF))
    mixed_grads = [jnp.concatenate(pair, axis=0) for pair in mixed_grads]
    first_part = times_back(
        mixed_grads[0],
        mixed_grads[1],
        [part[:, :wide] for part in joint_near],
        [part[:, :wide] for part in joint_far],
    )
    first_grad = first_part[:rows] + swap_core(first_part[rows:].astype(BF)).astype(F32)
    normal, normal_scale = centre(tokens.astype(F32))
    tokens_grad = middle_grad + centre_back(
        normal, normal_scale, plan.restore(first_grad, depth)
    )

    shrink_share = plan.reduce_rows(
        active_low, cotangents_turned[:, :half_width], cotangents_turned[:, half_width:]
    )
    expand_share = plan.reduce(second_both, lifted_near_grad, lifted_far_grad)
    output_share = plan.reduce(
        attended_rows, branch_both[:, :GROUP], branch_both[:, GROUP : 2 * GROUP]
    )
    joint_share = plan.reduce(
        jnp.concatenate([rows_in[:rows, :width] for rows_in in first], axis=0),
        mixed_grads[0],
        mixed_grads[1],
    )

    def spread(share):
        pair = [share, swap_far(share)]
        low, high = pick(near_x, pair, pair[::-1])
        both = jnp.concatenate([low, high], axis=1)
        there = swap_core(both)
        size = share.shape[1]
        cores = pick(core == 0, [both, there], [there, both])
        return [[part[:, :size], part[:, size:]] for part in cores]

    shrink_shares = spread(shrink_share)
    shrink_grad = jnp.concatenate(
        [
            inner_rows(picked(0), shrink_shares[0][i]) + inner_rows(picked(1), shrink_shares[1][i])
            for i in (0, 1)
        ],
        axis=1,
    )
    expand_shares = spread(expand_share)
    expand_halves = []
    for i in (0, 1):
        total = 0.0
        for c in (0, 1):
            inner = c * unit_half + slot % unit_pad
            fits = (slot % unit_pad < unit_half) & (inner < unit_rows)
            unit_at = jnp.where(fits, slot // unit_pad * unit_rows + inner, -1)
            back = (unit_at[:, None] == jnp.arange(FF)[None, :]).astype(BF)
            total = total + dot(expand_shares[c][i], back)
        expand_halves.append(total)
    expand_raw = jnp.concatenate(expand_halves, axis=1)
    expand_grad = expand_raw * gain_two
    second_gain_grad = jnp.sum(expand_raw * expand_weight.astype(F32), axis=1)
    output_shares = spread(output_share)
    output_grad = jnp.concatenate(output_shares[0] + output_shares[1], axis=1).astype(F32)
    joint_four = spread(joint_share)
    columns = []
    for kind in range(3):
        for c in (0, 1):
            for i in (0, 1):
                piece = joint_four[c][i][:, kind * GROUP : (kind + 1) * GROUP]
                columns.append(
                    lax.dot_general(
                        piece, turn, (((1,), (1,)), ((), ())), preferred_element_type=F32
                    )
                    if kind < 2
                    else piece.astype(F32)
                )
    joint_raw = jnp.concatenate(columns, axis=1)
    joint_grad = joint_raw * gain_one
    first_gain_grad = jnp.sum(joint_raw * joint_weight.astype(F32), axis=1)
    return (
        result.astype(BF),
        tokens_grad.astype(BF),
        first_gain_grad,
        joint_grad,
        output_grad,
        second_gain_grad,
        expand_grad,
        shrink_grad,
    )


def solution(mesh):
    placed = (
        P(("rep", "seq"), None),
        P("seq"),
        P("seq", None),
        P("seq", None),
        P("seq"),
        P("seq", None),
        P("seq", None),
        P(("rep", "seq")),
        P(("rep", "seq"), None),
    )
    return jax.shard_map(
        functools.partial(on_device, mesh.shape["seq"] == 8),
        mesh=mesh,
        in_specs=placed,
        out_specs=(
            P(("rep", "seq"), None),
            P(("rep", "seq"), None),
            P("seq"),
            P("seq", None),
            P("seq", None),
            P("seq"),
            P("seq", None),
            P("seq", None),
        ),
        check_vma=False,
    )
```

time: 1430 us -> 674 us (0.47)
  waiting for transfers between devices: 1110 us -> 209 us
  local copies, waits for them, and re-layouts: 14.7 us -> 109 us
  other arithmetic: 38.6 us -> 117 us
  blocking collectives: 61.8 us -> 0 us
  Pallas kernels: 0 us -> 60.1 us
  matrix products: 109 us -> 64.9 us
  starting transfers between devices: 66.2 us -> 104 us
    reduce_scatter x4 -> x0, waiting for transfers between devices: 745 us -> none  [the longest x1 352 us: on_device(): lax.psum_scatter(expand_grad, 'seq', scatter_dimension=0, tiled=True)]
    all_gather x4 -> x0, waiting for transfers between devices: 272 us -> none  [the longest x1 145 us: on_device(): lax.all_gather(expand_weight, 'seq', axis=0, tiled=True)]
    ppermute x20 -> x67, waiting for transfers between devices: 61.6 us -> 209 us  [the longest x21 71.4 us: along(): return lax.ppermute(array, 'seq', route)]
    pallas_call x0 -> x9, Pallas kernels: none -> 60.1 us  [the longest x8 42.9 us: call_kernel(): pl.pallas_call(kernel, grid=grid, in_specs=specs, out_specs=tuple((pl.Blo...]
    unnamed x139 -> x368, local copies, waits for them, and re-layouts: 6.75 us -> 58.1 us
    unnamed x0 -> x77, other arithmetic: none -> 49.4 us
    ppermute x20 -> x67, starting transfers between devices: 65.4 us -> 104 us  [the longest x21 38.7 us: along(): return lax.ppermute(array, 'seq', route)]
    all_gather x2 -> x0, blocking collectives: 35.8 us -> none  [the longest x1 19.5 us: on_device(): lax.all_gather(norm_first, 'seq', axis=0, tiled=True)]
  transfers between devices with their start and end apart: 29 -> 67, of which waited for: 13 -> 21; matrix products, arithmetic and copies ran while one was open for 8% -> 32% of each run, Pallas kernels for 0% -> 6%
where the time goes in v1:
time: 674 us; the launch traced here: 668 us
  waiting for transfers between devices  209 us (31%)
  other arithmetic  117 us (17%)
  local copies, waits for them, and re-layouts  109 us (16%)
  starting transfers between devices  104 us (15%)
  matrix products  64.9 us (10%)
  Pallas kernels  60.1 us (9%)
    ppermute x21, waiting for transfers between devices, along(): return lax.ppermute(array, 'seq', route)  71.4 us
    unnamed x368, local copies, waits for them, and re-layouts  58.1 us
    ppermute x21, waiting for transfers between devices, cross(): return lax.ppermute(array, ('rep', 'seq'), route)  52 us
    unnamed x77, other arithmetic  49.4 us
    pallas_call x8, Pallas kernels, call_kernel(): pl.pallas_call(kernel, grid=grid, in_specs=specs, out_specs=tuple((pl.Blo...  42.9 us
    ppermute x4, waiting for transfers between devices, on_device(): blocks.append(lax.ppermute(around, 'seq', route))  40.1 us
    ppermute x21, starting transfers between devices, along(): return lax.ppermute(array, 'seq', route)  38.7 us
    ppermute x21, starting transfers between devices, cross(): return lax.ppermute(array, ('rep', 'seq'), route)  36.1 us
  transfers between devices with their start and end apart: 67, of which 21 were waited for; matrix products, arithmetic and copies ran while one was open for 32% of the time, Pallas kernels for 6%

profile of v1, /device:TPU:0, one launch (start us, length us, event | category | flops | bytes accessed | tf_op | source)
XLA Modules:
  0.0 667.9 jit_solution(6182451585075559206)
XLA Ops:
  5.7 5.1 collective-permute-start.7
  22.4 23.5 %collective-permute-done.3 = bf16[256,1152]{0,1:T(8,128)(2,1)S(1)} collective-permute-done((bf16[256,1152]{0,1:T(8,128)(2,1)S(1)}, bf16[256,1152]{0,1:T(8,128)(2,1)S(1)}, u32[]{:S(2)}, u32[]{:S(2)}) %collective-permute-start.3) | collective-permute-done | bytes 589856 | tf_op jit(solution)/shard_map/ppermute | solution.py:526
  49.1 10.9 %collective-permute-start = (bf16[256,1152]{0,1:T(8,128)(2,1)S(1)}, bf16[256,1152]{0,1:T(8,128)(2,1)S(1)}, u32[]{:S(2)}, u32[]{:S(2)}) collective-permute-start(bf16[256,1152]{0,1:T(8,128)(2,1)S(1)} %pad_maximum_fusion.15), channel_id=1, source_target_pairs={{0,2},{1,3},{2,4},{3,5},{4,6},{5,7},{8,10},{9,11},{10,12},{11,13},... | collective-permute-start | bytes 1769480 | tf_op jit(solution)/shard_map/ppermute | solution.py:526
  60.2 9.4 %collective-permute-done.1 = bf16[256,1152]{0,1:T(8,128)(2,1)S(1)} collective-permute-done((bf16[256,1152]{0,1:T(8,128)(2,1)S(1)}, bf16[256,1152]{0,1:T(8,128)(2,1)S(1)}, u32[]{:S(2)}, u32[]{:S(2)}) %collective-permute-start.1) | collective-permute-done | bytes 589856 | tf_op jit(solution)/shard_map/ppermute | solution.py:526
  97.1 5.7 fusion.17
  114.7 5.5 copy.23.rows
  120.2 8.1 %collective-permute-done.15 = bf16[128,1408]{1,0:T(8,128)(2,1)S(1)} collective-permute-done((bf16[128,1408]{1,0:T(8,128)(2,1)S(1)}, bf16[128,1408]{1,0:T(8,128)(2,1)S(1)}, u32[]{:S(2)}, u32[]{:S(2)}) %collective-permute-start.15) | collective-permute-done | bytes 360480 | tf_op jit(solution)/shard_map/ppermute | solution.py:90
  129.5 4.6 collective-permute-done.16
  134.8 14.8 %collective-permute-done.17 = bf16[128,1408]{1,0:T(8,128)(2,1)S(1)} collective-permute-done((bf16[128,1408]{1,0:T(8,128)(2,1)S(1)}, bf16[128,1408]{1,0:T(8,128)(2,1)S(1)}, u32[]{:S(2)}, u32[]{:S(2)}) %collective-permute-start.17) | collective-permute-done | bytes 360480 | tf_op jit(solution)/shard_map/ppermute | solution.py:90
  162.5 5.5 copy.20.rows
  168.0 5.9 multiply_sine_fusion.1
  178.4 5.4 shard_map.161
  183.9 4.7 shard_map.162
  200.9 5.7 shard_map.163
  206.6 4.7 shard_map.164
  236.3 23.6 %collective-permute-done.24.refs_5_ = bf16[704,512]{1,0:T(8,128)(2,1)} collective-permute-done((bf16[704,512]{1,0:T(8,128)(2,1)}, bf16[704,512]{1,0:T(8,128)(2,1)}, u32[]{:S(2)}, u32[]{:S(2)}) %collective-permute-start.24) | collective-permute-done | bytes 720928 | tf_op jit(solution)/shard_map/ppermute | solution.py:99
  290.2 4.6 collective-permute-done.20.refs_3_
  297.2 17.2 %shard_map.165 = (bf16[512,1408]{1,0:T(8,128)(2,1)}, bf16[512,1408]{1,0:T(8,128)(2,1)}, bf16[512,1408]{1,0:T(8,128)(2,1)}, f32[512,1024]{1,0:T(8,128)}, f32[512,1024]{1,0:T(8,128)}) custom-call(s32[10]{0:T(128)S(1)} %stack.71.marks, bf16[512,1024]{1,0:T(8,128)(2,1)S(1)} %copy-done.34, bf16[512,1024]{1,0:T(8,128)(2,1)S(1)} %copy-done.33, ...), custom_call_target="tpu_custom_call" | custom-call | flops 8858370048 | bytes 20971520 | tf_op jit(solution)/shard_map/pallas_call | solution.py:417
  378.7 5.3 shard_map.166
  387.6 5.5 shard_map.168
  410.3 7.3 %collective-permute-done.43 = bf16[512,256]{1,0:T(8,128)(2,1)S(1)} collective-permute-done((bf16[512,256]{1,0:T(8,128)(2,1)S(1)}, bf16[512,256]{1,0:T(8,128)(2,1)S(1)}, u32[]{:S(2)}, u32[]{:S(2)}) %collective-permute-start.43) | collective-permute-done | bytes 262176 | tf_op jit(solution)/shard_map/ppermute | solution.py:99
  435.0 9.1 %collective-permute-start.51 = (bf16[512,1408]{1,0:T(8,128)(2,1)}, bf16[512,1408]{1,0:T(8,128)(2,1)}, u32[]{:S(2)}, u32[]{:S(2)}) collective-permute-start(bf16[512,1408]{1,0:T(8,128)(2,1)} %convolution_convert_fusion.3), channel_id=1, source_target_pairs={{0,1},{1,0},{2,3},{3,2},{4,5},{5,4},{6,7},{7,6},{8,24},{9,25},{10,... | collective-permute-start | bytes 4325384 | tf_op jit(solution)/shard_map/ppermute | solution.py:99
  448.5 40.1 %collective-permute-done.32 = bf16[2,256,640]{1,2,0:T(8,128)(2,1)S(1)} collective-permute-done((bf16[2,256,640]{1,2,0:T(8,128)(2,1)S(1)}, bf16[2,256,640]{1,2,0:T(8,128)(2,1)S(1)}, u32[]{:S(2)}, u32[]{:S(2)}) %collective-permute-start.32) | collective-permute-done | bytes 655392 | tf_op jit(solution)/shard_map/ppermute | solution.py:659
  509.2 5.8 shard_map.167
  515.1 5.8 shard_map.169
  544.0 5.4 collective-permute-done.36
  555.1 7.2 %collective-permute-done.35 = bf16[512,768]{1,0:T(8,128)(2,1)S(1)} collective-permute-done((bf16[512,768]{1,0:T(8,128)(2,1)S(1)}, bf16[512,768]{1,0:T(8,128)(2,1)S(1)}, u32[]{:S(2)}, u32[]{:S(2)}) %collective-permute-start.35) | collective-permute-done | bytes 786464 | tf_op jit(solution)/shard_map/ppermute | solution.py:99
  566.8 5.5 collective-permute-start.38
  585.6 22.3 %collective-permute-done.40 = bf16[128,768]{1,0:T(8,128)(2,1)} collective-permute-done((bf16[128,768]{1,0:T(8,128)(2,1)}, bf16[128,768]{1,0:T(8,128)(2,1)}, u32[]{:S(2)}, u32[]{:S(2)}) %collective-permute-start.40) | collective-permute-done | bytes 196640 | tf_op jit(solution)/shard_map/ppermute | solution.py:90
  607.9 15.5 %collective-permute-done.39 = bf16[128,768]{1,0:T(8,128)(2,1)} collective-permute-done((bf16[128,768]{1,0:T(8,128)(2,1)}, bf16[128,768]{1,0:T(8,128)(2,1)}, u32[]{:S(2)}, u32[]{:S(2)}) %collective-permute-start.39) | collective-permute-done | bytes 196640 | tf_op jit(solution)/shard_map/ppermute | solution.py:90
  632.5 6.2 collective-permute-done.57
  648.2 4.6 fusion.2
  (775 shorter events, 353.7 us)
Async XLA Ops:
  5.7 99.2 %collective-permute-start.7 = (bf16[128,1024]{1,0:T(8,128)(2,1)S(1)}, bf16[128,1024]{1,0:T(8,128)(2,1)}, u32[]{:S(2)}, u32[]{:S(2)}) collective-permute-start(bf16[128,1024]{1,0:T(8,128)(2,1)S(1)} %pad_maximum_fusion.26), channel_id=1, source_target_pairs={{0,6},{1,7},{2,0},{3,1},{4,2},{5,3},{6,4},{7,5},{8,14},{9,15},{10,... | collective-permute-start | bytes 786440 | tf_op jit(solution)/shard_map/ppermute | solution.py:90
  10.8 94.1 %collective-permute-start.6 = (bf16[128,1024]{1,0:T(8,128)(2,1)S(1)}, bf16[128,1024]{1,0:T(8,128)(2,1)}, u32[]{:S(2)}, u32[]{:S(2)}) collective-permute-start(bf16[128,1024]{1,0:T(8,128)(2,1)S(1)} %pad_maximum_fusion.26), channel_id=1, source_target_pairs={{0,4},{1,5},{2,6},{3,7},{4,0},{5,1},{6,2},{7,3},{8,12},{9,13},{10,... | collective-permute-start | bytes 786440 | tf_op jit(solution)/shard_map/ppermute | solution.py:90
  10.8 94.1 %collective-permute-start.5 = (bf16[128,1024]{1,0:T(8,128)(2,1)S(1)}, bf16[128,1024]{1,0:T(8,128)(2,1)}, u32[]{:S(2)}, u32[]{:S(2)}) collective-permute-start(bf16[128,1024]{1,0:T(8,128)(2,1)S(1)} %pad_maximum_fusion.26), channel_id=1, source_target_pairs={{0,2},{1,3},{2,4},{3,5},{4,6},{5,7},{6,0},{7,1},{8,10},{9,11},{10,... | collective-permute-start | bytes 786440 | tf_op jit(solution)/shard_map/ppermute | solution.py:90
  97.0 61.9 %collective-permute-start.4 = (bf16[1280,1152]{0,1:T(8,128)(2,1)}, bf16[1280,1152]{0,1:T(8,128)(2,1)}, u32[]{:S(2)}, u32[]{:S(2)}) collective-permute-start(bf16[1280,1152]{0,1:T(8,128)(2,1)} %slice_dynamic-update-slice_fusion), channel_id=1, source_target_pairs={{0,8},{8,0},{16,24},{24,16},{1,9},{9,1},{17,25},{25,17},{2,10},{10... | collective-permute-start | bytes 8847368 | tf_op jit(solution)/shard_map/ppermute | solution.py:62
  109.6 43.4 %collective-permute-start.9 = (bf16[512,1024]{1,0:T(8,128)(2,1)S(1)}, bf16[512,1024]{1,0:T(8,128)(2,1)}, u32[]{:S(2)}, u32[]{:S(2)}) collective-permute-start(bf16[512,1024]{1,0:T(8,128)(2,1)S(1)} %pad_maximum_fusion.6.near_top), channel_id=1, source_target_pairs={{0,16},{1,17},{2,18},{3,19},{4,20},{5,21},{6,22},{7,23},{8,9},{9,8... | collective-permute-start | bytes 3145736 | tf_op jit(solution)/shard_map/ppermute | solution.py:99
  111.0 43.3 %collective-permute-start.8 = (bf16[512,1024]{1,0:T(8,128)(2,1)S(1)}, bf16[512,1024]{1,0:T(8,128)(2,1)S(1)}, u32[]{:S(2)}, u32[]{:S(2)}) collective-permute-start(bf16[512,1024]{1,0:T(8,128)(2,1)S(1)} %pad_maximum_fusion.6.near_top), channel_id=1, source_target_pairs={{0,1},{1,0},{2,3},{3,2},{4,5},{5,4},{6,7},{7,6},{8,24},{9,25},{10,... | collective-permute-start | bytes 3145736 | tf_op jit(solution)/shard_map/ppermute | solution.py:99
  134.0 138.0 %collective-permute-start.14 = (bf16[256,1024]{0,1:T(8,128)(2,1)}, bf16[256,1024]{0,1:T(8,128)(2,1)}, u32[]{:S(2)}, u32[]{:S(2)}) collective-permute-start(bf16[256,1024]{0,1:T(8,128)(2,1)} %copy.31), channel_id=1, source_target_pairs={{0,8},{8,0},{16,24},{24,16},{1,9},{9,1},{17,25},{25,17},{2,10},{10... | collective-permute-start | bytes 1572872 | tf_op jit(solution)/shard_map/ppermute | solution.py:62
  150.3 74.3 %collective-permute-start.23 = (bf16[176,512]{1,0:T(8,128)(2,1)}, bf16[176,512]{1,0:T(8,128)(2,1)}, u32[]{:S(2)}, u32[]{:S(2)}) collective-permute-start(bf16[176,512]{1,0:T(8,128)(2,1)} %convolution_convert_fusion.8), channel_id=1, source_target_pairs={{0,6},{1,7},{2,0},{3,1},{4,2},{5,3},{6,4},{7,5},{8,14},{9,15},{10,... | collective-permute-start | bytes 540680 | tf_op jit(solution)/shard_map/ppermute | solution.py:90
  153.0 68.6 %collective-permute-start.22 = (bf16[176,512]{1,0:T(8,128)(2,1)}, bf16[176,512]{1,0:T(8,128)(2,1)}, u32[]{:S(2)}, u32[]{:S(2)}) collective-permute-start(bf16[176,512]{1,0:T(8,128)(2,1)} %convolution_convert_fusion.8), channel_id=1, source_target_pairs={{0,4},{1,5},{2,6},{3,7},{4,0},{5,1},{6,2},{7,3},{8,12},{9,13},{10,... | collective-permute-start | bytes 540680 | tf_op jit(solution)/shard_map/ppermute | solution.py:90
  154.3 63.6 %collective-permute-start.21 = (bf16[176,512]{1,0:T(8,128)(2,1)}, bf16[176,512]{1,0:T(8,128)(2,1)}, u32[]{:S(2)}, u32[]{:S(2)}) collective-permute-start(bf16[176,512]{1,0:T(8,128)(2,1)} %convolution_convert_fusion.8), channel_id=1, source_target_pairs={{0,2},{1,3},{2,4},{3,5},{4,6},{5,7},{6,0},{7,1},{8,10},{9,11},{10,... | collective-permute-start | bytes 540680 | tf_op jit(solution)/shard_map/ppermute | solution.py:90
  217.9 72.2 %collective-permute-start.19 = (bf16[512,1408]{1,0:T(8,128)(2,1)}, bf16[512,1408]{1,0:T(8,128)(2,1)}, u32[]{:S(2)}, u32[]{:S(2)}) collective-permute-start(bf16[512,1408]{1,0:T(8,128)(2,1)} %constant_dynamic-update-slice_fusion.29.refs_0_), channel_id=1, source_target_pairs={{0,1},{1,0},{2,3},{3,2},{4,5},{5,4},{6,7},{7,6},{8,24},{9,25},{10,... | collective-permute-start | bytes 4325384 | tf_op jit(solution)/shard_map/ppermute | solution.py:99
  221.6 40.4 %collective-permute-start.18 = (bf16[512,1408]{1,0:T(8,128)(2,1)}, bf16[512,1408]{1,0:T(8,128)(2,1)}, u32[]{:S(2)}, u32[]{:S(2)}) collective-permute-start(bf16[512,1408]{1,0:T(8,128)(2,1)} %constant_dynamic-update-slice_fusion.29.refs_0_), channel_id=1, source_target_pairs={{0,16},{1,17},{2,18},{3,19},{4,20},{5,21},{6,22},{7,23},{8,9},{9,8... | collective-permute-start | bytes 4325384 | tf_op jit(solution)/shard_map/ppermute | solution.py:99
  226.2 33.8 %collective-permute-start.24 = (bf16[704,512]{1,0:T(8,128)(2,1)}, bf16[704,512]{1,0:T(8,128)(2,1)}, u32[]{:S(2)}, u32[]{:S(2)}) collective-permute-start(bf16[704,512]{1,0:T(8,128)(2,1)} %constant_dynamic-update-slice_fusion.33.refs_4_), channel_id=1, source_target_pairs={{0,16},{1,17},{2,18},{3,19},{4,20},{5,21},{6,22},{7,23},{8,9},{9,8... | collective-permute-start | bytes 2162696 | tf_op jit(solution)/shard_map/ppermute | solution.py:99
  230.0 32.0 %collective-permute-start.12 = (bf16[1024,512]{1,0:T(8,128)(2,1)S(1)}, bf16[1024,512]{1,0:T(8,128)(2,1)S(1)}, u32[]{:S(2)}, u32[]{:S(2)}) collective-permute-start(bf16[1024,512]{1,0:T(8,128)(2,1)S(1)} %maximum_maximum_fusion), channel_id=1, source_target_pairs={{0,8},{8,0},{16,24},{24,16},{1,9},{9,1},{17,25},{25,17},{2,10},{10... | collective-permute-start | bytes 3145736 | tf_op jit(solution)/shard_map/ppermute | solution.py:62
  262.0 32.7 %collective-permute-start.20 = (bf16[512,1408]{1,0:T(8,128)(2,1)}, bf16[512,1408]{1,0:T(8,128)(2,1)}, u32[]{:S(2)}, u32[]{:S(2)}) collective-permute-start(bf16[512,1408]{1,0:T(8,128)(2,1)} %collective-permute-done.18.refs_1_), channel_id=1, source_target_pairs={{0,1},{1,0},{2,3},{3,2},{4,5},{5,4},{6,7},{7,6},{8,24},{9,25},{10,... | collective-permute-start | bytes 4325384 | tf_op jit(solution)/shard_map/ppermute | solution.py:99
  329.5 72.7 %collective-permute-start.59 = (bf16[704,512]{1,0:T(8,128)(2,1)}, bf16[704,512]{1,0:T(8,128)(2,1)}, u32[]{:S(2)}, u32[]{:S(2)}) collective-permute-start(bf16[704,512]{1,0:T(8,128)(2,1)} %broadcast_select_fusion.2), channel_id=1, source_target_pairs={{0,1},{1,0},{2,3},{3,2},{4,5},{5,4},{6,7},{7,6},{8,24},{9,25},{10,... | collective-permute-start | bytes 2162696 | tf_op jit(solution)/shard_map/ppermute | solution.py:99
  340.8 65.2 %collective-permute-start.52 = (bf16[512,1408]{1,0:T(8,128)(2,1)}, bf16[512,1408]{1,0:T(8,128)(2,1)}, u32[]{:S(2)}, u32[]{:S(2)}) collective-permute-start(bf16[512,1408]{1,0:T(8,128)(2,1)} %convolution_convert_fusion.2), channel_id=1, source_target_pairs={{0,1},{1,0},{2,3},{3,2},{4,5},{5,4},{6,7},{7,6},{8,24},{9,25},{10,... | collective-permute-start | bytes 4325384 | tf_op jit(solution)/shard_map/ppermute | solution.py:99
  354.2 49.0 %collective-permute-start.61 = (bf16[704,512]{1,0:T(8,128)(2,1)}, bf16[704,512]{1,0:T(8,128)(2,1)}, u32[]{:S(2)}, u32[]{:S(2)}) collective-permute-start(bf16[704,512]{1,0:T(8,128)(2,1)} %add_convert_fusion.3), channel_id=1, source_target_pairs={{0,16},{1,17},{2,18},{3,19},{4,20},{5,21},{6,22},{7,23},{8,9},{9,8... | collective-permute-start | bytes 2162696 | tf_op jit(solution)/shard_map/ppermute | solution.py:99
  360.6 37.8 %collective-permute-start.44 = (bf16[512,256]{1,0:T(8,128)(2,1)}, bf16[512,256]{1,0:T(8,128)(2,1)}, u32[]{:S(2)}, u32[]{:S(2)}) collective-permute-start(bf16[512,256]{1,0:T(8,128)(2,1)} %convolution_convert_fusion.6), channel_id=1, source_target_pairs={{0,1},{1,0},{2,3},{3,2},{4,5},{5,4},{6,7},{7,6},{8,24},{9,25},{10,... | collective-permute-start | bytes 786440 | tf_op jit(solution)/shard_map/ppermute | solution.py:99
  395.1 52.3 %collective-permute-start.31 = (bf16[2,256,640]{1,2,0:T(8,128)(2,1)S(1)}, bf16[2,256,640]{1,2,0:T(8,128)(2,1)S(1)}, u32[]{:S(2)}, u32[]{:S(2)}) collective-permute-start(bf16[2,256,640]{1,2,0:T(8,128)(2,1)S(1)} %pad_maximum_fusion.14), channel_id=1, source_target_pairs={{0,1},{1,2},{2,3},{3,4},{4,5},{5,6},{6,7},{8,9},{9,10},{10,11},{11... | collective-permute-start | bytes 1966088 | tf_op jit(solution)/shard_map/ppermute | solution.py:659
  398.4 47.6 %collective-permute-start.30 = (bf16[2,256,640]{1,2,0:T(8,128)(2,1)S(1)}, bf16[2,256,640]{1,2,0:T(8,128)(2,1)S(1)}, u32[]{:S(2)}, u32[]{:S(2)}) collective-permute-start(bf16[2,256,640]{1,2,0:T(8,128)(2,1)S(1)} %pad_maximum_fusion.14), channel_id=1, source_target_pairs={{0,2},{1,3},{2,4},{3,5},{4,6},{5,7},{8,10},{9,11},{10,12},{11,13},... | collective-permute-start | bytes 1966088 | tf_op jit(solution)/shard_map/ppermute | solution.py:659
  435.0 142.6 %collective-permute-start.27 = (bf16[256,1024]{0,1:T(8,128)(2,1)}, bf16[256,1024]{0,1:T(8,128)(2,1)}, u32[]{:S(2)}, u32[]{:S(2)}) collective-permute-start(bf16[256,1024]{0,1:T(8,128)(2,1)} %fusion.61), channel_id=1, source_target_pairs={{0,8},{8,0},{16,24},{24,16},{1,9},{9,1},{17,25},{25,17},{2,10},{10... | collective-permute-start | bytes 1572872 | tf_op jit(solution)/shard_map/ppermute | solution.py:62
  435.0 117.0 %collective-permute-start.51 = (bf16[512,1408]{1,0:T(8,128)(2,1)}, bf16[512,1408]{1,0:T(8,128)(2,1)}, u32[]{:S(2)}, u32[]{:S(2)}) collective-permute-start(bf16[512,1408]{1,0:T(8,128)(2,1)} %convolution_convert_fusion.3), channel_id=1, source_target_pairs={{0,1},{1,0},{2,3},{3,2},{4,5},{5,4},{6,7},{7,6},{8,24},{9,25},{10,... | collective-permute-start | bytes 4325384 | tf_op jit(solution)/shard_map/ppermute | solution.py:99
  444.1 44.5 %collective-permute-start.32 = (bf16[2,256,640]{1,2,0:T(8,128)(2,1)S(1)}, bf16[2,256,640]{1,2,0:T(8,128)(2,1)S(1)}, u32[]{:S(2)}, u32[]{:S(2)}) collective-permute-start(bf16[2,256,640]{1,2,0:T(8,128)(2,1)S(1)} %pad_maximum_fusion.14), channel_id=1, source_target_pairs={{1,0},{2,1},{3,2},{4,3},{5,4},{6,5},{7,6},{9,8},{10,9},{11,10},{12... | collective-permute-start | bytes 1966088 | tf_op jit(solution)/shard_map/ppermute | solution.py:659
  446.1 43.5 %collective-permute-start.33 = (bf16[2,256,640]{1,2,0:T(8,128)(2,1)S(1)}, bf16[2,256,640]{1,2,0:T(8,128)(2,1)S(1)}, u32[]{:S(2)}, u32[]{:S(2)}) collective-permute-start(bf16[2,256,640]{1,2,0:T(8,128)(2,1)S(1)} %pad_maximum_fusion.14), channel_id=1, source_target_pairs={{2,0},{3,1},{4,2},{5,3},{6,4},{7,5},{10,8},{11,9},{12,10},{13,11},... | collective-permute-start | bytes 1966088 | tf_op jit(solution)/shard_map/ppermute | solution.py:659
  447.4 104.6 %collective-permute-start.53 = (bf16[512,1408]{1,0:T(8,128)(2,1)}, bf16[512,1408]{1,0:T(8,128)(2,1)}, u32[]{:S(2)}, u32[]{:S(2)}) collective-permute-start(bf16[512,1408]{1,0:T(8,128)(2,1)} %fusion.13), channel_id=1, source_target_pairs={{0,16},{1,17},{2,18},{3,19},{4,20},{5,21},{6,22},{7,23},{8,9},{9,8... | collective-permute-start | bytes 4325384 | tf_op jit(solution)/shard_map/ppermute | solution.py:99
  488.6 45.8 %collective-permute-start.65 = (bf16[176,512]{1,0:T(8,128)(2,1)}, bf16[176,512]{1,0:T(8,128)(2,1)}, u32[]{:S(2)}, u32[]{:S(2)}) collective-permute-start(bf16[176,512]{1,0:T(8,128)(2,1)} %add_convert_fusion.7), channel_id=1, source_target_pairs={{0,16},{8,24},{16,0},{24,8},{1,17},{9,25},{17,1},{25,9},{2,18},{10... | collective-permute-start | bytes 540680 | tf_op jit(solution)/shard_map/ppermute | solution.py:66
  489.6 43.9 %collective-permute-start.49 = (bf16[128,256]{1,0:T(8,128)(2,1)}, bf16[128,256]{1,0:T(8,128)(2,1)}, u32[]{:S(2)}, u32[]{:S(2)}) collective-permute-start(bf16[128,256]{1,0:T(8,128)(2,1)} %add_convert_fusion.8), channel_id=1, source_target_pairs={{0,16},{8,24},{16,0},{24,8},{1,17},{9,25},{17,1},{25,9},{2,18},{10... | collective-permute-start | bytes 196616 | tf_op jit(solution)/shard_map/ppermute | solution.py:66
  573.2 51.4 %collective-permute-start.54 = (bf16[128,1408]{1,0:T(8,128)(2,1)}, bf16[128,1408]{1,0:T(8,128)(2,1)S(1)}, u32[]{:S(2)}, u32[]{:S(2)}) collective-permute-start(bf16[128,1408]{1,0:T(8,128)(2,1)} %get-tuple-element.262), channel_id=1, source_target_pairs={{0,6},{1,7},{2,0},{3,1},{4,2},{5,3},{6,4},{7,5},{8,14},{9,15},{10,... | collective-permute-start | bytes 1081352 | tf_op jit(solution)/shard_map/ppermute | solution.py:90
  575.6 49.1 %collective-permute-start.56 = (bf16[128,1408]{1,0:T(8,128)(2,1)}, bf16[128,1408]{1,0:T(8,128)(2,1)S(1)}, u32[]{:S(2)}, u32[]{:S(2)}) collective-permute-start(bf16[128,1408]{1,0:T(8,128)(2,1)} %get-tuple-element.263), channel_id=1, source_target_pairs={{0,2},{1,3},{2,4},{3,5},{4,6},{5,7},{6,0},{7,1},{8,10},{9,11},{10,... | collective-permute-start | bytes 1081352 | tf_op jit(solution)/shard_map/ppermute | solution.py:90
  575.6 49.1 %collective-permute-start.55 = (bf16[128,1408]{1,0:T(8,128)(2,1)}, bf16[128,1408]{1,0:T(8,128)(2,1)S(1)}, u32[]{:S(2)}, u32[]{:S(2)}) collective-permute-start(bf16[128,1408]{1,0:T(8,128)(2,1)} %get-tuple-element.264), channel_id=1, source_target_pairs={{0,4},{1,5},{2,6},{3,7},{4,0},{5,1},{6,2},{7,3},{8,12},{9,13},{10,... | collective-permute-start | bytes 1081352 | tf_op jit(solution)/shard_map/ppermute | solution.py:90
  580.9 42.5 %collective-permute-start.39 = (bf16[128,768]{1,0:T(8,128)(2,1)}, bf16[128,768]{1,0:T(8,128)(2,1)}, u32[]{:S(2)}, u32[]{:S(2)}) collective-permute-start(bf16[128,768]{1,0:T(8,128)(2,1)} %get-tuple-element.294), channel_id=1, source_target_pairs={{0,4},{1,5},{2,6},{3,7},{4,0},{5,1},{6,2},{7,3},{8,12},{9,13},{10,... | collective-permute-start | bytes 589832 | tf_op jit(solution)/shard_map/ppermute | solution.py:90
  (201 other events, 1922.5 us)

commit v2 on v1

v2 whole, which is shorter than its diff:
```python
import functools

import jax
import jax.numpy as jnp
from jax import lax
from jax.experimental import pallas as pl
from jax.experimental.pallas import tpu as pltpu
from jax.sharding import PartitionSpec as P

HEADS = 16
HEAD_DIM = 64
FF = 2624
HALO = 512
EPSILON = 1e-05
THETA = 160000.0
SCALE = 0.125
LANES = 128
GROUP = 256
FAR = -1e6
BF = jnp.bfloat16
F32 = jnp.float32


def dot(left, right):
    return jnp.dot(left, right, preferred_element_type=F32)


def inner_rows(left, right):
    return lax.dot_general(left, right, (((0,), (0,)), ((), ())), preferred_element_type=F32)


def outer_rows(left, right):
    return lax.dot_general(left, right, (((1,), (1,)), ((), ())), preferred_element_type=F32)


def pick(flag, one, two):
    return [jnp.where(flag, a, b) for a, b in zip(one, two)]


def centre(rows):
    middle = jnp.mean(rows, axis=-1, keepdims=True)
    centered = rows - middle
    spread = jnp.mean(centered * centered, axis=-1, keepdims=True)
    scale = lax.rsqrt(spread + EPSILON)
    return centered * scale, scale


def centre_back(normal, scale, grads):
    return scale * (
        grads
        - jnp.mean(grads, axis=-1, keepdims=True)
        - normal * jnp.mean(grads * normal, axis=-1, keepdims=True)
    )


def two_parts(values):
    high = lax.reduce_precision(values, 8, 7)
    return high.astype(BF), (values - high).astype(BF)


def swap_core(array):
    return lax.ppermute(array, "rep", [(i, i ^ 1) for i in range(lax.axis_size("rep"))])


def swap_far(array):
    return lax.ppermute(array, "rep", [(i, i ^ 2) for i in range(lax.axis_size("rep"))])


def after(array, *earlier):
    return lax.optimization_barrier((array,) + earlier)[0]


class Direct:
    depth = 4

    def __init__(self):
        self.place = lax.axis_index("seq")
        self.z = self.place // 2
        self.y = self.place % 2
        self.x = lax.axis_index("rep") // 2
        self.core = lax.axis_index("rep") % 2
        self.front = self.core == 0

    def along(self, array, flip):
        route = [(s, s ^ (2 * flip)) for s in range(2 * self.depth)]
        return lax.ppermute(array, "seq", route)

    def cross(self, array, turn):
        n = 2 * self.depth
        route = []
        for r in range(4):
            for s in range(n):
                to = (r ^ 2, s) if r % 2 == turn else (r, s ^ 1)
                route.append((r * n + s, to[0] * n + to[1]))
        return lax.ppermute(array, ("rep", "seq"), route)

    def around(self, array):
        rows = array.shape[0]
        last = 2 * self.depth
        low = lax.ppermute(array, "seq", [(s, s + 2) for s in range(last - 2)])
        high = lax.ppermute(array, "seq", [(s, s - 2) for s in range(2, last)])
        sent = jnp.concatenate([array, jnp.where(self.y == 0, high, low)], axis=0)
        beside = lax.ppermute(sent, "seq", [(s, s ^ 1) for s in range(last)])
        step = 1 - 2 * self.y
        return [array, low, high, beside[:rows], beside[rows:]], [0, -2, 2, step, -step]

    def collect(self, piece, at_once):
        if at_once:
            return jnp.concatenate([piece] + [self.along(piece, k) for k in (1, 2, 3)], axis=0)
        pair = jnp.concatenate([piece, self.along(piece, 1)], axis=0)
        return jnp.concatenate([pair, self.along(pair, 2)], axis=0)

    def share(self, rows):
        pair = jnp.concatenate([rows, self.cross(rows, 0)], axis=0)
        return pair, self.cross(pair, 1)

    def to_near(self, grid):
        turned = [pick(self.y == 0, pair, pair[::-1]) for pair in grid]
        near = []
        for y in (0, 1):
            a, b, c, d = [pair[y] for pair in turned]
            a, b, c, d = pick(self.z % 2 == 0, [a, b, c, d], [b, a, d, c])
            near.append(pick(self.z // 2 == 0, [a, b, c, d], [c, d, a, b]))
        return near

    def to_mesh(self, near):
        lines = []
        for a, b, c, d in near:
            a, b, c, d = pick(self.z % 2 == 0, [a, b, c, d], [b, a, d, c])
            lines.append(pick(self.z // 2 == 0, [a, b, c, d], [c, d, a, b]))
        return [pick(self.y == 0, list(pair), list(pair)[::-1]) for pair in zip(*lines)]

    def rows_of(self, size):
        return [
            (2 * (self.z ^ k) + (self.y ^ y)) * size for y in (0, 1) for k in range(self.depth)
        ]

    def columns(self, count):
        z, y = jnp.arange(count) // 2, jnp.arange(count) % 2
        return (4 * (y ^ self.y) + (z ^ self.z)).astype(jnp.int32)

    def order(self, array, size):
        n = self.depth
        cut = lambda s: array[..., s * size : (s + 1) * size]
        near = self.to_near([[cut(2 * z), cut(2 * z + 1)] for z in range(n)])
        return jnp.concatenate(near[0] + near[1], axis=-1)

    def restore(self, array, size):
        n = self.depth
        cut = lambda j: array[..., j * size : (j + 1) * size]
        grid = self.to_mesh([[cut(n * y + k) for k in range(n)] for y in (0, 1)])
        return jnp.concatenate([part for pair in grid for part in pair], axis=-1)

    def down(self, mine, at_once):
        rows = mine.shape[0] // 4
        cut = lambda k, n: mine[k * rows : (k + n) * rows]
        if at_once:
            total = cut(0, 1).astype(F32)
            for k in (1, 2, 3):
                total = total + self.along(cut(k, 1), k).astype(F32)
            return total.astype(BF)
        pair = (cut(0, 2).astype(F32) + self.along(cut(2, 2), 2).astype(F32)).astype(BF)
        return (pair[:rows].astype(F32) + self.along(pair[rows:], 1).astype(F32)).astype(BF)

    def reduce(self, left, near, far, at_once=False):
        half = left.shape[1] // 2
        top, bottom = left[:, :half], left[:, half:]
        sent = lax.dot_general(
            jnp.stack([jnp.where(self.front, bottom, top), bottom]),
            jnp.stack([jnp.where(self.front, near, far), far]),
            (((1,), (1,)), ((0,), (0,))),
            preferred_element_type=F32,
        ).astype(BF)
        back = self.cross(sent, 1)
        once = inner_rows(jnp.where(self.front, top, bottom), jnp.where(self.front, far, near))
        once_in = self.cross((once + back[1]).astype(BF), 0)
        mine = (inner_rows(top, near) + back[0] + once_in).astype(BF)
        return self.down(mine, at_once)

    def reduce_rows(self, left, near, far):
        rows = left.shape[1] // (2 * self.depth)
        blocks = []
        for part in (near, far):
            whole = inner_rows(left, part).astype(BF)
            cut = lambda s: whole[s * rows : (s + 1) * rows]
            lines = self.to_near([[cut(2 * z), cut(2 * z + 1)] for z in range(self.depth)])
            blocks.append([jnp.concatenate(line, axis=0) for line in lines])
        half = self.depth * rows
        sent = jnp.concatenate(
            [jnp.where(self.front, blocks[0][1], blocks[1][0]), blocks[1][1]], axis=0
        )
        back = self.cross(sent, 1)
        once = jnp.where(self.front, blocks[1][0], blocks[0][1])
        once_in = self.cross((once.astype(F32) + back[half:]).astype(BF), 0)
        mine = (blocks[0][0].astype(F32) + back[:half] + once_in).astype(BF)
        return self.down(mine, False)


class Plain:
    def __init__(self, rows):
        self.rows = rows
        self.x = lax.axis_index("rep") // 2
        self.core = lax.axis_index("rep") % 2
        self.front = jnp.bool_(True)

    def around(self, array):
        length = lax.axis_size("seq")
        reach = min(HALO // self.rows, length - 1)
        blocks, offsets = [array], [0]
        for offset in list(range(-reach, 0)) + list(range(1, reach + 1)):
            route = [(i + offset, i) for i in range(length) if 0 <= i + offset < length]
            blocks.append(lax.ppermute(array, "seq", route))
            offsets.append(offset)
        return blocks, offsets

    def collect(self, piece, at_once):
        return lax.all_gather(piece, "seq", axis=0, tiled=True)

    def share(self, near):
        far = swap_far(near)
        half = near.shape[0] // 2
        return (
            jnp.concatenate([near[:half], far[:half]], axis=0),
            jnp.concatenate([near[half:], far[half:]], axis=0),
        )

    def rows_of(self, size):
        return [jnp.int32(0), jnp.int32(lax.axis_size("seq") // 2 * size)]

    def columns(self, count):
        return jnp.zeros((1,), jnp.int32)

    def order(self, array, size):
        return array

    def restore(self, array, size):
        return array

    def reduce(self, left, near, far, at_once=False):
        mine = inner_rows(left, near) + swap_far(inner_rows(left, far).astype(BF))
        return lax.psum_scatter(mine, "seq", scatter_dimension=0, tiled=True).astype(BF)

    reduce_rows = reduce


def halves(front, pair, other):
    half = pair.shape[0] // 2
    one, two = pair[half:], other[:half]
    near = jnp.concatenate([pair[:half], jnp.where(front, two, one)], axis=0)
    far = jnp.concatenate([jnp.where(front, one, two), other[half:]], axis=0)
    return near, far


def lane_masks():
    lane = lax.broadcasted_iota(jnp.int32, (1, GROUP), 1)
    turned = [(lane % LANES) // (HEAD_DIM // 2) == i for i in range(4)]
    plain = [lane // HEAD_DIM == i for i in range(4)]
    return turned, plain


def only(mask, array):
    return jnp.where(mask, array, jnp.zeros_like(array))


def spin(raw, c, s, way):
    a, b = raw[:, :LANES], raw[:, LANES:]
    return a * c - way * (b * s), b * c + way * (a * s)


def prepare_kernel(places, *refs):
    *blocks, out = refs
    width = blocks[0].shape[1] - LANES
    rows = out.shape[0] // len(blocks)
    count = places.shape[0]
    size = width // count
    for i, block in enumerate(blocks):
        normal = centre(block[:, :width].astype(F32))[0].astype(BF)
        at = slice(i * rows, (i + 1) * rows)
        out[at, width:] = block[:, width:]
        for s in range(count):
            to = pl.multiple_of(places[s] * size, LANES)
            out[at, pl.ds(to, size)] = normal[:, s * size : (s + 1) * size]


def mix_kernel(rows, near, far, tables, *refs):
    near_out, far_out, cosine, sine = refs[-4:]
    half = near.shape[0]
    marks = rows[:, half : half + LANES].astype(F32)
    lane = lax.broadcasted_iota(jnp.int32, (1, LANES), 1).astype(F32)
    exact = lambda flags, table: jnp.dot(
        flags.astype(F32), table, preferred_element_type=F32, precision=lax.Precision.HIGHEST
    )
    coarse = exact(marks[:, 0:1] == lane, tables[:LANES])
    fine = exact(marks[:, 1:2] == lane, tables[LANES:])
    c = coarse[:, :LANES] * fine[:, :LANES] - coarse[:, LANES:] * fine[:, LANES:]
    s = coarse[:, LANES:] * fine[:, :LANES] + coarse[:, :LANES] * fine[:, LANES:]
    for weight, out in ((near, near_out), (far, far_out)):
        raw = dot(rows[:, :half], weight[...])
        for kind, scale in ((0, SCALE), (1, 1.0)):
            at = kind * GROUP
            a, b = spin(raw[:, at : at + GROUP], c, s, 1.0)
            out[:, at : at + LANES] = (a * scale).astype(BF)
            out[:, at + LANES : at + GROUP] = (b * scale).astype(BF)
        out[:, 2 * GROUP :] = raw[:, 2 * GROUP :].astype(BF)

    @pl.when(pl.program_id(0) == 0)
    def _():
        cosine[...] = c
        sine[...] = s


def attend_kernel(q0, k0, v0, q1, k1, v1, doc_row, doc_column, attended, attended_low, logs):
    turned, plain = lane_masks()
    allowed = doc_column[...] == doc_row[0]
    lane = lax.broadcasted_iota(jnp.int32, (1, LANES), 1)
    totals = jnp.zeros((q0.shape[0], LANES), F32)
    for group, (q, k, v) in enumerate(((q0, k0, v0), (q1, k1, v1))):
        queries, keys, values = q[...], k[...], v[...]
        kept = jnp.zeros(queries.shape, F32)
        for i in range(4):
            raw = outer_rows(only(turned[i], queries), keys)
            raw = jnp.where(allowed, raw, -jnp.inf)
            top = jnp.max(raw, axis=-1, keepdims=True)
            weights = jnp.exp(raw - top)
            total = jnp.sum(weights, axis=-1, keepdims=True)
            found = dot(weights.astype(BF), values) / total
            kept = jnp.where(plain[i], found, kept)
            totals = jnp.where(lane == 4 * group + i, top + jnp.log(total), totals)
        attended[:, group * GROUP : (group + 1) * GROUP] = kept
        attended_low[:, group * GROUP : (group + 1) * GROUP] = kept.astype(BF)
    logs[...] = totals


def around_kernel(grads, attended, logs, around, numbers):
    heads = HEADS // 2
    width = grads.shape[1]
    row = lax.broadcasted_iota(jnp.int32, (width, LANES), 0)
    lane = lax.broadcasted_iota(jnp.int32, (width, LANES), 1)
    low = grads[...].astype(BF)
    delta = jnp.dot(
        low.astype(F32) * attended[...],
        (row // HEAD_DIM == lane - 2 * heads).astype(F32),
        preferred_element_type=F32,
        precision=lax.Precision.HIGHEST,
    )
    both = logs[...] + delta
    numbers[...] = both
    high = both.astype(BF).astype(F32)
    around[:, :width] = low
    around[:, width:] = (high + pltpu.roll(both - high, heads, 1)).astype(BF)


def query_kernel(q0, k0, v0, q1, k1, v1, around, numbers, doc_row, doc_column, cosine, sine, d_q):
    turned, plain = lane_masks()
    allowed = doc_column[...] == doc_row[0]
    c, s = cosine[...] * SCALE, sine[...] * SCALE
    for group, (q, k, v) in enumerate(((q0, k0, v0), (q1, k1, v1))):
        queries, keys, values = q[...], k[...], v[...]
        grads = around[:, group * GROUP : (group + 1) * GROUP]
        kept = jnp.zeros(queries.shape, F32)
        for i in range(4):
            at = 4 * group + i
            raw = outer_rows(only(turned[i], queries), keys)
            weights = jnp.where(allowed, jnp.exp(raw - numbers[:, at : at + 1]), 0.0)
            d_weights = outer_rows(only(plain[i], grads), values)
            d_raw = (weights * (d_weights - numbers[:, 16 + at : 17 + at])).astype(BF)
            kept = jnp.where(turned[i], dot(d_raw, keys), kept)
        a, b = spin(kept, c, s, -1.0)
        d_q[:, group * GROUP : group * GROUP + LANES] = a.astype(BF)
        d_q[:, group * GROUP + LANES : (group + 1) * GROUP] = b.astype(BF)


def key_kernel(q0, k0, v0, q1, k1, v1, d_q, doc_row, doc_column, cosine, sine, *refs):
    *around, near, far = refs
    turned, plain = lane_masks()
    rows = k0.shape[0]
    c, s = cosine[...], sine[...]
    column = doc_column[...]
    kept = [[jnp.zeros(k0.shape, F32), jnp.zeros(k0.shape, F32)] for _ in (0, 1)]
    for j, block in enumerate(around):
        part = slice(j * rows, (j + 1) * rows)
        allowed = column == doc_row[0, :, part]
        numbers = block[:, 2 * GROUP :].astype(F32)
        numbers = (numbers + pltpu.roll(numbers, LANES - HEADS // 2, 1)).T
        for group, (q, k, v) in enumerate(((q0, k0, v0), (q1, k1, v1))):
            queries, keys, values = q[part, :], k[...], v[...]
            grads = block[:, group * GROUP : (group + 1) * GROUP]
            add_k = jnp.zeros(k0.shape, F32)
            add_v = jnp.zeros(k0.shape, F32)
            for i in range(4):
                at = 4 * group + i
                raw = outer_rows(only(turned[i], keys), queries)
                weights = jnp.where(allowed, jnp.exp(raw - numbers[at : at + 1, :]), 0.0)
                add_v = jnp.where(plain[i], dot(weights.astype(BF), grads), add_v)
                d_weights = outer_rows(only(plain[i], values), grads)
                d_raw = (weights * (d_weights - numbers[16 + at : 17 + at, :])).astype(BF)
                add_k = jnp.where(turned[i], dot(d_raw, queries), add_k)
            kept[group][0] += add_k
            kept[group][1] += add_v
    for group, out in enumerate((near, far)):
        a, b = spin(kept[group][0], c, s, -1.0)
        out[:, :GROUP] = d_q[:, group * GROUP : (group + 1) * GROUP]
        out[:, GROUP : GROUP + LANES] = a.astype(BF)
        out[:, GROUP + LANES : 2 * GROUP] = b.astype(BF)
        out[:, 2 * GROUP :] = kept[group][1].astype(BF)


def call_kernel(kernel, ins, outs, flops, grid=1, aliases=None):
    spec = lambda block, at: (
        pl.BlockSpec(memory_space=pltpu.SMEM if block is None else pl.ANY)
        if at is None
        else pl.BlockSpec(block, at)
    )
    return pl.pallas_call(
        kernel,
        grid=(grid,),
        in_specs=[spec(block, at) for _, block, at in ins],
        out_specs=tuple(pl.BlockSpec(block, at) for _, _, block, at in outs),
        out_shape=tuple(jax.ShapeDtypeStruct(shape, kind) for shape, kind, _, _ in outs),
        input_output_aliases=aliases or {},
        compiler_params=pltpu.CompilerParams(vmem_limit_bytes=40 * 2**20),
        cost_estimate=pl.CostEstimate(
            flops=flops, bytes_accessed=8 * 2**20, transcendentals=3 * 2**20
        ),
    )(*[a for a, _, _ in ins])


def gelu_parts(inner):
    share = 0.5 * (1.0 + lax.erf(inner * 0.7071067811865476))
    return inner * share, share + inner * (0.3989422804014327 * jnp.exp(-0.5 * inner * inner))


def hidden_kernel(marks, rows, grads, pair, other, shrink_pair, shrink_other, *refs):
    active, lifted_grads, out, out_there, d_rows, d_there = refs[:6]
    expand_w, shrink_w, semaphore = refs[6:]
    units = shrink_w.shape[0]
    half = pair.shape[0] // 2
    wide = shrink_pair.shape[1]
    places = marks.shape[0] - 2
    block = units // places
    front = marks[0] == 1
    x = marks[1]
    step = pl.program_id(0)

    def weights(source, start, at, row):
        return source.at[pl.ds(start, half)], expand_w.at[at, pl.ds(row, half)]

    def shrinks(source, high, at, low):
        found = []
        for j in range(places // 2):
            start = high * (units // 2) + j * block
            row = pl.multiple_of(marks[2 + low * (places // 2) + j], 16)
            column = pl.multiple_of(at * wide, LANES)
            found.append(
                (
                    source.at[pl.ds(start, block)],
                    shrink_w.at[pl.ds(row, block), pl.ds(column, wide)],
                )
            )
        return found

    def begin(moves, first):
        copies = [
            pltpu.make_async_copy(a, b, semaphore.at[first + k]) for k, (a, b) in enumerate(moves)
        ]
        for copy in copies:
            copy.start()
        return copies

    @pl.when(step == 0)
    def _():
        moves = [weights(pair, 0, x, 0), weights(other, half, 1 - x, half)]
        moves += shrinks(shrink_pair, 0, x, 0) + shrinks(shrink_other, 1, 1 - x, 1)
        copies = begin(moves, 0)
        for flag, low, high in ((front, other, pair), (jnp.logical_not(front), pair, other)):

            @pl.when(flag)
            def _():
                start = 0 if low is other else half
                back = half - start
                shrink_low = shrink_other if low is other else shrink_pair
                shrink_high = shrink_pair if low is other else shrink_other
                crossed = [weights(low, start, x, half), weights(high, back, 1 - x, 0)]
                crossed += shrinks(shrink_low, start // half, x, 1)
                crossed += shrinks(shrink_high, back // half, 1 - x, 0)
                for copy in begin(crossed, len(moves)):
                    copy.wait()

        for copy in copies:
            copy.wait()

    values, dy = rows[...], grads[...]
    tile = 256
    for at in range(0, units, tile):
        cut = slice(at, min(at + tile, units))
        inner = dot(values, expand_w[0, :, cut])
        gate = dot(values, expand_w[1, :, cut])
        d_active = outer_rows(dy, shrink_w[cut, :])
        value, slope = gelu_parts(inner)
        active[:, cut] = (value * gate).astype(BF)
        lifted_grads[x, :, cut] = (d_active * gate * slope).astype(BF)
        lifted_grads[1 - x, :, cut] = (d_active * value).astype(BF)
    result = dot(active[...], shrink_w[...])
    back = outer_rows(lifted_grads[x], expand_w[0]) + outer_rows(lifted_grads[1 - x], expand_w[1])

    @pl.when(step == 0)
    def _():
        out[...] = result
        d_rows[...] = back

    @pl.when(step == 1)
    def _():
        out_there[...] = result.astype(BF)
        d_there[...] = back.astype(BF)


def hidden(marks, rows, grads, expand, shrink):
    count, width = rows.shape
    units = expand[0].shape[1]
    size = count // 2
    moving = lambda i: (i, 0)
    still = lambda i: (0, 0)
    held = pl.BlockSpec(memory_space=pl.ANY)
    outs = [
        ((count, units), BF, (size, units), moving),
        ((2, count, units), BF, (2, size, units), lambda i: (0, i, 0)),
        ((size, width), F32, (size, width), still),
        ((size, width), BF, (size, width), still),
        ((size, width), F32, (size, width), still),
        ((size, width), BF, (size, width), still),
    ]
    return pl.pallas_call(
        hidden_kernel,
        grid=(2,),
        in_specs=[pl.BlockSpec(memory_space=pltpu.SMEM)]
        + [pl.BlockSpec((size, width), moving)] * 2
        + [held] * 4,
        out_specs=tuple(pl.BlockSpec(block, at) for _, _, block, at in outs),
        out_shape=tuple(jax.ShapeDtypeStruct(shape, kind) for shape, kind, _, _ in outs),
        scratch_shapes=[
            pltpu.VMEM((2, width, units), BF),
            pltpu.VMEM((units, width), BF),
            pltpu.SemaphoreType.DMA((2 * marks.shape[0],)),
        ],
        compiler_params=pltpu.CompilerParams(vmem_limit_bytes=48 * 2**20),
        cost_estimate=pl.CostEstimate(
            flops=12 * count * width * units,
            bytes_accessed=20 * 2**20,
            transcendentals=2 * count * units,
        ),
    )(marks, rows, grads, *expand, *shrink)


def on_device(
    direct,
    tokens,
    norm_first,
    joint_weight,
    output_weight,
    norm_second,
    expand_weight,
    shrink_weight,
    document_start,
    cotangent,
):
    rows, width = tokens.shape
    plan = Direct() if direct else Plain(rows)
    length = lax.axis_size("seq")
    here = lax.axis_index("seq")
    x, core = plan.x, plan.core
    near_x = x == 0
    depth = joint_weight.shape[0]
    unit_rows = shrink_weight.shape[0]
    unit_half = (unit_rows + 1) // 2
    units = -(-unit_half * length // LANES) * LANES
    while units % length:
        units += LANES
    unit_pad = units // length
    half_width = width // 2

    def mine(array, start):
        parts = [array[:, start + i * GROUP : start + (i + 1) * GROUP] for i in range(4)]
        low, high = pick(near_x, parts[0::2], parts[1::2])
        return jnp.where(core == 0, low, high)

    source = jnp.arange(GROUP)
    turn = (
        source[:, None]
        == ((source % LANES) // 32 * HEAD_DIM + source // LANES * 32 + source % 32)[None, :]
    ).astype(BF)
    gain_one = norm_first.astype(F32)[:, None]
    gain_two = norm_second.astype(F32)[:, None]
    joint_piece = jnp.concatenate(
        [
            (dot(mine(joint_weight, 0), turn) * gain_one).astype(BF),
            (dot(mine(joint_weight, width), turn) * gain_one).astype(BF),
            (mine(joint_weight, 2 * width).astype(F32) * gain_one).astype(BF),
            mine(output_weight, 0),
        ],
        axis=1,
    )
    slot = jnp.arange(units)
    inner = core * unit_half + slot % unit_pad
    fits = (slot % unit_pad < unit_half) & (inner < unit_rows)
    unit_of = jnp.where(fits, slot // unit_pad * unit_rows + inner, -2 * FF)
    spread_units = (jnp.arange(2 * FF)[:, None] == (unit_of + x * FF)[None, :]).astype(BF)
    expand_piece = (dot(expand_weight, spread_units) * gain_two).astype(BF)
    slot_row = jnp.arange(unit_pad)

    def picked(c):
        row = c * unit_half + slot_row
        row = jnp.where((slot_row < unit_half) & (row < unit_rows), row, -1)
        return (row[:, None] == jnp.arange(unit_rows)[None, :]).astype(BF)

    shrink_piece = dot(
        picked(core),
        jnp.where(near_x, shrink_weight[:, :half_width], shrink_weight[:, half_width:]),
    ).astype(BF)

    joint_rows = plan.collect(joint_piece, True)
    anchor = (lax.axis_index("rep") * length + here) * rows
    position = anchor + jnp.arange(rows, dtype=jnp.int32) - document_start
    marks = jnp.pad(
        jnp.stack([(position + 1) // 16, (position + 1) % 16], axis=1), ((0, 0), (0, LANES - 2))
    ).astype(BF)
    blocks, offsets = plan.around(jnp.concatenate([tokens, marks], axis=1))
    block_count = len(blocks)
    span = block_count * rows
    still = lambda i: (0, 0)
    moving = lambda i: (i, 0)
    (sent,) = call_kernel(
        prepare_kernel,
        [(plan.columns(width // depth), None, None)]
        + [(block, (rows, width + LANES), still) for block in blocks],
        [((span, width + LANES), BF, (span, width + LANES), still)],
        20 * span * width,
    )
    first = (sent, swap_core(sent))
    offset_rows = jnp.stack([jnp.int32(offset) for offset in offsets]) * rows
    index = (here * rows + offset_rows[:, None] + jnp.arange(rows)[None, :]).reshape(1, span)
    document_rows = []
    for rows_in in first:
        code = rows_in[:, width : width + 2].astype(F32).T
        code = code[:1] * 16.0 + code[1:]
        document_rows.append(jnp.where(code > 0, index.astype(F32) - (code - 1.0), FAR))
    document_row = jnp.stack(document_rows)
    document_column = jnp.concatenate([row[:, :rows] for row in document_rows], axis=1).T
    halves_of_head = HEAD_DIM // 2
    frequency = THETA ** (-(jnp.arange(halves_of_head, dtype=F32) * 2.0) / HEAD_DIM)
    frequency = jnp.tile(frequency, LANES // halves_of_head)[None, :]
    steps = jnp.arange(LANES, dtype=F32)[:, None]
    angle = jnp.concatenate([16.0 * steps * frequency, (steps - 1.0) * frequency], axis=0)
    tables = jnp.concatenate([jnp.cos(angle), jnp.sin(angle)], axis=1)
    cotangents = jnp.concatenate([cotangent, swap_core(cotangent)], axis=0)

    expand_rows = plan.collect(after(expand_piece, joint_rows), False)
    shrink_rows = plan.collect(after(shrink_piece, expand_rows), False)
    joint_near, joint_far = halves(plan.front, *plan.share(joint_rows))
    expand_both = plan.share(expand_rows)
    shrink_both = plan.share(shrink_rows)
    output_mine = jnp.concatenate([joint_near[:, 3 * GROUP :], joint_far[:, 3 * GROUP :]], axis=1)
    output_all = jnp.concatenate([output_mine, swap_core(output_mine)], axis=1)

    def turn_columns(array):
        parts = [array[:, i * GROUP : (i + 1) * GROUP] for i in range(4)]
        parts = pick(core == 0, parts, parts[2:] + parts[:2])
        left, right = pick(near_x, parts[:2], parts[1::-1]), pick(near_x, parts[2:], parts[:1:-1])
        return jnp.concatenate(left + right, axis=-1)

    wide = 3 * GROUP
    mixed = ()
    turns = []
    for t in (0, 1):
        there = functools.partial(lambda shift, i: (i + shift, 0), t * block_count)
        *mixed, cosine, sine = call_kernel(
            mix_kernel,
            [
                (first[t], (rows, width + LANES), moving),
                (joint_near, (width, wide), still),
                (joint_far, (width, wide), still),
                (tables, (2 * LANES, 2 * LANES), still),
            ]
            + [(array, (8, LANES), None) for array in mixed],
            [((2 * span, wide), BF, (rows, wide), there)] * 2
            + [((rows, LANES), F32, (rows, LANES), still)] * 2,
            2 * span * width * 2 * wide,
            block_count,
            {4 + i: i for i in range(len(mixed))},
        )
        turns.append((cosine, sine))
    cosine, sine = [jnp.concatenate(pair, axis=0) for pair in zip(*turns)]
    score_flops = 2 * 2 * rows * span * GROUP * 8
    column = lambda kind, every: (
        ((span, GROUP), lambda i: (i, kind))
        if every
        else ((rows, GROUP), lambda i: (i * block_count, kind))
    )
    wide_keys = [
        (array, *column(kind, kind > 0)) for array in mixed for kind in range(3)
    ]
    wide_queries = [
        (array, *column(kind, kind == 0)) for array in mixed for kind in range(3)
    ]
    documents = [
        (document_row, (1, 1, span), lambda i: (i, 0, 0)),
        (document_column, (rows, 1), moving),
    ]
    both = lambda w, kind: ((2 * rows, w), kind, (rows, w), moving)
    attended, attended_low, logs = call_kernel(
        attend_kernel,
        wide_keys + documents,
        [both(2 * GROUP, F32), both(2 * GROUP, BF), both(LANES, F32)],
        2 * score_flops,
        2,
    )
    attended_there = swap_core(attended_low)
    attended_there = jnp.concatenate([attended_there[rows:], attended_there[:rows]], axis=0)
    attended_rows = plan.order(
        turn_columns(jnp.concatenate([attended_low, attended_there], axis=1)), depth
    )
    middle = tokens.astype(F32) + turn_columns(dot(attended_rows[:rows], output_all))
    second, second_scale = centre(middle)
    second_low = plan.order(second.astype(BF), depth)
    second_both = jnp.concatenate([second_low, swap_core(second_low)], axis=0)

    where = jnp.stack(
        [plan.front.astype(jnp.int32), x.astype(jnp.int32)]
        + [row.astype(jnp.int32) for row in plan.rows_of(unit_pad)]
    )
    active_low, lifted_grads, out, out_there, second_grad, second_there = hidden(
        where, second_both, cotangents, expand_both, shrink_both
    )
    result = middle + out + swap_core(out_there).astype(F32)
    second_grad = second_grad + swap_core(second_there).astype(F32)
    middle_grad = cotangent.astype(F32) + centre_back(
        second, second_scale, plan.restore(second_grad, depth)
    )
    branch = middle_grad.astype(BF)
    branch_both = turn_columns(jnp.concatenate([branch, swap_core(branch)], axis=0))
    attended_grad = turn_columns(plan.restore(outer_rows(branch_both, output_all), depth))
    around, numbers = call_kernel(
        around_kernel,
        [
            (attended_grad[:, : 2 * GROUP], (rows, 2 * GROUP), moving),
            (attended, (rows, 2 * GROUP), moving),
            (logs, (rows, LANES), moving),
        ],
        [both(2 * GROUP + LANES, BF), both(LANES, F32)],
        2**28,
        2,
    )
    arounds, _ = plan.around(around)
    turning = [(cosine, (rows, LANES), moving), (sine, (rows, LANES), moving)]
    (query_grad,) = call_kernel(
        query_kernel,
        wide_keys
        + [
            (around, (rows, 2 * GROUP), moving),
            (numbers, (rows, LANES), moving),
        ]
        + documents
        + turning,
        [both(2 * GROUP, BF)],
        3 * score_flops,
        2,
    )
    mixed_grads = call_kernel(
        key_kernel,
        wide_queries
        + [(query_grad, (rows, 2 * GROUP), moving)]
        + documents
        + turning
        + [(block, (rows, 2 * GROUP + LANES), moving) for block in arounds],
        [both(wide, BF), both(wide, BF)],
        4 * score_flops,
        2,
    )
    first_part = outer_rows(mixed_grads[0], joint_near[:, :wide]) + outer_rows(
        mixed_grads[1], joint_far[:, :wide]
    )
    first_grad = first_part[:rows] + swap_core(first_part[rows:].astype(BF)).astype(F32)
    normal, normal_scale = centre(tokens.astype(F32))
    tokens_grad = middle_grad + centre_back(
        normal, normal_scale, plan.restore(first_grad, depth)
    )

    left, right = cotangents[:, :half_width], cotangents[:, half_width:]
    shrink_share = plan.reduce_rows(active_low, *pick(near_x, [left, right], [right, left]))
    expand_share = plan.reduce(second_both, lifted_grads[0], lifted_grads[1])
    output_share = plan.reduce(
        attended_rows, branch_both[:, :GROUP], branch_both[:, GROUP : 2 * GROUP]
    )
    joint_share = plan.reduce(
        jnp.concatenate([rows_in[:rows, :width] for rows_in in first], axis=0),
        mixed_grads[0],
        mixed_grads[1],
        True,
    )

    def spread(share):
        pair = [share, swap_far(share)]
        low, high = pick(near_x, pair, pair[::-1])
        both = jnp.concatenate([low, high], axis=1)
        there = swap_core(both)
        size = share.shape[1]
        cores = pick(core == 0, [both, there], [there, both])
        return [[part[:, :size], part[:, size:]] for part in cores]

    shrink_shares = spread(shrink_share)
    shrink_grad = jnp.concatenate(
        [
            inner_rows(picked(0), shrink_shares[0][i]) + inner_rows(picked(1), shrink_shares[1][i])
            for i in (0, 1)
        ],
        axis=1,
    )
    expand_shares = spread(expand_share)
    expand_raw = 0.0
    for c in (0, 1):
        inner = c * unit_half + slot % unit_pad
        fits = (slot % unit_pad < unit_half) & (inner < unit_rows)
        unit_at = jnp.where(fits, slot // unit_pad * unit_rows + inner, -1)
        back = (unit_at[:, None] == jnp.arange(FF)[None, :]).astype(BF)
        expand_raw = expand_raw + dot(jnp.concatenate(expand_shares[c], axis=0), back)
    expand_raw = jnp.concatenate([expand_raw[:depth], expand_raw[depth:]], axis=1)
    expand_grad = expand_raw * gain_two
    second_gain_grad = jnp.sum(expand_raw * expand_weight.astype(F32), axis=1)
    output_shares = spread(output_share)
    output_grad = jnp.concatenate(output_shares[0] + output_shares[1], axis=1).astype(F32)
    joint_four = spread(joint_share)
    columns = []
    for kind in range(3):
        for c in (0, 1):
            for i in (0, 1):
                piece = joint_four[c][i][:, kind * GROUP : (kind + 1) * GROUP]
                columns.append(
                    lax.dot_general(
                        piece, turn, (((1,), (1,)), ((), ())), preferred_element_type=F32
                    )
                    if kind < 2
                    else piece.astype(F32)
                )
    joint_raw = jnp.concatenate(columns, axis=1)
    joint_grad = joint_raw * gain_one
    first_gain_grad = jnp.sum(joint_raw * joint_weight.astype(F32), axis=1)
    return (
        result.astype(BF),
        tokens_grad.astype(BF),
        first_gain_grad,
        joint_grad,
        output_grad,
        second_gain_grad,
        expand_grad,
        shrink_grad,
    )


def solution(mesh):
    placed = (
        P(("rep", "seq"), None),
        P("seq"),
        P("seq", None),
        P("seq", None),
        P("seq"),
        P("seq", None),
        P("seq", None),
        P(("rep", "seq")),
        P(("rep", "seq"), None),
    )
    return jax.shard_map(
        functools.partial(on_device, mesh.shape["seq"] == 8),
        mesh=mesh,
        in_specs=placed,
        out_specs=(
            P(("rep", "seq"), None),
            P(("rep", "seq"), None),
            P("seq"),
            P("seq", None),
            P("seq", None),
            P("seq"),
            P("seq", None),
            P("seq", None),
        ),
        check_vma=False,
    )
```

time: 674 us -> 458 us (0.68)
  other arithmetic: 117 us -> 40.4 us
  local copies, waits for them, and re-layouts: 109 us -> 42.3 us
  waiting for transfers between devices: 209 us -> 169 us
  starting transfers between devices: 104 us -> 78.4 us
  matrix products: 64.9 us -> 45.7 us
  Pallas kernels: 60.1 us -> 71.7 us
    ppermute x8 -> x6, waiting for transfers between devices: 74.5 us -> 15.9 us  [the longest x2 15.9 us: around(): beside = lax.ppermute(sent, 'seq', [(s, s ^ 1) for s in range(last)])]
    unnamed x77 -> x23, other arithmetic: 49.4 us -> 5.85 us
    ppermute x21 -> x16, waiting for transfers between devices: 71.4 us -> 97.1 us  [along(): return lax.ppermute(array, 'seq', route)]
    unnamed x368 -> x188, local copies, waits for them, and re-layouts: 58.1 us -> 34.6 us
    concatenate x11 -> x7, local copies, waits for them, and re-layouts: 21.2 us -> 3.21 us  [the longest x3 2.19 us: share(): pair = jnp.concatenate([rows, self.cross(rows, 0)], axis=0)]
    ppermute x21 -> x14, starting transfers between devices: 36.1 us -> 19.6 us  [cross(): return lax.ppermute(array, ('rep', 'seq'), route)]
    dot_general x18 -> x12, matrix products: 29.8 us -> 13.4 us  [inner_rows(): lax.dot_general(left, right, (((0,), (0,)), ((), ())), preferred_element_...]
    pallas_call x8 -> x7, Pallas kernels: 42.9 us -> 55.2 us  [call_kernel(): pl.pallas_call(kernel, grid=(grid,), in_specs=[spec(block, at) for _, blo...]
  transfers between devices with their start and end apart: 67 -> 53, of which waited for: 21 -> 17; matrix products, arithmetic and copies ran while one was open for 32% -> 20% of each run, Pallas kernels for 6% -> 12%
where the time goes in v2:
time: 458 us; the launch traced here: 451 us
  waiting for transfers between devices  169 us (37%)
  starting transfers between devices  78.4 us (17%)
  Pallas kernels  71.7 us (16%)
  matrix products  45.7 us (10%)
  local copies, waits for them, and re-layouts  42.3 us (9%)
  other arithmetic  40.4 us (9%)
    ppermute x16, waiting for transfers between devices, along(): return lax.ppermute(array, 'seq', route)  97.1 us
    pallas_call x7, Pallas kernels, call_kernel(): pl.pallas_call(kernel, grid=(grid,), in_specs=[spec(block, at) for _, blo...  55.2 us
    ppermute x14, waiting for transfers between devices, cross(): return lax.ppermute(array, ('rep', 'seq'), route)  44.5 us
    ppermute x16, starting transfers between devices, along(): return lax.ppermute(array, 'seq', route)  34.9 us
    unnamed x188, local copies, waits for them, and re-layouts  34.6 us
    dot_general x7, matrix products, dot(): return jnp.dot(left, right, preferred_element_type=F32)  21.5 us
    ppermute x14, starting transfers between devices, cross(): return lax.ppermute(array, ('rep', 'seq'), route)  19.6 us
    pallas_call x1, Pallas kernels, hidden(): pl.pallas_call(hidden_kernel, grid=(2,), in_specs=[pl.BlockSpec(memory_sp...  16.5 us
  transfers between devices with their start and end apart: 53, of which 17 were waited for; matrix products, arithmetic and copies ran while one was open for 20% of the time, Pallas kernels for 12%

profile of v2, /device:TPU:0, one launch (start us, length us, event | category | flops | bytes accessed | tf_op | source)
XLA Modules:
  0.0 450.9 jit_solution(11102163771419656523)
XLA Ops:
  4.1 5.6 %collective-permute-start = (bf16[256,1152]{1,0:T(8,128)(2,1)S(1)}, bf16[256,1152]{1,0:T(8,128)(2,1)S(1)}, u32[]{:S(2)}, u32[]{:S(2)}) collective-permute-start(bf16[256,1152]{1,0:T(8,128)(2,1)S(1)} %pad_maximum_fusion.17.refs_0_), channel_id=1, source_target_pairs={{0,2},{1,3},{2,4},{3,5},{4,6},{5,7},{8,10},{9,11},{10,12},{11,13},... | collective-permute-start | bytes 1769480 | tf_op jit(solution)/shard_map/ppermute | solution.py:100
  23.5 7.8 %fusion.15 = bf16[128,1408]{1,0:T(8,128)(2,1)} fusion(bf16[128,5248]{1,0:T(8,128)(2,1)} %param.14, s32[1408]{0:T(1024)S(1)} %select_add_fusion, f32[128]{0:T(128)S(1)} %convert_element_type.282), kind=kOutput, calls=%fused_computation.30 | convolution fusion | flops 1899380736 | bytes 1710080 | tf_op jit(solution)/shard_map/dot_general | solution.py:25
  42.8 6.4 %collective-permute-start.13 = (bf16[128,1408]{1,0:T(8,128)(2,1)}, bf16[128,1408]{1,0:T(8,128)(2,1)S(1)}, u32[]{:S(2)}, u32[]{:S(2)}) collective-permute-start(bf16[128,1408]{1,0:T(8,128)(2,1)} %fusion.15), channel_id=1, source_target_pairs={{0,2},{1,3},{2,0},{3,1},{4,6},{5,7},{6,4},{7,5},{8,10},{9,11},{10,... | collective-permute-start | bytes 1081352 | tf_op jit(solution)/shard_map/ppermute | solution.py:86
  57.4 3.6 collective-permute-start.14
  63.2 15.9 %collective-permute-done.2 = bf16[512,1152]{1,0:T(8,128)(2,1)S(1)} collective-permute-done((bf16[512,1152]{1,0:T(8,128)(2,1)S(1)}, bf16[512,1152]{1,0:T(8,128)(2,1)S(1)}, u32[]{:S(2)}, u32[]{:S(2)}) %collective-permute-start.2) | collective-permute-done | bytes 1179680 | tf_op jit(solution)/shard_map/ppermute | solution.py:103
  82.3 8.0 %collective-permute-done.14 = bf16[256,1408]{1,0:T(8,128)(2,1)S(1)} collective-permute-done((bf16[256,1408]{1,0:T(8,128)(2,1)S(1)}, bf16[256,1408]{1,0:T(8,128)(2,1)S(1)}, u32[]{:S(2)}, u32[]{:S(2)}) %collective-permute-start.14) | collective-permute-done | bytes 720928 | tf_op jit(solution)/shard_map/ppermute | solution.py:86
  91.2 4.2 collective-permute-start.17
  100.2 3.6 collective-permute-start.18
  104.7 14.7 %collective-permute-done.18 = bf16[352,512]{1,0:T(8,128)(2,1)S(1)} collective-permute-done((bf16[352,512]{1,0:T(8,128)(2,1)S(1)}, bf16[352,512]{1,0:T(8,128)(2,1)S(1)}, u32[]{:S(2)}, u32[]{:S(2)}) %collective-permute-start.18) | collective-permute-done | bytes 360480 | tf_op jit(solution)/shard_map/ppermute | solution.py:86
  124.2 6.9 %collective-permute-done.19 = bf16[704,512]{1,0:T(8,128)(2,1)S(1)} collective-permute-done((bf16[704,512]{1,0:T(8,128)(2,1)S(1)}, bf16[704,512]{1,0:T(8,128)(2,1)S(1)}, u32[]{:S(2)}, u32[]{:S(2)}) %collective-permute-start.19) | collective-permute-done | bytes 720928 | tf_op jit(solution)/shard_map/ppermute | solution.py:95
  137.3 8.3 %shard_map.153 = (bf16[2560,768]{1,0:T(8,128)(2,1)S(1)}, bf16[2560,768]{1,0:T(8,128)(2,1)}, f32[256,128]{1,0:T(8,128)S(1)}, f32[256,128]{1,0:T(8,128)S(1)}) custom-call(bf16[1280,1152]{1,0:T(8,128)(2,1)S(1)} %shard_map.152.rows, bf16[1024,1024]{1,0:T(8,128)(2,1)S(1)} %get-tuple-element.216.near, bf16[1024,1024]{1,0:T(8,128)(2,1)S(1)} %pad_maximum_fusion.1.far, ...), custom_call_target="tpu_custom_call" | custom-call | flops 4026531840 | bytes 8388608 | tf_op jit(solution)/shard_map/pallas_call | solution.py:414
  155.4 8.3 %shard_map.154 = (bf16[2560,768]{1,0:T(8,128)(2,1)S(1)}, bf16[2560,768]{1,0:T(8,128)(2,1)}, f32[256,128]{1,0:T(8,128)S(1)}, f32[256,128]{1,0:T(8,128)S(1)}) custom-call(bf16[1280,1152]{1,0:T(8,128)(2,1)S(1)} %copy-done.10, bf16[1024,1024]{1,0:T(8,128)(2,1)S(1)} %get-tuple-element.216.near, ...), custom_call_target="tpu_custom_call", output_to_operand_aliasing={{0}: (4, {}), {1}: (5, {})} | custom-call | flops 4026531840 | bytes 8388608 | tf_op jit(solution)/shard_map/pallas_call | solution.py:414
  169.9 9.9 %shard_map.155 = (f32[512,512]{1,0:T(8,128)S(1)}, bf16[512,512]{1,0:T(8,128)(2,1)S(1)}, f32[512,128]{1,0:T(8,128)S(1)}) custom-call(bf16[2560,768]{1,0:T(8,128)(2,1)S(1)} %copy-done.3, bf16[2560,768]{1,0:T(8,128)(2,1)S(1)} %copy-done.3, bf16[2560,768]{1,0:T(8,128)(2,1)S(1)} %copy-done.3, bf16[2560,768]{1,0:T(8,128)(2,1)S(1)} %copy-done.5, ...), custom_call_target="tpu_custom_call" | custom-call | flops 5368709120 | bytes 8388608 | tf_op jit(solution)/shard_map/pallas_call | solution.py:414
  190.4 16.5 %shard_map.156 = (bf16[512,1408]{1,0:T(8,128)(2,1)}, bf16[2,512,1408]{2,1,0:T(8,128)(2,1)}, f32[256,1024]{1,0:T(8,128)S(1)}, bf16[256,1024]{1,0:T(8,128)(2,1)S(1...) custom-call(s32[10]{0:T(128)S(1)} %stack.133.marks, bf16[512,1024]{1,0:T(8,128)(2,1)S(1)} %pad_maximum_fusion.4.rows, ...), custom_call_target="tpu_custom_call" | custom-call | flops 8858370048 | bytes 20971520 | tf_op jit(solution)/shard_map/pallas_call | solution.py:532
  222.4 3.4 convolution_convert_fusion
  236.4 4.6 %collective-permute-start.24 = (bf16[512,640]{1,0:T(8,128)(2,1)S(1)}, bf16[512,640]{1,0:T(8,128)(2,1)S(1)}, u32[]{:S(2)}, u32[]{:S(2)}) collective-permute-start(bf16[512,640]{1,0:T(8,128)(2,1)S(1)} %get-tuple-element.44.around.refs_0_), channel_id=1, source_target_pairs={{0,2},{1,3},{2,4},{3,5},{4,6},{5,7},{8,10},{9,11},{10,12},{11,13},... | collective-permute-start | bytes 1966088 | tf_op jit(solution)/shard_map/ppermute | solution.py:100
  241.0 30.8 %collective-permute-done.35 = bf16[2,512,256]{2,1,0:T(8,128)(2,1)S(1)} collective-permute-done((bf16[2,512,256]{2,1,0:T(8,128)(2,1)}, bf16[2,512,256]{2,1,0:T(8,128)(2,1)S(1)}, u32[]{:S(2)}, u32[]{:S(2)}) %collective-permute-start.35) | collective-permute-done | bytes 524320 | tf_op jit(solution)/shard_map/ppermute | solution.py:95
  274.4 11.3 %shard_map.158.d_q = bf16[512,512]{1,0:T(8,128)(2,1)S(1)} custom-call(bf16[2560,768]{1,0:T(8,128)(2,1)S(1)} %copy-done.4, bf16[2560,768]{1,0:T(8,128)(2,1)S(1)} %copy-done.4, bf16[2560,768]{1,0:T(8,128)(2,1)S(1)} %copy-done.4, bf16[2560,768]{1,0:T(8,128)(2,1)S(1)} %copy-done.6, bf16[2560,768]{1,0:T(8,128)(2,1)S(1)} %copy-done.6, ...), custom_call_target="tpu_custom_call" | custom-call | flops 8053063680 | bytes 8388608 | tf_op jit(solution)/shard_map/pallas_call | solution.py:414
  288.6 5.8 %collective-permute-done.37 = bf16[256,256]{1,0:T(8,128)(2,1)S(1)} collective-permute-done((bf16[256,256]{1,0:T(8,128)(2,1)S(1)}, bf16[256,256]{1,0:T(8,128)(2,1)S(1)}, u32[]{:S(2)}, u32[]{:S(2)}) %collective-permute-start.37) | collective-permute-done | bytes 131104 | tf_op jit(solution)/shard_map/ppermute | solution.py:86
  294.6 4.1 collective-permute-done.38
  305.9 14.0 %collective-permute-done.49 = bf16[352,512]{1,0:T(8,128)(2,1)S(1)} collective-permute-done((bf16[352,512]{1,0:T(8,128)(2,1)S(1)}, bf16[352,512]{1,0:T(8,128)(2,1)S(1)}, u32[]{:S(2)}, u32[]{:S(2)}) %collective-permute-start.49) | collective-permute-done | bytes 360480 | tf_op jit(solution)/shard_map/ppermute | solution.py:86
  321.1 5.5 %collective-permute-done.50 = bf16[176,512]{1,0:T(8,128)(2,1)S(1)} collective-permute-done((bf16[176,512]{1,0:T(8,128)(2,1)S(1)}, bf16[176,512]{1,0:T(8,128)(2,1)S(1)}, u32[]{:S(2)}, u32[]{:S(2)}) %collective-permute-start.50) | collective-permute-done | bytes 180256 | tf_op jit(solution)/shard_map/ppermute | solution.py:86
  326.7 3.5 fusion.8
  332.6 13.6 %shard_map.159 = (bf16[512,768]{1,0:T(8,128)(2,1)S(1)}, bf16[512,768]{1,0:T(8,128)(2,1)S(1)}) custom-call(bf16[2560,768]{1,0:T(8,128)(2,1)S(1)} %copy-done.4, bf16[2560,768]{1,0:T(8,128)(2,1)S(1)} %copy-done.4, bf16[2560,768]{1,0:T(8,128)(2,1)S(1)} %copy-done.4, bf16[2560,768]{1,0:T(8,128)(2,1)S(1)} %copy-done.6, bf16[2560,768]{1,0:T(8,128)(2,1)S(1)} %copy-done.6, ...), custom_call_target="tpu_custom_call" | custom-call | flops 10737418240 | bytes 8388608 | tf_op jit(solution)/shard_map/pallas_call | solution.py:414
  360.0 4.3 collective-permute-start.43
  364.2 6.8 %collective-permute-done.28 = bf16[2,512,768]{2,1,0:T(8,128)(2,1)S(1)} collective-permute-done((bf16[2,512,768]{2,1,0:T(8,128)(2,1)S(1)}, bf16[2,512,768]{2,1,0:T(8,128)(2,1)S(1)}, u32[]{:S(2)}, u32[]{:S(2)}) %collective-permute-start.28) | collective-permute-done | bytes 1572896 | tf_op jit(solution)/shard_map/ppermute | solution.py:95
  372.9 22.1 %collective-permute-done.43 = bf16[256,1408]{1,0:T(8,128)(2,1)S(1)} collective-permute-done((bf16[256,1408]{1,0:T(8,128)(2,1)S(1)}, bf16[256,1408]{1,0:T(8,128)(2,1)S(1)}, u32[]{:S(2)}, u32[]{:S(2)}) %collective-permute-start.43) | collective-permute-done | bytes 720928 | tf_op jit(solution)/shard_map/ppermute | solution.py:86
  402.7 14.8 %collective-permute-done.30 = bf16[128,768]{1,0:T(8,128)(2,1)S(1)} collective-permute-done((bf16[128,768]{1,0:T(8,128)(2,1)S(1)}, bf16[128,768]{1,0:T(8,128)(2,1)S(1)}, u32[]{:S(2)}, u32[]{:S(2)}) %collective-permute-start.30) | collective-permute-done | bytes 196640 | tf_op jit(solution)/shard_map/ppermute | solution.py:86
  420.1 5.6 %collective-permute-done.33 = bf16[128,768]{1,0:T(8,128)(2,1)S(1)} collective-permute-done((bf16[128,768]{1,0:T(8,128)(2,1)S(1)}, bf16[128,768]{1,0:T(8,128)(2,1)S(1)}, u32[]{:S(2)}, u32[]{:S(2)}) %collective-permute-start.33) | collective-permute-done | bytes 196640 | tf_op jit(solution)/shard_map/ppermute | solution.py:66
  425.9 6.1 %collective-permute-done.45 = bf16[128,1408]{1,0:T(8,128)(2,1)S(1)} collective-permute-done((bf16[128,1408]{1,0:T(8,128)(2,1)S(1)}, bf16[128,1408]{1,0:T(8,128)(2,1)S(1)}, u32[]{:S(2)}, u32[]{:S(2)}) %collective-permute-start.45) | collective-permute-done | bytes 360480 | tf_op jit(solution)/shard_map/ppermute | solution.py:66
  436.4 4.6 %fusion.2 = f32[256,2624]{0,1:T(8,128)S(1)} fusion(s32[1408]{0:T(1024)S(1)} %add_select_fusion.2, bf16[128,1408]{1,0:T(8,128)(2,1)S(1)} %get-tuple-element.338, bf16[128,1408]{1,0:T(8,128)(2,1)S(1)} %get-tuple-element.339), kind=kOutput, calls=%fused_computation.5 | convolution fusion | flops 1896767488 | bytes 3413504 | tf_op jit(solution)/shard_map/dot_general | solution.py:25
  441.1 4.8 %fusion.6 = f32[256,2624]{0,1:T(8,128)S(1)} fusion(f32[256,2624]{0,1:T(8,128)S(1)} %fusion.2, s32[1408]{0:T(1024)S(1)} %copy-done.72, bf16[128,1408]{1,0:T(8,128)(2,1)S(1)} %get-tuple-element.282, bf16[128,1408]{1,0:T(8,128)(2,1)S(1)} %get-tuple-element.281), kind=kOutput, calls=%fused_computation.9 | convolution fusion | flops 1897439232 | bytes 6100480 | tf_op jit(solution)/shard_map/dot_general | solution.py:25
  (478 shorter events, 162.3 us)
Async XLA Ops:
  2.8 46.4 %collective-permute-start.1 = (bf16[256,1152]{1,0:T(8,128)(2,1)S(1)}, bf16[256,1152]{1,0:T(8,128)(2,1)S(1)}, u32[]{:S(2)}, u32[]{:S(2)}) collective-permute-start(bf16[256,1152]{1,0:T(8,128)(2,1)S(1)} %pad_maximum_fusion.17.refs_0_), channel_id=1, source_target_pairs={{2,0},{3,1},{4,2},{5,3},{6,4},{7,5},{10,8},{11,9},{12,10},{13,11},... | collective-permute-start | bytes 1769480 | tf_op jit(solution)/shard_map/ppermute | solution.py:101
  4.1 45.1 %collective-permute-start = (bf16[256,1152]{1,0:T(8,128)(2,1)S(1)}, bf16[256,1152]{1,0:T(8,128)(2,1)S(1)}, u32[]{:S(2)}, u32[]{:S(2)}) collective-permute-start(bf16[256,1152]{1,0:T(8,128)(2,1)S(1)} %pad_maximum_fusion.17.refs_0_), channel_id=1, source_target_pairs={{0,2},{1,3},{2,4},{3,5},{4,6},{5,7},{8,10},{9,11},{10,12},{11,13},... | collective-permute-start | bytes 1769480 | tf_op jit(solution)/shard_map/ppermute | solution.py:100
  14.6 22.3 %collective-permute-start.5 = (bf16[128,1024]{1,0:T(8,128)(2,1)}, bf16[128,1024]{1,0:T(8,128)(2,1)S(1)}, u32[]{:S(2)}, u32[]{:S(2)}) collective-permute-start(bf16[128,1024]{1,0:T(8,128)(2,1)} %get-tuple-element.321), channel_id=1, source_target_pairs={{0,4},{1,5},{2,6},{3,7},{4,0},{5,1},{6,2},{7,3},{8,12},{9,13},{10,... | collective-permute-start | bytes 786440 | tf_op jit(solution)/shard_map/ppermute | solution.py:86
  17.7 19.3 %collective-permute-start.4 = (bf16[128,1024]{1,0:T(8,128)(2,1)}, bf16[128,1024]{1,0:T(8,128)(2,1)S(1)}, u32[]{:S(2)}, u32[]{:S(2)}) collective-permute-start(bf16[128,1024]{1,0:T(8,128)(2,1)} %get-tuple-element.321), channel_id=1, source_target_pairs={{0,2},{1,3},{2,0},{3,1},{4,6},{5,7},{6,4},{7,5},{8,10},{9,11},{10,... | collective-permute-start | bytes 786440 | tf_op jit(solution)/shard_map/ppermute | solution.py:86
  17.7 22.6 %collective-permute-start.6 = (bf16[128,1024]{1,0:T(8,128)(2,1)}, bf16[128,1024]{1,0:T(8,128)(2,1)S(1)}, u32[]{:S(2)}, u32[]{:S(2)}) collective-permute-start(bf16[128,1024]{1,0:T(8,128)(2,1)} %get-tuple-element.321), channel_id=1, source_target_pairs={{0,6},{1,7},{2,4},{3,5},{4,2},{5,3},{6,0},{7,1},{8,14},{9,15},{10,... | collective-permute-start | bytes 786440 | tf_op jit(solution)/shard_map/ppermute | solution.py:86
  36.9 67.0 %collective-permute-start.12 = (bf16[256,1024]{1,0:T(8,128)(2,1)}, bf16[256,1024]{1,0:T(8,128)(2,1)S(1)}, u32[]{:S(2)}, u32[]{:S(2)}) collective-permute-start(bf16[256,1024]{1,0:T(8,128)(2,1)} %param.17), channel_id=1, source_target_pairs={{0,8},{8,0},{16,24},{24,16},{1,9},{9,1},{17,25},{25,17},{2,10},{10... | collective-permute-start | bytes 1572872 | tf_op jit(solution)/shard_map/ppermute | solution.py:62
  41.3 20.6 %collective-permute-start.7 = (bf16[512,1024]{1,0:T(8,128)(2,1)S(1)}, bf16[512,1024]{1,0:T(8,128)(2,1)S(1)}, u32[]{:S(2)}, u32[]{:S(2)}) collective-permute-start(bf16[512,1024]{1,0:T(8,128)(2,1)S(1)} %pad_maximum_fusion.7), channel_id=1, source_target_pairs={{0,16},{1,17},{2,18},{3,19},{4,20},{5,21},{6,22},{7,23},{8,9},{9,8... | collective-permute-start | bytes 3145736 | tf_op jit(solution)/shard_map/ppermute | solution.py:95
  50.2 28.9 %collective-permute-start.2 = (bf16[512,1152]{1,0:T(8,128)(2,1)S(1)}, bf16[512,1152]{1,0:T(8,128)(2,1)S(1)}, u32[]{:S(2)}, u32[]{:S(2)}) collective-permute-start(bf16[512,1152]{1,0:T(8,128)(2,1)S(1)} %pad_maximum_fusion.6), channel_id=1, source_target_pairs={{0,1},{1,0},{2,3},{3,2},{4,5},{5,4},{6,7},{7,6},{8,9},{9,8},{10,11... | collective-permute-start | bytes 3538952 | tf_op jit(solution)/shard_map/ppermute | solution.py:103
  57.4 32.8 %collective-permute-start.14 = (bf16[256,1408]{1,0:T(8,128)(2,1)S(1)}, bf16[256,1408]{1,0:T(8,128)(2,1)S(1)}, u32[]{:S(2)}, u32[]{:S(2)}) collective-permute-start(bf16[256,1408]{1,0:T(8,128)(2,1)S(1)} %pad_maximum_fusion.12), channel_id=1, source_target_pairs={{0,4},{1,5},{2,6},{3,7},{4,0},{5,1},{6,2},{7,3},{8,12},{9,13},{10,... | collective-permute-start | bytes 2162696 | tf_op jit(solution)/shard_map/ppermute | solution.py:86
  61.9 73.4 %collective-permute-start.8 = (bf16[1024,1024]{1,0:T(8,128)(2,1)S(1)}, bf16[1024,1024]{1,0:T(8,128)(2,1)S(1)}, u32[]{:S(2)}, u32[]{:S(2)}) collective-permute-start(bf16[1024,1024]{1,0:T(8,128)(2,1)S(1)} %constant_dynamic-update-slice_fusion), channel_id=1, source_target_pairs={{0,1},{1,0},{2,3},{3,2},{4,5},{5,4},{6,7},{7,6},{8,24},{9,25},{10,... | collective-permute-start | bytes 6291464 | tf_op jit(solution)/shard_map/ppermute | solution.py:95
  81.6 63.9 %collective-permute-start.3 = (bf16[1280,1152]{1,0:T(8,128)(2,1)S(1)}, bf16[1280,1152]{1,0:T(8,128)(2,1)S(1)}, u32[]{:S(2)}, u32[]{:S(2)}) collective-permute-start(bf16[1280,1152]{1,0:T(8,128)(2,1)S(1)} %shard_map.152.rows), channel_id=1, source_target_pairs={{0,8},{8,0},{16,24},{24,16},{1,9},{9,1},{17,25},{25,17},{2,10},{10... | collective-permute-start | bytes 8847368 | tf_op jit(solution)/shard_map/ppermute | solution.py:62
  95.4 38.1 %collective-permute-start.15 = (bf16[512,1408]{1,0:T(8,128)(2,1)S(1)}, bf16[512,1408]{1,0:T(8,128)(2,1)S(1)}, u32[]{:S(2)}, u32[]{:S(2)}) collective-permute-start(bf16[512,1408]{1,0:T(8,128)(2,1)S(1)} %get-tuple-element.287), channel_id=1, source_target_pairs={{0,16},{1,17},{2,18},{3,19},{4,20},{5,21},{6,22},{7,23},{8,9},{9,8... | collective-permute-start | bytes 4325384 | tf_op jit(solution)/shard_map/ppermute | solution.py:95
  100.2 19.1 %collective-permute-start.18 = (bf16[352,512]{1,0:T(8,128)(2,1)S(1)}, bf16[352,512]{1,0:T(8,128)(2,1)S(1)}, u32[]{:S(2)}, u32[]{:S(2)}) collective-permute-start(bf16[352,512]{1,0:T(8,128)(2,1)S(1)} %pad_maximum_fusion.22), channel_id=1, source_target_pairs={{0,4},{1,5},{2,6},{3,7},{4,0},{5,1},{6,2},{7,3},{8,12},{9,13},{10,... | collective-permute-start | bytes 1081352 | tf_op jit(solution)/shard_map/ppermute | solution.py:86
  132.0 58.1 %collective-permute-start.20 = (bf16[1408,512]{1,0:T(8,128)(2,1)}, bf16[1408,512]{1,0:T(8,128)(2,1)}, u32[]{:S(2)}, u32[]{:S(2)}) collective-permute-start(bf16[1408,512]{1,0:T(8,128)(2,1)} %constant_dynamic-update-slice_fusion.36.shrink_pair), channel_id=1, source_target_pairs={{0,1},{1,0},{2,3},{3,2},{4,5},{5,4},{6,7},{7,6},{8,24},{9,25},{10,... | collective-permute-start | bytes 4325384 | tf_op jit(solution)/shard_map/ppermute | solution.py:95
  134.8 55.3 %collective-permute-start.16 = (bf16[1024,1408]{1,0:T(8,128)(2,1)}, bf16[1024,1408]{1,0:T(8,128)(2,1)}, u32[]{:S(2)}, u32[]{:S(2)}) collective-permute-start(bf16[1024,1408]{1,0:T(8,128)(2,1)} %constant_dynamic-update-slice_fusion.32.pair), channel_id=1, source_target_pairs={{0,1},{1,0},{2,3},{3,2},{4,5},{5,4},{6,7},{7,6},{8,24},{9,25},{10,... | collective-permute-start | bytes 8650760 | tf_op jit(solution)/shard_map/ppermute | solution.py:95
  216.1 70.5 %collective-permute-start.47 = (bf16[1408,512]{1,0:T(8,128)(2,1)}, bf16[1408,512]{1,0:T(8,128)(2,1)}, u32[]{:S(2)}, u32[]{:S(2)}) collective-permute-start(bf16[1408,512]{1,0:T(8,128)(2,1)} %select_dynamic-update-slice_fusion.2), channel_id=1, source_target_pairs={{0,1},{1,0},{2,3},{3,2},{4,5},{5,4},{6,7},{7,6},{8,24},{9,25},{10,... | collective-permute-start | bytes 4325384 | tf_op jit(solution)/shard_map/ppermute | solution.py:95
  225.8 100.9 %collective-permute-start.41 = (bf16[2,512,1408]{2,1,0:T(8,128)(2,1)}, bf16[2,512,1408]{2,1,0:T(8,128)(2,1)}, u32[]{:S(2)}, u32[]{:S(2)}) collective-permute-start(bf16[2,512,1408]{2,1,0:T(8,128)(2,1)} %convolution_convert_fusion), channel_id=1, source_target_pairs={{0,1},{1,0},{2,3},{3,2},{4,5},{5,4},{6,7},{7,6},{8,24},{9,25},{10,... | collective-permute-start | bytes 8650760 | tf_op jit(solution)/shard_map/ppermute | solution.py:95
  232.4 39.4 %collective-permute-start.35 = (bf16[2,512,256]{2,1,0:T(8,128)(2,1)}, bf16[2,512,256]{2,1,0:T(8,128)(2,1)S(1)}, u32[]{:S(2)}, u32[]{:S(2)}) collective-permute-start(bf16[2,512,256]{2,1,0:T(8,128)(2,1)} %convolution_convert_fusion.4), channel_id=1, source_target_pairs={{0,1},{1,0},{2,3},{3,2},{4,5},{5,4},{6,7},{7,6},{8,24},{9,25},{10,... | collective-permute-start | bytes 1572872 | tf_op jit(solution)/shard_map/ppermute | solution.py:95
  234.9 59.6 %collective-permute-start.25 = (bf16[512,640]{1,0:T(8,128)(2,1)S(1)}, bf16[512,640]{1,0:T(8,128)(2,1)S(1)}, u32[]{:S(2)}, u32[]{:S(2)}) collective-permute-start(bf16[512,640]{1,0:T(8,128)(2,1)S(1)} %get-tuple-element.44.around.refs_0_), channel_id=1, source_target_pairs={{2,0},{3,1},{4,2},{5,3},{6,4},{7,5},{10,8},{11,9},{12,10},{13,11},... | collective-permute-start | bytes 1966088 | tf_op jit(solution)/shard_map/ppermute | solution.py:101
  236.4 58.1 %collective-permute-start.24 = (bf16[512,640]{1,0:T(8,128)(2,1)S(1)}, bf16[512,640]{1,0:T(8,128)(2,1)S(1)}, u32[]{:S(2)}, u32[]{:S(2)}) collective-permute-start(bf16[512,640]{1,0:T(8,128)(2,1)S(1)} %get-tuple-element.44.around.refs_0_), channel_id=1, source_target_pairs={{0,2},{1,3},{2,4},{3,5},{4,6},{5,7},{8,10},{9,11},{10,12},{11,13},... | collective-permute-start | bytes 1966088 | tf_op jit(solution)/shard_map/ppermute | solution.py:100
  302.0 18.0 %collective-permute-start.49 = (bf16[352,512]{1,0:T(8,128)(2,1)S(1)}, bf16[352,512]{1,0:T(8,128)(2,1)S(1)}, u32[]{:S(2)}, u32[]{:S(2)}) collective-permute-start(bf16[352,512]{1,0:T(8,128)(2,1)S(1)} %slice.837), channel_id=1, source_target_pairs={{0,4},{1,5},{2,6},{3,7},{4,0},{5,1},{6,2},{7,3},{8,12},{9,13},{10,... | collective-permute-start | bytes 1081352 | tf_op jit(solution)/shard_map/ppermute | solution.py:86
  304.2 28.2 %collective-permute-start.26 = (bf16[1024,640]{1,0:T(8,128)(2,1)S(1)}, bf16[1024,640]{1,0:T(8,128)(2,1)S(1)}, u32[]{:S(2)}, u32[]{:S(2)}) collective-permute-start(bf16[1024,640]{1,0:T(8,128)(2,1)S(1)} %pad_maximum_fusion.5), channel_id=1, source_target_pairs={{0,1},{1,0},{2,3},{3,2},{4,5},{5,4},{6,7},{7,6},{8,9},{9,8},{10,11... | collective-permute-start | bytes 3932168 | tf_op jit(solution)/shard_map/ppermute | solution.py:103
  305.9 14.3 %collective-permute-start.40 = (bf16[128,512]{1,0:T(8,128)(2,1)S(1)}, bf16[128,512]{1,0:T(8,128)(2,1)S(1)}, u32[]{:S(2)}, u32[]{:S(2)}) collective-permute-start(bf16[128,512]{1,0:T(8,128)(2,1)S(1)} %pad_maximum_fusion.29), channel_id=1, source_target_pairs={{0,8},{8,0},{16,24},{24,16},{1,9},{9,1},{17,25},{25,17},{2,10},{10... | collective-permute-start | bytes 393224 | tf_op jit(solution)/shard_map/ppermute | solution.py:62
  330.3 26.6 %collective-permute-start.42 = (bf16[512,1408]{1,0:T(8,128)(2,1)}, bf16[512,1408]{1,0:T(8,128)(2,1)}, u32[]{:S(2)}, u32[]{:S(2)}) collective-permute-start(bf16[512,1408]{1,0:T(8,128)(2,1)} %fusion.8), channel_id=1, source_target_pairs={{0,16},{1,17},{2,18},{3,19},{4,20},{5,21},{6,22},{7,23},{8,9},{9,8... | collective-permute-start | bytes 4325384 | tf_op jit(solution)/shard_map/ppermute | solution.py:95
  332.4 18.5 %collective-permute-start.52 = (bf16[176,1024]{1,0:T(8,128)(2,1)S(1)}, bf16[176,1024]{1,0:T(8,128)(2,1)}, u32[]{:S(2)}, u32[]{:S(2)}) collective-permute-start(bf16[176,1024]{1,0:T(8,128)(2,1)S(1)} %pad_maximum_fusion.23), channel_id=1, source_target_pairs={{0,8},{8,0},{16,24},{24,16},{1,9},{9,1},{17,25},{25,17},{2,10},{10... | collective-permute-start | bytes 1081352 | tf_op jit(solution)/shard_map/ppermute | solution.py:62
  350.5 20.5 %collective-permute-start.28 = (bf16[2,512,768]{2,1,0:T(8,128)(2,1)S(1)}, bf16[2,512,768]{2,1,0:T(8,128)(2,1)S(1)}, u32[]{:S(2)}, u32[]{:S(2)}) collective-permute-start(bf16[2,512,768]{2,1,0:T(8,128)(2,1)S(1)} %convolution_convert_fusion.3), channel_id=1, source_target_pairs={{0,1},{1,0},{2,3},{3,2},{4,5},{5,4},{6,7},{7,6},{8,24},{9,25},{10,... | collective-permute-start | bytes 4718600 | tf_op jit(solution)/shard_map/ppermute | solution.py:95
  360.0 35.1 %collective-permute-start.43 = (bf16[256,1408]{1,0:T(8,128)(2,1)S(1)}, bf16[256,1408]{1,0:T(8,128)(2,1)S(1)}, u32[]{:S(2)}, u32[]{:S(2)}) collective-permute-start(bf16[256,1408]{1,0:T(8,128)(2,1)S(1)} %slice.807), channel_id=1, source_target_pairs={{0,4},{1,5},{2,6},{3,7},{4,0},{5,1},{6,2},{7,3},{8,12},{9,13},{10,... | collective-permute-start | bytes 2162696 | tf_op jit(solution)/shard_map/ppermute | solution.py:86
  371.7 24.2 %collective-permute-start.29 = (bf16[512,768]{1,0:T(8,128)(2,1)S(1)}, bf16[512,768]{1,0:T(8,128)(2,1)S(1)}, u32[]{:S(2)}, u32[]{:S(2)}) collective-permute-start(bf16[512,768]{1,0:T(8,128)(2,1)S(1)} %fusion.24), channel_id=1, source_target_pairs={{0,16},{1,17},{2,18},{3,19},{4,20},{5,21},{6,22},{7,23},{8,9},{9,8... | collective-permute-start | bytes 2359304 | tf_op jit(solution)/shard_map/ppermute | solution.py:95
  395.3 24.7 %collective-permute-start.44 = (bf16[128,1408]{1,0:T(8,128)(2,1)S(1)}, bf16[128,1408]{1,0:T(8,128)(2,1)S(1)}, u32[]{:S(2)}, u32[]{:S(2)}) collective-permute-start(bf16[128,1408]{1,0:T(8,128)(2,1)S(1)} %slice.809), channel_id=1, source_target_pairs={{0,2},{1,3},{2,0},{3,1},{4,6},{5,7},{6,4},{7,5},{8,10},{9,11},{10,... | collective-permute-start | bytes 1081352 | tf_op jit(solution)/shard_map/ppermute | solution.py:86
  396.6 21.0 %collective-permute-start.30 = (bf16[128,768]{1,0:T(8,128)(2,1)S(1)}, bf16[128,768]{1,0:T(8,128)(2,1)S(1)}, u32[]{:S(2)}, u32[]{:S(2)}) collective-permute-start(bf16[128,768]{1,0:T(8,128)(2,1)S(1)} %get-tuple-element.267), channel_id=1, source_target_pairs={{0,2},{1,3},{2,0},{3,1},{4,6},{5,7},{6,4},{7,5},{8,10},{9,11},{10,... | collective-permute-start | bytes 589832 | tf_op jit(solution)/shard_map/ppermute | solution.py:86
  398.1 19.4 %collective-permute-start.32 = (bf16[128,768]{1,0:T(8,128)(2,1)S(1)}, bf16[128,768]{1,0:T(8,128)(2,1)S(1)}, u32[]{:S(2)}, u32[]{:S(2)}) collective-permute-start(bf16[128,768]{1,0:T(8,128)(2,1)S(1)} %get-tuple-element.268), channel_id=1, source_target_pairs={{0,6},{1,7},{2,4},{3,5},{4,2},{5,3},{6,0},{7,1},{8,14},{9,15},{10,... | collective-permute-start | bytes 589832 | tf_op jit(solution)/shard_map/ppermute | solution.py:86
  401.5 16.1 %collective-permute-start.31 = (bf16[128,768]{1,0:T(8,128)(2,1)S(1)}, bf16[128,768]{1,0:T(8,128)(2,1)S(1)}, u32[]{:S(2)}, u32[]{:S(2)}) collective-permute-start(bf16[128,768]{1,0:T(8,128)(2,1)S(1)} %get-tuple-element.269), channel_id=1, source_target_pairs={{0,4},{1,5},{2,6},{3,7},{4,0},{5,1},{6,2},{7,3},{8,12},{9,13},{10,... | collective-permute-start | bytes 589832 | tf_op jit(solution)/shard_map/ppermute | solution.py:86
  (100 other events, 1055.1 us)

commit v3 on v2

--- a/solution.py
+++ b/solution.py
@@ -17,6 +17,7 @@
 LANES = 128
 GROUP = 256
 FAR = -1e6
+LONG = 10**11
 BF = jnp.bfloat16
 F32 = jnp.float32
 
@@ -66,14 +67,27 @@
     return lax.ppermute(array, "rep", [(i, i ^ 2) for i in range(lax.axis_size("rep"))])
 
 
-def after(array, *earlier):
-    return lax.optimization_barrier((array,) + earlier)[0]
-
-
-class Direct:
+class Moves:
+    def __init__(self):
+        self.recent = []
+
+    def send(self, array, axes, route):
+        self.recent.append(array)
+        return lax.ppermute(array, axes, route)
+
+    def across(self, array, flip):
+        return self.send(array, "rep", [(i, i ^ flip) for i in range(lax.axis_size("rep"))])
+
+    def given(self):
+        found, self.recent = self.recent, []
+        return found
+
+
+class Direct(Moves):
     depth = 4
 
     def __init__(self):
+        super().__init__()
         self.place = lax.axis_index("seq")
         self.z = self.place // 2
         self.y = self.place % 2
@@ -83,7 +97,7 @@
 
     def along(self, array, flip):
         route = [(s, s ^ (2 * flip)) for s in range(2 * self.depth)]
-        return lax.ppermute(array, "seq", route)
+        return self.send(array, "seq", route)
 
     def cross(self, array, turn):
         n = 2 * self.depth
@@ -92,27 +106,37 @@
             for s in range(n):
                 to = (r ^ 2, s) if r % 2 == turn else (r, s ^ 1)
                 route.append((r * n + s, to[0] * n + to[1]))
-        return lax.ppermute(array, ("rep", "seq"), route)
+        return self.send(array, ("rep", "seq"), route)
 
     def around(self, array):
         rows = array.shape[0]
         last = 2 * self.depth
-        low = lax.ppermute(array, "seq", [(s, s + 2) for s in range(last - 2)])
-        high = lax.ppermute(array, "seq", [(s, s - 2) for s in range(2, last)])
+        low = self.send(array, "seq", [(s, s + 2) for s in range(last - 2)])
+        high = self.send(array, "seq", [(s, s - 2) for s in range(2, last)])
+        low = yield low
+        high = yield high
         sent = jnp.concatenate([array, jnp.where(self.y == 0, high, low)], axis=0)
-        beside = lax.ppermute(sent, "seq", [(s, s ^ 1) for s in range(last)])
+        beside = yield self.send(sent, "seq", [(s, s ^ 1) for s in range(last)])
         step = 1 - 2 * self.y
         return [array, low, high, beside[:rows], beside[rows:]], [0, -2, 2, step, -step]
 
-    def collect(self, piece, at_once):
+    def gather(self, piece, at_once):
         if at_once:
-            return jnp.concatenate([piece] + [self.along(piece, k) for k in (1, 2, 3)], axis=0)
-        pair = jnp.concatenate([piece, self.along(piece, 1)], axis=0)
-        return jnp.concatenate([pair, self.along(pair, 2)], axis=0)
-
-    def share(self, rows):
-        pair = jnp.concatenate([rows, self.cross(rows, 0)], axis=0)
-        return pair, self.cross(pair, 1)
+            sent = [self.along(piece, k) for k in (1, 2, 3)]
+            found = [piece]
+            for array in sent:
+                array = yield array
+                found.append(array)
+            rows = jnp.concatenate(found, axis=0)
+        else:
+            there = yield self.along(piece, 1)
+            pair = jnp.concatenate([piece, there], axis=0)
+            there = yield self.along(pair, 2)
+            rows = jnp.concatenate([pair, there], axis=0)
+        once = yield self.cross(rows, 0)
+        pair = jnp.concatenate([rows, once], axis=0)
+        other = yield self.cross(pair, 1)
+        return pair, other
 
     def to_near(self, grid):
         turned = [pick(self.y == 0, pair, pair[::-1]) for pair in grid]
@@ -155,14 +179,20 @@
         rows = mine.shape[0] // 4
         cut = lambda k, n: mine[k * rows : (k + n) * rows]
         if at_once:
+            sent = [self.along(cut(k, 1), k) for k in (1, 2, 3)]
             total = cut(0, 1).astype(F32)
-            for k in (1, 2, 3):
-                total = total + self.along(cut(k, 1), k).astype(F32)
-            return total.astype(BF)
-        pair = (cut(0, 2).astype(F32) + self.along(cut(2, 2), 2).astype(F32)).astype(BF)
-        return (pair[:rows].astype(F32) + self.along(pair[rows:], 1).astype(F32)).astype(BF)
-
-    def reduce(self, left, near, far, at_once=False):
+            for array in sent:
+                array = yield array
+                total = total + array.astype(F32)
+            share = total.astype(BF)
+        else:
+            there = yield self.along(cut(2, 2), 2)
+            pair = (cut(0, 2).astype(F32) + there.astype(F32)).astype(BF)
+            there = yield self.along(pair[rows:], 1)
+            share = (pair[:rows].astype(F32) + there.astype(F32)).astype(BF)
+        return (yield from self.spread(share))
+
+    def reduce(self, left, near, far, at_once):
         half = left.shape[1] // 2
         top, bottom = left[:, :half], left[:, half:]
         sent = lax.dot_general(
@@ -171,33 +201,36 @@
             (((1,), (1,)), ((0,), (0,))),
             preferred_element_type=F32,
         ).astype(BF)
-        back = self.cross(sent, 1)
+        back = yield self.cross(sent, 1)
         once = inner_rows(jnp.where(self.front, top, bottom), jnp.where(self.front, far, near))
-        once_in = self.cross((once + back[1]).astype(BF), 0)
+        once_in = yield self.cross((once + back[1]).astype(BF), 0)
         mine = (inner_rows(top, near) + back[0] + once_in).astype(BF)
-        return self.down(mine, at_once)
-
-    def reduce_rows(self, left, near, far):
-        rows = left.shape[1] // (2 * self.depth)
-        blocks = []
-        for part in (near, far):
-            whole = inner_rows(left, part).astype(BF)
-            cut = lambda s: whole[s * rows : (s + 1) * rows]
-            lines = self.to_near([[cut(2 * z), cut(2 * z + 1)] for z in range(self.depth)])
-            blocks.append([jnp.concatenate(line, axis=0) for line in lines])
-        half = self.depth * rows
-        sent = jnp.concatenate(
-            [jnp.where(self.front, blocks[0][1], blocks[1][0]), blocks[1][1]], axis=0
-        )
-        back = self.cross(sent, 1)
-        once = jnp.where(self.front, blocks[1][0], blocks[0][1])
-        once_in = self.cross((once.astype(F32) + back[half:]).astype(BF), 0)
-        mine = (blocks[0][0].astype(F32) + back[:half] + once_in).astype(BF)
-        return self.down(mine, False)
-
-
-class Plain:
+        return (yield from self.down(mine, at_once))
+
+    def reduce_blocks(self, near, far):
+        back = yield self.across(far, 2)
+        total = (near.astype(F32) + back.astype(F32)).astype(BF)
+        lines = self.to_near([total[2 * z : 2 * z + 2] for z in range(self.depth)])
+        mine, sent = [jnp.concatenate(line, axis=0) for line in lines]
+        route = [(s, s ^ 1) for s in range(2 * self.depth)]
+        back = yield self.send(sent, "seq", route)
+        mine = (mine.astype(F32) + back.astype(F32)).astype(BF)
+        return (yield from self.down(mine, False))
+
+    def spread(self, share):
+        there = yield self.across(share, 2)
+        pair = [share, there]
+        low, high = pick(self.x == 0, pair, pair[::-1])
+        both = jnp.concatenate([low, high], axis=1)
+        there = yield self.across(both, 1)
+        size = share.shape[1]
+        cores = pick(self.core == 0, [both, there], [there, both])
+        return [[part[:, :size], part[:, size:]] for part in cores]
+
+
+class Plain(Moves):
     def __init__(self, rows):
+        super().__init__()
         self.rows = rows
         self.x = lax.axis_index("rep") // 2
         self.core = lax.axis_index("rep") % 2
@@ -209,15 +242,13 @@
         blocks, offsets = [array], [0]
         for offset in list(range(-reach, 0)) + list(range(1, reach + 1)):
             route = [(i + offset, i) for i in range(length) if 0 <= i + offset < length]
-            blocks.append(lax.ppermute(array, "seq", route))
+            blocks.append((yield self.send(array, "seq", route)))
             offsets.append(offset)
         return blocks, offsets
 
-    def collect(self, piece, at_once):
-        return lax.all_gather(piece, "seq", axis=0, tiled=True)
-
-    def share(self, near):
-        far = swap_far(near)
+    def gather(self, piece, at_once):
+        near = yield lax.all_gather(piece, "seq", axis=0, tiled=True)
+        far = yield self.across(near, 2)
         half = near.shape[0] // 2
         return (
             jnp.concatenate([near[:half], far[:half]], axis=0),
@@ -237,10 +268,48 @@
         return array
 
     def reduce(self, left, near, far, at_once=False):
-        mine = inner_rows(left, near) + swap_far(inner_rows(left, far).astype(BF))
-        return lax.psum_scatter(mine, "seq", scatter_dimension=0, tiled=True).astype(BF)
-
-    reduce_rows = reduce
+        back = yield self.across(inner_rows(left, far).astype(BF), 2)
+        mine = inner_rows(left, near) + back
+        share = lax.psum_scatter(mine, "seq", scatter_dimension=0, tiled=True).astype(BF)
+        return (yield from self.spread(share))
+
+    def reduce_blocks(self, near, far):
+        back = yield self.across(far, 2)
+        mine = (near.astype(F32) + back).reshape(-1, near.shape[2])
+        share = lax.psum_scatter(mine, "seq", scatter_dimension=0, tiled=True).astype(BF)
+        return (yield from self.spread(share))
+
+    spread = Direct.spread
+
+
+def gate(array, *earlier):
+    return lax.optimization_barrier((array,) + earlier)[0]
+
+
+class Chain:
+    def __init__(self, plan, steps):
+        self.plan, self.steps = plan, steps
+        self.value = None
+        self.sent = next(steps)
+        self.operands = tuple(plan.given())
+
+    def hold(self, *earlier):
+        if self.sent is not None:
+            self.sent = gate(self.sent, *earlier)
+
+    def step(self, count=1):
+        for _ in range(count):
+            if self.sent is not None:
+                try:
+                    self.sent = self.steps.send(self.sent)
+                except StopIteration as end:
+                    self.sent, self.value = None, end.value
+                self.operands = tuple(self.plan.given())
+
+    def end(self):
+        while self.sent is not None:
+            self.step()
+        return self.value
 
 
 def halves(front, pair, other):
@@ -282,9 +351,11 @@
             out[at, pl.ds(to, size)] = normal[:, s * size : (s + 1) * size]
 
 
-def mix_kernel(rows, near, far, tables, *refs):
-    near_out, far_out, cosine, sine = refs[-4:]
+def mix_kernel(ours, theirs, near, far, tables, near_out, far_out, cosine, sine):
+    count = pl.num_programs(0) // 2
+    step = pl.program_id(0)
     half = near.shape[0]
+    rows = jnp.where(step < count, ours[...], theirs[...])
     marks = rows[:, half : half + LANES].astype(F32)
     lane = lax.broadcasted_iota(jnp.int32, (1, LANES), 1).astype(F32)
     exact = lambda flags, table: jnp.dot(
@@ -303,7 +374,7 @@
             out[:, at + LANES : at + GROUP] = (b * scale).astype(BF)
         out[:, 2 * GROUP :] = raw[:, 2 * GROUP :].astype(BF)
 
-    @pl.when(pl.program_id(0) == 0)
+    @pl.when(step % count == 0)
     def _():
         cosine[...] = c
         sine[...] = s
@@ -405,11 +476,33 @@
         out[:, 2 * GROUP :] = kept[group][1].astype(BF)
 
 
-def call_kernel(kernel, ins, outs, flops, grid=1, aliases=None):
+def pack_kernel(place, active, grads, attended, branch, near, far):
+    count, depth = near.shape[0], attended.shape[1] // near.shape[0]
+    rows = active.shape[1] // count
+    wide = near.shape[2]
+    for i in (0, 1):
+        one = inner_rows(active[...], grads[:, i * wide : (i + 1) * wide]).astype(BF)
+        two = inner_rows(attended[...], branch[i]).astype(BF)
+
+        def store(out):
+            for s in range(count):
+                out[s, :rows] = one[s * rows : (s + 1) * rows]
+                at = s * depth
+                out[s, rows:, :GROUP] = two[at : at + depth // 2]
+                out[s, rows:, GROUP:] = two[at + depth // 2 : at + depth]
+
+        @pl.when(place[0] == i)
+        def _():
+            store(near)
+
+        @pl.when(place[0] != i)
+        def _():
+            store(far)
+
+
+def call_kernel(kernel, ins, outs, grid=1, room=56, micros=5):
     spec = lambda block, at: (
-        pl.BlockSpec(memory_space=pltpu.SMEM if block is None else pl.ANY)
-        if at is None
-        else pl.BlockSpec(block, at)
+        pl.BlockSpec(memory_space=pltpu.SMEM) if block is None else pl.BlockSpec(block, at)
     )
     return pl.pallas_call(
         kernel,
@@ -417,11 +510,8 @@
         in_specs=[spec(block, at) for _, block, at in ins],
         out_specs=tuple(pl.BlockSpec(block, at) for _, _, block, at in outs),
         out_shape=tuple(jax.ShapeDtypeStruct(shape, kind) for shape, kind, _, _ in outs),
-        input_output_aliases=aliases or {},
-        compiler_params=pltpu.CompilerParams(vmem_limit_bytes=40 * 2**20),
-        cost_estimate=pl.CostEstimate(
-            flops=flops, bytes_accessed=8 * 2**20, transcendentals=3 * 2**20
-        ),
+        compiler_params=pltpu.CompilerParams(vmem_limit_bytes=room * 2**20),
+        cost_estimate=pl.CostEstimate(flops=micros * 10**9, bytes_accessed=1, transcendentals=0),
     )(*[a for a, _, _ in ins])
 
 
@@ -448,7 +538,7 @@
     def shrinks(source, high, at, low):
         found = []
         for j in range(places // 2):
-            start = high * (units // 2) + j * block
+            start = high * (source.shape[0] // 2) + j * block
             row = pl.multiple_of(marks[2 + low * (places // 2) + j], 16)
             column = pl.multiple_of(at * wide, LANES)
             found.append(
@@ -542,12 +632,8 @@
             pltpu.VMEM((units, width), BF),
             pltpu.SemaphoreType.DMA((2 * marks.shape[0],)),
         ],
-        compiler_params=pltpu.CompilerParams(vmem_limit_bytes=48 * 2**20),
-        cost_estimate=pl.CostEstimate(
-            flops=12 * count * width * units,
-            bytes_accessed=20 * 2**20,
-            transcendentals=2 * count * units,
-        ),
+        compiler_params=pltpu.CompilerParams(vmem_limit_bytes=36 * 2**20),
+        cost_estimate=pl.CostEstimate(flops=8 * 10**9, bytes_accessed=1, transcendentals=0),
     )(marks, rows, grads, *expand, *shrink)
 
 
@@ -617,13 +703,20 @@
         jnp.where(near_x, shrink_weight[:, :half_width], shrink_weight[:, half_width:]),
     ).astype(BF)
 
-    joint_rows = plan.collect(joint_piece, True)
     anchor = (lax.axis_index("rep") * length + here) * rows
     position = anchor + jnp.arange(rows, dtype=jnp.int32) - document_start
     marks = jnp.pad(
         jnp.stack([(position + 1) // 16, (position + 1) % 16], axis=1), ((0, 0), (0, LANES - 2))
     ).astype(BF)
-    blocks, offsets = plan.around(jnp.concatenate([tokens, marks], axis=1))
+    packed = jnp.concatenate([tokens, marks], axis=1)
+    joint = Chain(plan, plan.gather(joint_piece, True))
+    near_tokens = Chain(plan, plan.around(packed))
+    joint.step(3)
+    expand = Chain(plan, plan.gather(gate(expand_piece, *joint.operands), False))
+    joint.step(2)
+    blocks, offsets = near_tokens.end()
+    expand.step(2)
+    shrink = Chain(plan, plan.gather(gate(shrink_piece, *expand.operands), False))
     block_count = len(blocks)
     span = block_count * rows
     still = lambda i: (0, 0)
@@ -633,7 +726,7 @@
         [(plan.columns(width // depth), None, None)]
         + [(block, (rows, width + LANES), still) for block in blocks],
         [((span, width + LANES), BF, (span, width + LANES), still)],
-        20 * span * width,
+        micros=2,
     )
     first = (sent, swap_core(sent))
     offset_rows = jnp.stack([jnp.int32(offset) for offset in offsets]) * rows
@@ -653,11 +746,7 @@
     tables = jnp.concatenate([jnp.cos(angle), jnp.sin(angle)], axis=1)
     cotangents = jnp.concatenate([cotangent, swap_core(cotangent)], axis=0)
 
-    expand_rows = plan.collect(after(expand_piece, joint_rows), False)
-    shrink_rows = plan.collect(after(shrink_piece, expand_rows), False)
-    joint_near, joint_far = halves(plan.front, *plan.share(joint_rows))
-    expand_both = plan.share(expand_rows)
-    shrink_both = plan.share(shrink_rows)
+    joint_near, joint_far = halves(plan.front, *joint.value)
     output_mine = jnp.concatenate([joint_near[:, 3 * GROUP :], joint_far[:, 3 * GROUP :]], axis=1)
     output_all = jnp.concatenate([output_mine, swap_core(output_mine)], axis=1)
 
@@ -668,28 +757,22 @@
         return jnp.concatenate(left + right, axis=-1)
 
     wide = 3 * GROUP
-    mixed = ()
-    turns = []
-    for t in (0, 1):
-        there = functools.partial(lambda shift, i: (i + shift, 0), t * block_count)
-        *mixed, cosine, sine = call_kernel(
-            mix_kernel,
-            [
-                (first[t], (rows, width + LANES), moving),
-                (joint_near, (width, wide), still),
-                (joint_far, (width, wide), still),
-                (tables, (2 * LANES, 2 * LANES), still),
-            ]
-            + [(array, (8, LANES), None) for array in mixed],
-            [((2 * span, wide), BF, (rows, wide), there)] * 2
-            + [((rows, LANES), F32, (rows, LANES), still)] * 2,
-            2 * span * width * 2 * wide,
-            block_count,
-            {4 + i: i for i in range(len(mixed))},
-        )
-        turns.append((cosine, sine))
-    cosine, sine = [jnp.concatenate(pair, axis=0) for pair in zip(*turns)]
-    score_flops = 2 * 2 * rows * span * GROUP * 8
+    *mixed, cosine, sine = call_kernel(
+        mix_kernel,
+        [
+            (first[0], (rows, width + LANES), lambda i: (jnp.minimum(i, block_count - 1), 0)),
+            (first[1], (rows, width + LANES), lambda i: (jnp.maximum(i - block_count, 0), 0)),
+            (joint_near, (width, wide), still),
+            (joint_far, (width, wide), still),
+            (tables, (2 * LANES, 2 * LANES), still),
+        ],
+        [((2 * span, wide), BF, (rows, wide), moving)] * 2
+        + [((2 * rows, LANES), F32, (rows, LANES), lambda i: (i // block_count, 0))] * 2,
+        2 * block_count,
+        micros=7,
+    )
+    expand.step()
+    shrink.step(2)
     column = lambda kind, every: (
         ((span, GROUP), lambda i: (i, kind))
         if every
@@ -710,9 +793,11 @@
         attend_kernel,
         wide_keys + documents,
         [both(2 * GROUP, F32), both(2 * GROUP, BF), both(LANES, F32)],
-        2 * score_flops,
         2,
-    )
+        micros=5,
+    )
+    shrink.step()
+    shrink.step()
     attended_there = swap_core(attended_low)
     attended_there = jnp.concatenate([attended_there[rows:], attended_there[:rows]], axis=0)
     attended_rows = plan.order(
@@ -722,6 +807,8 @@
     second, second_scale = centre(middle)
     second_low = plan.order(second.astype(BF), depth)
     second_both = jnp.concatenate([second_low, swap_core(second_low)], axis=0)
+    expand_both = expand.end()
+    shrink_both = shrink.end()
 
     where = jnp.stack(
         [plan.front.astype(jnp.int32), x.astype(jnp.int32)]
@@ -730,6 +817,7 @@
     active_low, lifted_grads, out, out_there, second_grad, second_there = hidden(
         where, second_both, cotangents, expand_both, shrink_both
     )
+    expand = Chain(plan, plan.reduce(second_both, lifted_grads[0], lifted_grads[1], False))
     result = middle + out + swap_core(out_there).astype(F32)
     second_grad = second_grad + swap_core(second_there).astype(F32)
     middle_grad = cotangent.astype(F32) + centre_back(
@@ -746,10 +834,30 @@
             (logs, (rows, LANES), moving),
         ],
         [both(2 * GROUP + LANES, BF), both(LANES, F32)],
-        2**28,
         2,
     )
-    arounds, _ = plan.around(around)
+    near_grads = Chain(plan, plan.around(around))
+    branch_sides = jnp.stack(
+        pick(near_x, *[[branch_both[:, i * GROUP : (i + 1) * GROUP] for i in o] for o in ((0, 1), (1, 0))])
+    )
+    kinds = [
+        ((length, unit_pad + depth // 2, half_width), BF),
+        (length, unit_pad + depth // 2, half_width),
+        lambda i: (0, 0, 0),
+    ]
+    sums = call_kernel(
+        pack_kernel,
+        [
+            (x.astype(jnp.int32)[None], None, 0),
+            (active_low, (2 * rows, units), still),
+            (cotangents, (2 * rows, width), still),
+            (plan.restore(attended_rows, depth), (2 * rows, width), still),
+            (branch_sides, (2, 2 * rows, GROUP), lambda i: (0, 0, 0)),
+        ],
+        [(*kinds[0], kinds[1], kinds[2])] * 2,
+    )
+    near_grads.step(2)
+    shrink = Chain(plan, plan.reduce_blocks(*sums))
     turning = [(cosine, (rows, LANES), moving), (sine, (rows, LANES), moving)]
     (query_grad,) = call_kernel(
         query_kernel,
@@ -761,9 +869,11 @@
         + documents
         + turning,
         [both(2 * GROUP, BF)],
-        3 * score_flops,
         2,
-    )
+        micros=13,
+    )
+    expand.step()
+    arounds, _ = near_grads.end()
     mixed_grads = call_kernel(
         key_kernel,
         wide_queries
@@ -772,9 +882,17 @@
         + turning
         + [(block, (rows, 2 * GROUP + LANES), moving) for block in arounds],
         [both(wide, BF), both(wide, BF)],
-        4 * score_flops,
         2,
-    )
+        micros=16,
+    )
+    own_first = jnp.concatenate([rows_in[:rows, :width] for rows_in in first], axis=0)
+    joint = Chain(plan, plan.reduce(own_first, *mixed_grads, True))
+    expand.step()
+    shrink.step()
+    joint.step()
+    moved = joint.operands + expand.operands
+    expand.hold(*moved)
+    shrink.hold(*moved)
     first_part = outer_rows(mixed_grads[0], joint_near[:, :wide]) + outer_rows(
         mixed_grads[1], joint_far[:, :wide]
     )
@@ -784,37 +902,15 @@
         normal, normal_scale, plan.restore(first_grad, depth)
     )
 
-    left, right = cotangents[:, :half_width], cotangents[:, half_width:]
-    shrink_share = plan.reduce_rows(active_low, *pick(near_x, [left, right], [right, left]))
-    expand_share = plan.reduce(second_both, lifted_grads[0], lifted_grads[1])
-    output_share = plan.reduce(
-        attended_rows, branch_both[:, :GROUP], branch_both[:, GROUP : 2 * GROUP]
-    )
-    joint_share = plan.reduce(
-        jnp.concatenate([rows_in[:rows, :width] for rows_in in first], axis=0),
-        mixed_grads[0],
-        mixed_grads[1],
-        True,
-    )
-
-    def spread(share):
-        pair = [share, swap_far(share)]
-        low, high = pick(near_x, pair, pair[::-1])
-        both = jnp.concatenate([low, high], axis=1)
-        there = swap_core(both)
-        size = share.shape[1]
-        cores = pick(core == 0, [both, there], [there, both])
-        return [[part[:, :size], part[:, size:]] for part in cores]
-
-    shrink_shares = spread(shrink_share)
-    shrink_grad = jnp.concatenate(
-        [
-            inner_rows(picked(0), shrink_shares[0][i]) + inner_rows(picked(1), shrink_shares[1][i])
-            for i in (0, 1)
-        ],
-        axis=1,
-    )
-    expand_shares = spread(expand_share)
+    expand.step()
+    shrink.step()
+    joint.step()
+    shrink.hold(*joint.operands)
+    expand.step()
+    expand.step()
+    joint.step(3)
+    shrink.step()
+    expand_shares = expand.end()
     expand_raw = 0.0
     for c in (0, 1):
         inner = c * unit_half + slot % unit_pad
@@ -823,23 +919,33 @@
         back = (unit_at[:, None] == jnp.arange(FF)[None, :]).astype(BF)
         expand_raw = expand_raw + dot(jnp.concatenate(expand_shares[c], axis=0), back)
     expand_raw = jnp.concatenate([expand_raw[:depth], expand_raw[depth:]], axis=1)
+    shrink.step()
+    joint.step()
+    shrink_shares = shrink.end()
+    joint_four = joint.end()
+
+    shrink_grad = jnp.concatenate(
+        [
+            inner_rows(picked(0), shrink_shares[0][i][:unit_pad])
+            + inner_rows(picked(1), shrink_shares[1][i][:unit_pad])
+            for i in (0, 1)
+        ],
+        axis=1,
+    )
     expand_grad = expand_raw * gain_two
     second_gain_grad = jnp.sum(expand_raw * expand_weight.astype(F32), axis=1)
-    output_shares = spread(output_share)
-    output_grad = jnp.concatenate(output_shares[0] + output_shares[1], axis=1).astype(F32)
-    joint_four = spread(joint_share)
+    output_grad = []
+    for pair in shrink_shares:
+        for share in pair:
+            share = share[unit_pad:]
+            output_grad.append(jnp.concatenate([share[:, :GROUP], share[:, GROUP:]], axis=0))
+    output_grad = jnp.concatenate(output_grad, axis=1).astype(F32)
     columns = []
     for kind in range(3):
         for c in (0, 1):
             for i in (0, 1):
                 piece = joint_four[c][i][:, kind * GROUP : (kind + 1) * GROUP]
-                columns.append(
-                    lax.dot_general(
-                        piece, turn, (((1,), (1,)), ((), ())), preferred_element_type=F32
-                    )
-                    if kind < 2
-                    else piece.astype(F32)
-                )
+                columns.append(outer_rows(piece, turn) if kind < 2 else piece.astype(F32))
     joint_raw = jnp.concatenate(columns, axis=1)
     joint_grad = joint_raw * gain_one
     first_gain_grad = jnp.sum(joint_raw * joint_weight.astype(F32), axis=1)

time: 458 us -> 448 us (0.978)
  waiting for transfers between devices: 169 us -> 147 us
  Pallas kernels: 71.7 us -> 90.5 us
  starting transfers between devices: 78.4 us -> 71.9 us
  other arithmetic: 40.4 us -> 45.6 us
  matrix products: 45.7 us -> 40.8 us
    ppermute x40 -> x38, waiting for transfers between devices: 169 us -> 144 us  [send(): return lax.ppermute(array, axes, route)]
    pallas_call x7, Pallas kernels: 55.2 us -> 76.2 us  [call_kernel(): pl.pallas_call(kernel, grid=(grid,), in_specs=[spec(block, at) for _, blo...]
    unnamed x188 -> x155, local copies, waits for them, and re-layouts: 34.6 us -> 20.1 us
    ppermute x40 -> x38, starting transfers between devices: 74.8 us -> 70 us  [send(): return lax.ppermute(array, axes, route)]
    slice x2, local copies, waits for them, and re-layouts: 0.21 us -> 4.79 us  [around(): beside[rows:]]
    dot_general x12 -> x8, matrix products: 13.4 us -> 9.42 us  [inner_rows(): lax.dot_general(left, right, (((0,), (0,)), ((), ())), preferred_element_...]
  transfers between devices with their start and end apart: 53 -> 47, of which waited for: 17 -> 20; matrix products, arithmetic and copies ran while one was open for 20% -> 24% of each run, Pallas kernels for 12% -> 17%
where the time goes in v3:
time: 448 us; the launch traced here: 441 us
  waiting for transfers between devices  147 us (33%)
  Pallas kernels  90.5 us (20%)
  starting transfers between devices  71.9 us (16%)
  other arithmetic  45.6 us (10%)
  local copies, waits for them, and re-layouts  42.7 us (10%)
  matrix products  40.8 us (9%)
    ppermute x38, waiting for transfers between devices, send(): return lax.ppermute(array, axes, route)  144 us
    pallas_call x7, Pallas kernels, call_kernel(): pl.pallas_call(kernel, grid=(grid,), in_specs=[spec(block, at) for _, blo...  76.2 us
    ppermute x38, starting transfers between devices, send(): return lax.ppermute(array, axes, route)  70 us
    dot_general x7, matrix products, dot(): return jnp.dot(left, right, preferred_element_type=F32)  20.7 us
    unnamed x155, local copies, waits for them, and re-layouts  20.1 us
    pallas_call x1, Pallas kernels, hidden(): pl.pallas_call(hidden_kernel, grid=(2,), in_specs=[pl.BlockSpec(memory_sp...  14.3 us
    dot_general x8, matrix products, inner_rows(): lax.dot_general(left, right, (((0,), (0,)), ((), ())), preferred_element_...  9.42 us
  transfers between devices with their start and end apart: 47, of which 20 were waited for; matrix products, arithmetic and copies ran while one was open for 24% of the time, Pallas kernels for 17%

profile of v3, /device:TPU:0, one launch (start us, length us, event | category | flops | bytes accessed | tf_op | source)
XLA Modules:
  0.0 440.9 jit_solution(18208635701160409644)
XLA Ops:
  4.1 6.4 %collective-permute-start = (bf16[256,1152]{1,0:T(8,128)(2,1)S(1)}, bf16[256,1152]{1,0:T(8,128)(2,1)}, u32[]{:S(2)}, u32[]{:S(2)}) collective-permute-start(bf16[256,1152]{1,0:T(8,128)(2,1)S(1)} %pad_maximum_fusion.16.refs_0_), channel_id=1, source_target_pairs={{0,2},{1,3},{2,4},{3,5},{4,6},{5,7},{8,10},{9,11},{10,12},{11,13},... | collective-permute-start | bytes 1769480 | tf_op jit(solution)/shard_map/ppermute | solution.py:76
  15.4 3.1 collective-permute-start.5
  22.9 7.1 %fusion.15 = bf16[128,1408]{1,0:T(8,128)(2,1)S(1)} fusion(bf16[128,5248]{1,0:T(8,128)(2,1)} %param.14, s32[1408]{0:T(1024)S(1)} %select_add_fusion, f32[128]{0:T(128)S(1)} %convert_element_type.231), kind=kOutput, calls=%fused_computation.29 | convolution fusion | flops 1899380736 | bytes 1710080 | tf_op jit(solution)/shard_map/dot_general | solution.py:26
  45.1 4.3 collective-permute-start.13
  52.6 4.8 %collective-permute-done.13 = bf16[128,1408]{1,0:T(8,128)(2,1)S(1)} collective-permute-done((bf16[128,1408]{1,0:T(8,128)(2,1)S(1)}, bf16[128,1408]{1,0:T(8,128)(2,1)S(1)}, u32[]{:S(2)}, u32[]{:S(2)}) %collective-permute-start.13) | collective-permute-done | bytes 360480 | tf_op jit(solution)/shard_map/ppermute | solution.py:76
  65.2 5.1 %shard_map.152.ours = bf16[1280,1152]{1,0:T(8,128)(2,1)} custom-call(s32[8]{0:T(128)} %fusion.160.places, bf16[256,1152]{1,0:T(8,128)(2,1)} %copy-done.39, bf16[256,1152]{1,0:T(8,128)(2,1)} %collective-permute-done.refs_1_, bf16[256,1152]{1,0:T(8,128)(2,1)} %collective-permute-done.1.refs_2_, bf16[256,1152]{1,0:T(8,128)(2,1)} %get-tuple-element.230.refs_3_, ...), custom_call_target="tpu_custom_call" | custom-call | flops 2000000000 | bytes 1 | tf_op jit(solution)/shard_map/pallas_call | solution.py:507
  77.2 14.9 %collective-permute-done.14 = bf16[256,1408]{1,0:T(8,128)(2,1)} collective-permute-done((bf16[256,1408]{1,0:T(8,128)(2,1)}, bf16[256,1408]{1,0:T(8,128)(2,1)}, u32[]{:S(2)}, u32[]{:S(2)}) %collective-permute-start.14) | collective-permute-done | bytes 720928 | tf_op jit(solution)/shard_map/ppermute | solution.py:76
  94.2 5.5 %collective-permute-done.17 = bf16[176,512]{1,0:T(8,128)(2,1)S(1)} collective-permute-done((bf16[176,512]{1,0:T(8,128)(2,1)S(1)}, bf16[176,512]{1,0:T(8,128)(2,1)S(1)}, u32[]{:S(2)}, u32[]{:S(2)}) %collective-permute-start.17) | collective-permute-done | bytes 180256 | tf_op jit(solution)/shard_map/ppermute | solution.py:76
  104.4 12.5 %collective-permute-done.18 = bf16[352,512]{1,0:T(8,128)(2,1)S(1)} collective-permute-done((bf16[352,512]{1,0:T(8,128)(2,1)S(1)}, bf16[352,512]{1,0:T(8,128)(2,1)S(1)}, u32[]{:S(2)}, u32[]{:S(2)}) %collective-permute-start.18) | collective-permute-done | bytes 360480 | tf_op jit(solution)/shard_map/ppermute | solution.py:76
  121.8 7.5 %collective-permute-done.19 = bf16[704,512]{1,0:T(8,128)(2,1)S(1)} collective-permute-done((bf16[704,512]{1,0:T(8,128)(2,1)S(1)}, bf16[704,512]{1,0:T(8,128)(2,1)S(1)}, u32[]{:S(2)}, u32[]{:S(2)}) %collective-permute-start.19) | collective-permute-done | bytes 720928 | tf_op jit(solution)/shard_map/ppermute | solution.py:76
  144.0 18.4 %shard_map.153 = (bf16[2560,768]{1,0:T(8,128)(2,1)}, bf16[2560,768]{1,0:T(8,128)(2,1)}, f32[512,128]{1,0:T(8,128)}, f32[512,128]{1,0:T(8,128)}) custom-call(bf16[1280,1152]{1,0:T(8,128)(2,1)} %shard_map.152.ours, bf16[1280,1152]{1,0:T(8,128)(2,1)} %copy-done.47, bf16[1024,1024]{1,0:T(8,128)(2,1)} %copy-done.12, bf16[1024,1024]{1,0:T(8,128)(2,1)} %pad_maximum_fusion.1.far, ...), custom_call_target="tpu_custom_call" | custom-call | flops 7000000000 | bytes 1 | tf_op jit(solution)/shard_map/pallas_call | solution.py:507
  162.4 12.4 %shard_map.154 = (f32[512,512]{1,0:T(8,128)}, bf16[512,512]{1,0:T(8,128)(2,1)}, f32[512,128]{1,0:T(8,128)}) custom-call(bf16[2560,768]{1,0:T(8,128)(2,1)} %get-tuple-element.32.q0.k0.v0, bf16[2560,768]{1,0:T(8,128)(2,1)} %get-tuple-element.32.q0.k0.v0, bf16[2560,768]{1,0:T(8,128)(2,1)} %get-tuple-element.32.q0.k0.v0, ...), custom_call_target="tpu_custom_call" | custom-call | flops 5000000000 | bytes 1 | tf_op jit(solution)/shard_map/pallas_call | solution.py:507
  188.4 23.1 %collective-permute-done.16.other = bf16[1024,1408]{1,0:T(8,128)(2,1)S(1)} collective-permute-done((bf16[1024,1408]{1,0:T(8,128)(2,1)S(1)}, bf16[1024,1408]{1,0:T(8,128)(2,1)S(1)}, u32[]{:S(2)}, u32[]{:S(2)}) %collective-permute-start.16) | collective-permute-done | bytes 2883616 | tf_op jit(solution)/shard_map/ppermute | solution.py:76
  211.5 14.3 %shard_map.155 = (bf16[512,1408]{1,0:T(8,128)(2,1)S(1)}, bf16[2,512,1408]{2,1,0:T(8,128)(2,1)S(1)}, f32[256,1024]{1,0:T(8,128)S(1)}, bf16[256,1024]{1,0:T(8,128)...) custom-call(s32[10]{0:T(128)S(1)} %stack.126.marks, bf16[512,1024]{1,0:T(8,128)(2,1)S(1)} %pad_maximum_fusion.4.rows, ...), custom_call_target="tpu_custom_call" | custom-call | flops 8000000000 | bytes 1 | tf_op jit(solution)/shard_map/pallas_call | solution.py:622
  231.3 3.4 convolution_convert_fusion
  240.5 3.4 shard_map.156
  245.2 5.6 %collective-permute-start.24 = (bf16[512,640]{1,0:T(8,128)(2,1)}, bf16[512,640]{1,0:T(8,128)(2,1)}, u32[]{:S(2)}, u32[]{:S(2)}) collective-permute-start(bf16[512,640]{1,0:T(8,128)(2,1)} %get-tuple-element.43.around.refs_0_), channel_id=1, source_target_pairs={{0,2},{1,3},{2,4},{3,5},{4,6},{5,7},{8,10},{9,11},{10,12},{11,13},... | collective-permute-start | bytes 1966088 | tf_op jit(solution)/shard_map/ppermute | solution.py:76
  251.7 7.4 %shard_map.159 = (bf16[8,240,512]{2,1,0:T(8,128)(2,1)}, bf16[8,240,512]{2,1,0:T(8,128)(2,1)}) custom-call(s32[1]{0:T(128)} %bitcast.6.place, bf16[512,1408]{1,0:T(8,128)(2,1)} %copy-done.5, bf16[512,1024]{1,0:T(8,128)(2,1)} %copy-done, bf16[512,1024]{1,0:T(8,128)(2,1)} %copy-done.48, bf16[2,512,256]{2,1,0:T(8,128)(2,1)} %pad_maximum_fusion.18.branch), custom_call_target="tpu_custom_call" | custom-call | flops 5000000000 | bytes 1 | tf_op jit(solution)/shard_map/pallas_call | solution.py:507
  267.2 13.4 %shard_map.157.d_q = bf16[512,512]{1,0:T(8,128)(2,1)} custom-call(bf16[2560,768]{1,0:T(8,128)(2,1)} %get-tuple-element.32.q0.k0.v0, bf16[2560,768]{1,0:T(8,128)(2,1)} %get-tuple-element.32.q0.k0.v0, bf16[2560,768]{1,0:T(8,128)(2,1)} %get-tuple-element.32.q0.k0.v0, bf16[2560,768]{1,0:T(8,128)(2,1)} %get-tuple-element.33.q1.k1.v1, ...), custom_call_target="tpu_custom_call" | custom-call | flops 12999999488 | bytes 1 | tf_op jit(solution)/shard_map/pallas_call | solution.py:507
  280.6 3.5 fusion.8
  285.7 12.8 %collective-permute-done.26 = bf16[1024,640]{1,0:T(8,128)(2,1)} collective-permute-done((bf16[1024,640]{1,0:T(8,128)(2,1)}, bf16[1024,640]{1,0:T(8,128)(2,1)}, u32[]{:S(2)}, u32[]{:S(2)}) %collective-permute-start.26) | collective-permute-done | bytes 1310752 | tf_op jit(solution)/shard_map/ppermute | solution.py:76
  300.9 16.0 %shard_map.158 = (bf16[512,768]{1,0:T(8,128)(2,1)}, bf16[512,768]{1,0:T(8,128)(2,1)}) custom-call(bf16[2560,768]{1,0:T(8,128)(2,1)} %get-tuple-element.32.q0.k0.v0, bf16[2560,768]{1,0:T(8,128)(2,1)} %get-tuple-element.32.q0.k0.v0, bf16[2560,768]{1,0:T(8,128)(2,1)} %get-tuple-element.32.q0.k0.v0, bf16[2560,768]{1,0:T(8,128)(2,1)} %get-tuple-element.33.q1.k1.v1, ...), custom_call_target="tpu_custom_call" | custom-call | flops 16000000000 | bytes 1 | tf_op jit(solution)/shard_map/pallas_call | solution.py:507
  331.7 3.7 collective-permute-start.43
  336.7 18.9 %collective-permute-done.28 = bf16[2,512,768]{2,1,0:T(8,128)(2,1)S(1)} collective-permute-done((bf16[2,512,768]{2,1,0:T(8,128)(2,1)S(1)}, bf16[2,512,768]{2,1,0:T(8,128)(2,1)S(1)}, u32[]{:S(2)}, u32[]{:S(2)}) %collective-permute-start.28) | collective-permute-done | bytes 1572896 | tf_op jit(solution)/shard_map/ppermute | solution.py:76
  356.2 5.6 %collective-permute-start.29 = (bf16[512,768]{1,0:T(8,128)(2,1)S(1)}, bf16[512,768]{1,0:T(8,128)(2,1)S(1)}, u32[]{:S(2)}, u32[]{:S(2)}) collective-permute-start(bf16[512,768]{1,0:T(8,128)(2,1)S(1)} %fusion.24), channel_id=1, source_target_pairs={{0,16},{1,17},{2,18},{3,19},{4,20},{5,21},{6,22},{7,23},{8,9},{9,8... | collective-permute-start | bytes 2359304 | tf_op jit(solution)/shard_map/ppermute | solution.py:76
  361.9 10.7 %collective-permute-done.36 = bf16[960,512]{1,0:T(8,128)(2,1)S(1)} collective-permute-done((bf16[960,512]{1,0:T(8,128)(2,1)S(1)}, bf16[960,512]{1,0:T(8,128)(2,1)S(1)}, u32[]{:S(2)}, u32[]{:S(2)}) %collective-permute-start.36) | collective-permute-done | bytes 983072 | tf_op jit(solution)/shard_map/ppermute | solution.py:76
  372.9 3.7 collective-permute-start.39
  383.7 13.9 %collective-permute-done.39 = bf16[480,512]{1,0:T(8,128)(2,1)S(1)} collective-permute-done((bf16[480,512]{1,0:T(8,128)(2,1)S(1)}, bf16[480,512]{1,0:T(8,128)(2,1)S(1)}, u32[]{:S(2)}, u32[]{:S(2)}) %collective-permute-start.39) | collective-permute-done | bytes 491552 | tf_op jit(solution)/shard_map/ppermute | solution.py:76
  399.1 5.9 %collective-permute-done.30 = bf16[128,768]{1,0:T(8,128)(2,1)S(1)} collective-permute-done((bf16[128,768]{1,0:T(8,128)(2,1)S(1)}, bf16[128,768]{1,0:T(8,128)(2,1)S(1)}, u32[]{:S(2)}, u32[]{:S(2)}) %collective-permute-start.30) | collective-permute-done | bytes 196640 | tf_op jit(solution)/shard_map/ppermute | solution.py:76
  413.8 3.4 collective-permute-done.41
  426.6 4.6 %fusion.2 = f32[256,2624]{0,1:T(8,128)S(1)} fusion(s32[1408]{0:T(1024)S(1)} %copy-done.50, bf16[128,1408]{1,0:T(8,128)(2,1)S(1)} %get-tuple-element.267, bf16[128,1408]{1,0:T(8,128)(2,1)S(1)} %get-tuple-element.266), kind=kOutput, calls=%fused_computation.5 | convolution fusion | flops 1896767488 | bytes 3413504 | tf_op jit(solution)/shard_map/dot_general | solution.py:26
  431.2 4.7 %fusion.6 = f32[256,2624]{0,1:T(8,128)S(1)} fusion(f32[256,2624]{0,1:T(8,128)S(1)} %fusion.2, s32[1408]{0:T(1024)S(1)} %copy-done.49, bf16[128,1408]{1,0:T(8,128)(2,1)S(1)} %get-tuple-element.265, bf16[128,1408]{1,0:T(8,128)(2,1)S(1)} %get-tuple-element.264), kind=kOutput, calls=%fused_computation.9 | convolution fusion | flops 1897439232 | bytes 6100480 | tf_op jit(solution)/shard_map/dot_general | solution.py:26
  (422 shorter events, 158.1 us)
Async XLA Ops:
  2.8 27.2 %collective-permute-start.1 = (bf16[256,1152]{1,0:T(8,128)(2,1)S(1)}, bf16[256,1152]{1,0:T(8,128)(2,1)}, u32[]{:S(2)}, u32[]{:S(2)}) collective-permute-start(bf16[256,1152]{1,0:T(8,128)(2,1)S(1)} %pad_maximum_fusion.16.refs_0_), channel_id=1, source_target_pairs={{2,0},{3,1},{4,2},{5,3},{6,4},{7,5},{10,8},{11,9},{12,10},{13,11},... | collective-permute-start | bytes 1769480 | tf_op jit(solution)/shard_map/ppermute | solution.py:76
  4.1 27.4 %collective-permute-start = (bf16[256,1152]{1,0:T(8,128)(2,1)S(1)}, bf16[256,1152]{1,0:T(8,128)(2,1)}, u32[]{:S(2)}, u32[]{:S(2)}) collective-permute-start(bf16[256,1152]{1,0:T(8,128)(2,1)S(1)} %pad_maximum_fusion.16.refs_0_), channel_id=1, source_target_pairs={{0,2},{1,3},{2,4},{3,5},{4,6},{5,7},{8,10},{9,11},{10,12},{11,13},... | collective-permute-start | bytes 1769480 | tf_op jit(solution)/shard_map/ppermute | solution.py:76
  15.4 26.1 %collective-permute-start.5 = (bf16[128,1024]{1,0:T(8,128)(2,1)}, bf16[128,1024]{1,0:T(8,128)(2,1)}, u32[]{:S(2)}, u32[]{:S(2)}) collective-permute-start(bf16[128,1024]{1,0:T(8,128)(2,1)} %get-tuple-element.318), channel_id=1, source_target_pairs={{0,4},{1,5},{2,6},{3,7},{4,0},{5,1},{6,2},{7,3},{8,12},{9,13},{10,... | collective-permute-start | bytes 786440 | tf_op jit(solution)/shard_map/ppermute | solution.py:76
  18.5 23.1 %collective-permute-start.4 = (bf16[128,1024]{1,0:T(8,128)(2,1)}, bf16[128,1024]{1,0:T(8,128)(2,1)S(1)}, u32[]{:S(2)}, u32[]{:S(2)}) collective-permute-start(bf16[128,1024]{1,0:T(8,128)(2,1)} %get-tuple-element.318), channel_id=1, source_target_pairs={{0,2},{1,3},{2,0},{3,1},{4,6},{5,7},{6,4},{7,5},{8,10},{9,11},{10,... | collective-permute-start | bytes 786440 | tf_op jit(solution)/shard_map/ppermute | solution.py:76
  18.5 82.0 %collective-permute-start.12 = (bf16[256,1024]{1,0:T(8,128)(2,1)S(1)}, bf16[256,1024]{1,0:T(8,128)(2,1)}, u32[]{:S(2)}, u32[]{:S(2)}) collective-permute-start(bf16[256,1024]{1,0:T(8,128)(2,1)S(1)} %copy-done.24), channel_id=1, source_target_pairs={{0,8},{8,0},{16,24},{24,16},{1,9},{9,1},{17,25},{25,17},{2,10},{10... | collective-permute-start | bytes 1572872 | tf_op jit(solution)/shard_map/ppermute | solution.py:63
  33.7 29.1 %collective-permute-start.2 = (bf16[512,1152]{1,0:T(8,128)(2,1)}, bf16[512,1152]{1,0:T(8,128)(2,1)}, u32[]{:S(2)}, u32[]{:S(2)}) collective-permute-start(bf16[512,1152]{1,0:T(8,128)(2,1)} %pad_maximum_fusion.6), channel_id=1, source_target_pairs={{0,1},{1,0},{2,3},{3,2},{4,5},{5,4},{6,7},{7,6},{8,9},{9,8},{10,11... | collective-permute-start | bytes 3538952 | tf_op jit(solution)/shard_map/ppermute | solution.py:76
  43.6 30.0 %collective-permute-start.7 = (bf16[512,1024]{1,0:T(8,128)(2,1)S(1)}, bf16[512,1024]{1,0:T(8,128)(2,1)S(1)}, u32[]{:S(2)}, u32[]{:S(2)}) collective-permute-start(bf16[512,1024]{1,0:T(8,128)(2,1)S(1)} %pad_maximum_fusion.7), channel_id=1, source_target_pairs={{0,16},{1,17},{2,18},{3,19},{4,20},{5,21},{6,22},{7,23},{8,9},{9,8... | collective-permute-start | bytes 3145736 | tf_op jit(solution)/shard_map/ppermute | solution.py:76
  58.4 33.6 %collective-permute-start.14 = (bf16[256,1408]{1,0:T(8,128)(2,1)}, bf16[256,1408]{1,0:T(8,128)(2,1)}, u32[]{:S(2)}, u32[]{:S(2)}) collective-permute-start(bf16[256,1408]{1,0:T(8,128)(2,1)} %pad_maximum_fusion.13), channel_id=1, source_target_pairs={{0,4},{1,5},{2,6},{3,7},{4,0},{5,1},{6,2},{7,3},{8,12},{9,13},{10,... | collective-permute-start | bytes 2162696 | tf_op jit(solution)/shard_map/ppermute | solution.py:76
  70.3 62.5 %collective-permute-start.3 = (bf16[1280,1152]{1,0:T(8,128)(2,1)}, bf16[1280,1152]{1,0:T(8,128)(2,1)S(1)}, u32[]{:S(2)}, u32[]{:S(2)}) collective-permute-start(bf16[1280,1152]{1,0:T(8,128)(2,1)} %shard_map.152.ours), channel_id=1, source_target_pairs={{0,8},{8,0},{16,24},{24,16},{1,9},{9,1},{17,25},{25,17},{2,10},{10... | collective-permute-start | bytes 8847368 | tf_op jit(solution)/shard_map/ppermute | solution.py:63
  74.6 54.8 %collective-permute-start.8 = (bf16[1024,1024]{1,0:T(8,128)(2,1)}, bf16[1024,1024]{1,0:T(8,128)(2,1)S(1)}, u32[]{:S(2)}, u32[]{:S(2)}) collective-permute-start(bf16[1024,1024]{1,0:T(8,128)(2,1)} %constant_dynamic-update-slice_fusion), channel_id=1, source_target_pairs={{0,1},{1,0},{2,3},{3,2},{4,5},{5,4},{6,7},{7,6},{8,24},{9,25},{10,... | collective-permute-start | bytes 6291464 | tf_op jit(solution)/shard_map/ppermute | solution.py:76
  99.7 17.2 %collective-permute-start.18 = (bf16[352,512]{1,0:T(8,128)(2,1)S(1)}, bf16[352,512]{1,0:T(8,128)(2,1)S(1)}, u32[]{:S(2)}, u32[]{:S(2)}) collective-permute-start(bf16[352,512]{1,0:T(8,128)(2,1)S(1)} %pad_maximum_fusion.21), channel_id=1, source_target_pairs={{0,4},{1,5},{2,6},{3,7},{4,0},{5,1},{6,2},{7,3},{8,12},{9,13},{10,... | collective-permute-start | bytes 1081352 | tf_op jit(solution)/shard_map/ppermute | solution.py:76
  101.6 73.6 %collective-permute-start.15 = (bf16[512,1408]{1,0:T(8,128)(2,1)}, bf16[512,1408]{1,0:T(8,128)(2,1)}, u32[]{:S(2)}, u32[]{:S(2)}) collective-permute-start(bf16[512,1408]{1,0:T(8,128)(2,1)} %get-tuple-element.270), channel_id=1, source_target_pairs={{0,16},{1,17},{2,18},{3,19},{4,20},{5,21},{6,22},{7,23},{8,9},{9,8... | collective-permute-start | bytes 4325384 | tf_op jit(solution)/shard_map/ppermute | solution.py:76
  116.9 12.4 %collective-permute-start.19 = (bf16[704,512]{1,0:T(8,128)(2,1)S(1)}, bf16[704,512]{1,0:T(8,128)(2,1)S(1)}, u32[]{:S(2)}, u32[]{:S(2)}) collective-permute-start(bf16[704,512]{1,0:T(8,128)(2,1)S(1)} %pad_maximum_fusion.14), channel_id=1, source_target_pairs={{0,16},{1,17},{2,18},{3,19},{4,20},{5,21},{6,22},{7,23},{8,9},{9,8... | collective-permute-start | bytes 2162696 | tf_op jit(solution)/shard_map/ppermute | solution.py:76
  129.3 59.1 %collective-permute-start.20 = (bf16[1408,512]{1,0:T(8,128)(2,1)S(1)}, bf16[1408,512]{1,0:T(8,128)(2,1)}, u32[]{:S(2)}, u32[]{:S(2)}) collective-permute-start(bf16[1408,512]{1,0:T(8,128)(2,1)S(1)} %constant_dynamic-update-slice_fusion.36.shrink_pair), channel_id=1, source_target_pairs={{0,1},{1,0},{2,3},{3,2},{4,5},{5,4},{6,7},{7,6},{8,24},{9,25},{10,... | collective-permute-start | bytes 4325384 | tf_op jit(solution)/shard_map/ppermute | solution.py:76
  177.0 34.5 %collective-permute-start.16 = (bf16[1024,1408]{1,0:T(8,128)(2,1)S(1)}, bf16[1024,1408]{1,0:T(8,128)(2,1)S(1)}, u32[]{:S(2)}, u32[]{:S(2)}) collective-permute-start(bf16[1024,1408]{1,0:T(8,128)(2,1)S(1)} %constant_dynamic-update-slice_fusion.32.pair), channel_id=1, source_target_pairs={{0,1},{1,0},{2,3},{3,2},{4,5},{5,4},{6,7},{7,6},{8,24},{9,25},{10,... | collective-permute-start | bytes 8650760 | tf_op jit(solution)/shard_map/ppermute | solution.py:76
  234.8 45.8 %collective-permute-start.37 = (bf16[2,512,1408]{2,1,0:T(8,128)(2,1)}, bf16[2,512,1408]{2,1,0:T(8,128)(2,1)}, u32[]{:S(2)}, u32[]{:S(2)}) collective-permute-start(bf16[2,512,1408]{2,1,0:T(8,128)(2,1)} %convolution_convert_fusion), channel_id=1, source_target_pairs={{0,1},{1,0},{2,3},{3,2},{4,5},{5,4},{6,7},{7,6},{8,24},{9,25},{10,... | collective-permute-start | bytes 8650760 | tf_op jit(solution)/shard_map/ppermute | solution.py:76
  243.9 19.1 %collective-permute-start.25 = (bf16[512,640]{1,0:T(8,128)(2,1)}, bf16[512,640]{1,0:T(8,128)(2,1)}, u32[]{:S(2)}, u32[]{:S(2)}) collective-permute-start(bf16[512,640]{1,0:T(8,128)(2,1)} %get-tuple-element.43.around.refs_0_), channel_id=1, source_target_pairs={{2,0},{3,1},{4,2},{5,3},{6,4},{7,5},{10,8},{11,9},{12,10},{13,11},... | collective-permute-start | bytes 1966088 | tf_op jit(solution)/shard_map/ppermute | solution.py:76
  245.2 18.9 %collective-permute-start.24 = (bf16[512,640]{1,0:T(8,128)(2,1)}, bf16[512,640]{1,0:T(8,128)(2,1)}, u32[]{:S(2)}, u32[]{:S(2)}) collective-permute-start(bf16[512,640]{1,0:T(8,128)(2,1)} %get-tuple-element.43.around.refs_0_), channel_id=1, source_target_pairs={{0,2},{1,3},{2,4},{3,5},{4,6},{5,7},{8,10},{9,11},{10,12},{11,13},... | collective-permute-start | bytes 1966088 | tf_op jit(solution)/shard_map/ppermute | solution.py:76
  259.1 64.9 %collective-permute-start.35 = (bf16[8,240,512]{2,1,0:T(8,128)(2,1)}, bf16[8,240,512]{2,1,0:T(8,128)(2,1)}, u32[]{:S(2)}, u32[]{:S(2)}) collective-permute-start(bf16[8,240,512]{2,1,0:T(8,128)(2,1)} %get-tuple-element.51), channel_id=1, source_target_pairs={{0,16},{8,24},{16,0},{24,8},{1,17},{9,25},{17,1},{25,9},{2,18},{10... | collective-permute-start | bytes 5898248 | tf_op jit(solution)/shard_map/ppermute | solution.py:76
  266.5 32.0 %collective-permute-start.26 = (bf16[1024,640]{1,0:T(8,128)(2,1)}, bf16[1024,640]{1,0:T(8,128)(2,1)}, u32[]{:S(2)}, u32[]{:S(2)}) collective-permute-start(bf16[1024,640]{1,0:T(8,128)(2,1)} %pad_maximum_fusion.5), channel_id=1, source_target_pairs={{0,1},{1,0},{2,3},{3,2},{4,5},{5,4},{6,7},{7,6},{8,9},{9,8},{10,11... | collective-permute-start | bytes 3932168 | tf_op jit(solution)/shard_map/ppermute | solution.py:76
  284.2 44.6 %collective-permute-start.38 = (bf16[512,1408]{1,0:T(8,128)(2,1)}, bf16[512,1408]{1,0:T(8,128)(2,1)}, u32[]{:S(2)}, u32[]{:S(2)}) collective-permute-start(bf16[512,1408]{1,0:T(8,128)(2,1)} %fusion.8), channel_id=1, source_target_pairs={{0,16},{1,17},{2,18},{3,19},{4,20},{5,21},{6,22},{7,23},{8,9},{9,8... | collective-permute-start | bytes 4325384 | tf_op jit(solution)/shard_map/ppermute | solution.py:76
  322.6 33.0 %collective-permute-start.28 = (bf16[2,512,768]{2,1,0:T(8,128)(2,1)S(1)}, bf16[2,512,768]{2,1,0:T(8,128)(2,1)S(1)}, u32[]{:S(2)}, u32[]{:S(2)}) collective-permute-start(bf16[2,512,768]{2,1,0:T(8,128)(2,1)S(1)} %convolution_convert_fusion.1), channel_id=1, source_target_pairs={{0,1},{1,0},{2,3},{3,2},{4,5},{5,4},{6,7},{7,6},{8,24},{9,25},{10,... | collective-permute-start | bytes 4718600 | tf_op jit(solution)/shard_map/ppermute | solution.py:76
  326.5 46.1 %collective-permute-start.36 = (bf16[960,512]{1,0:T(8,128)(2,1)S(1)}, bf16[960,512]{1,0:T(8,128)(2,1)S(1)}, u32[]{:S(2)}, u32[]{:S(2)}) collective-permute-start(bf16[960,512]{1,0:T(8,128)(2,1)S(1)} %pad_maximum_fusion.10), channel_id=1, source_target_pairs={{0,1},{1,0},{2,3},{3,2},{4,5},{5,4},{6,7},{7,6},{8,9},{9,8},{10,11... | collective-permute-start | bytes 2949128 | tf_op jit(solution)/shard_map/ppermute | solution.py:76
  331.7 44.9 %collective-permute-start.43 = (bf16[256,1408]{1,0:T(8,128)(2,1)S(1)}, bf16[256,1408]{1,0:T(8,128)(2,1)S(1)}, u32[]{:S(2)}, u32[]{:S(2)}) collective-permute-start(bf16[256,1408]{1,0:T(8,128)(2,1)S(1)} %slice.770), channel_id=1, source_target_pairs={{0,4},{1,5},{2,6},{3,7},{4,0},{5,1},{6,2},{7,3},{8,12},{9,13},{10,... | collective-permute-start | bytes 2162696 | tf_op jit(solution)/shard_map/ppermute | solution.py:76
  356.2 23.1 %collective-permute-start.29 = (bf16[512,768]{1,0:T(8,128)(2,1)S(1)}, bf16[512,768]{1,0:T(8,128)(2,1)S(1)}, u32[]{:S(2)}, u32[]{:S(2)}) collective-permute-start(bf16[512,768]{1,0:T(8,128)(2,1)S(1)} %fusion.24), channel_id=1, source_target_pairs={{0,16},{1,17},{2,18},{3,19},{4,20},{5,21},{6,22},{7,23},{8,9},{9,8... | collective-permute-start | bytes 2359304 | tf_op jit(solution)/shard_map/ppermute | solution.py:76
  372.9 24.7 %collective-permute-start.39 = (bf16[480,512]{1,0:T(8,128)(2,1)S(1)}, bf16[480,512]{1,0:T(8,128)(2,1)S(1)}, u32[]{:S(2)}, u32[]{:S(2)}) collective-permute-start(bf16[480,512]{1,0:T(8,128)(2,1)S(1)} %slice.772), channel_id=1, source_target_pairs={{0,4},{1,5},{2,6},{3,7},{4,0},{5,1},{6,2},{7,3},{8,12},{9,13},{10,... | collective-permute-start | bytes 1474568 | tf_op jit(solution)/shard_map/ppermute | solution.py:76
  376.9 21.1 %collective-permute-start.44 = (bf16[128,1408]{1,0:T(8,128)(2,1)S(1)}, bf16[128,1408]{1,0:T(8,128)(2,1)S(1)}, u32[]{:S(2)}, u32[]{:S(2)}) collective-permute-start(bf16[128,1408]{1,0:T(8,128)(2,1)S(1)} %slice.785), channel_id=1, source_target_pairs={{0,2},{1,3},{2,0},{3,1},{4,6},{5,7},{6,4},{7,5},{8,10},{9,11},{10,... | collective-permute-start | bytes 1081352 | tf_op jit(solution)/shard_map/ppermute | solution.py:76
  380.1 24.9 %collective-permute-start.30 = (bf16[128,768]{1,0:T(8,128)(2,1)S(1)}, bf16[128,768]{1,0:T(8,128)(2,1)S(1)}, u32[]{:S(2)}, u32[]{:S(2)}) collective-permute-start(bf16[128,768]{1,0:T(8,128)(2,1)S(1)} %get-tuple-element.261), channel_id=1, source_target_pairs={{0,2},{1,3},{2,0},{3,1},{4,6},{5,7},{6,4},{7,5},{8,10},{9,11},{10,... | collective-permute-start | bytes 589832 | tf_op jit(solution)/shard_map/ppermute | solution.py:76
  380.2 24.8 %collective-permute-start.32 = (bf16[128,768]{1,0:T(8,128)(2,1)S(1)}, bf16[128,768]{1,0:T(8,128)(2,1)S(1)}, u32[]{:S(2)}, u32[]{:S(2)}) collective-permute-start(bf16[128,768]{1,0:T(8,128)(2,1)S(1)} %get-tuple-element.262), channel_id=1, source_target_pairs={{0,6},{1,7},{2,4},{3,5},{4,2},{5,3},{6,0},{7,1},{8,14},{9,15},{10,... | collective-permute-start | bytes 589832 | tf_op jit(solution)/shard_map/ppermute | solution.py:76
  381.7 24.4 %collective-permute-start.31 = (bf16[128,768]{1,0:T(8,128)(2,1)S(1)}, bf16[128,768]{1,0:T(8,128)(2,1)S(1)}, u32[]{:S(2)}, u32[]{:S(2)}) collective-permute-start(bf16[128,768]{1,0:T(8,128)(2,1)S(1)} %get-tuple-element.263), channel_id=1, source_target_pairs={{0,4},{1,5},{2,6},{3,7},{4,0},{5,1},{6,2},{7,3},{8,12},{9,13},{10,... | collective-permute-start | bytes 589832 | tf_op jit(solution)/shard_map/ppermute | solution.py:76
  398.1 12.5 %collective-permute-start.45 = (bf16[128,1408]{1,0:T(8,128)(2,1)S(1)}, bf16[128,1408]{1,0:T(8,128)(2,1)S(1)}, u32[]{:S(2)}, u32[]{:S(2)}) collective-permute-start(bf16[128,1408]{1,0:T(8,128)(2,1)S(1)} %add_convert_fusion.5), channel_id=1, source_target_pairs={{0,16},{8,24},{16,0},{24,8},{1,17},{9,25},{17,1},{25,9},{2,18},{10... | collective-permute-start | bytes 1081352 | tf_op jit(solution)/shard_map/ppermute | solution.py:76
  413.3 12.4 %collective-permute-start.46 = (bf16[128,2816]{1,0:T(8,128)(2,1)S(1)}, bf16[128,2816]{1,0:T(8,128)(2,1)S(1)}, u32[]{:S(2)}, u32[]{:S(2)}) collective-permute-start(bf16[128,2816]{1,0:T(8,128)(2,1)S(1)} %pad_maximum_fusion.15), channel_id=1, source_target_pairs={{0,8},{8,0},{16,24},{24,16},{1,9},{9,1},{17,25},{25,17},{2,10},{10... | collective-permute-start | bytes 2162696 | tf_op jit(solution)/shard_map/ppermute | solution.py:76
  (75 other events, 726.0 us)
